TPU v7x, 1024 devices: a whole 8x8x8 slice. The times are simulated.
1024 devices in a mesh: cl: 128 (over z, x, core), grp: 8 (over y).
Axes of the slice: x: 8, y: 8, z: 8, core: 2. Of those that a mesh axis runs over, the one named last changes fastest.
Arguments:
- basis: float32 [16, 8, 1024, 128], P(None, 'grp', 'cl'), may hold values from -6 to 6
- near_blocks: bfloat16 [8, 1024, 4, 128, 128], P('grp', 'cl'), may hold values from -0.25 to 0.25
- near_list: int32 [8, 1024, 4], P('grp', 'cl'), may hold values from 0 to 23
- source_basis: bfloat16 [8, 1024, 32, 128], P('grp', 'cl'), may hold values from -0.5 to 0.5
- target_basis: bfloat16 [8, 1024, 32, 128], P('grp', 'cl'), may hold values from -1 to 1
- coupling: bfloat16 [8, 2048, 1024], P('grp', 'cl'), may hold values from -0.75 to 0.75
- far_target: int32 [8, 2048], P('grp'), may hold values from 0 to 1023, as said below
- far_source: int32 [8, 2048], P('grp', 'cl'), may hold values from 0 to 1023, as said below
- far_count: int32 [8, 128], P('grp', 'cl'), may hold values from 8 to 16
Outputs:
- next_vector: float32 [8, 1024, 128], P('grp', 'cl')
- hessenberg: float32 [17], replicated
Inputs may be any that keep to these rules, and one draw needn't show every extreme that they name: `far_target`: slots are owned in blocks of 16, block d by owner d of the group, whose clusters are d * 8 to (d + 1) * 8 - 1. Except for slot 1 of each owner, a slot's target lies within 16 clusters before or 23 after the owner's first cluster. Slot 1's target is a cluster of owner (d + 64) % 128. `far_source`: except for slot 0 of each owner, a slot's source lies within 80 clusters before or 87 after the owner's first cluster, and where the slot's target obeys the rule above the source differs from it by 16 to 64 clusters. Slot 0's source is a cluster of owner (d + 64) % 128.
All inputs are finite; a program needn't handle non-finite values.
Results may differ from a plain program's by a relative error of at most 0.0039.
Values may be sent and summed in bfloat16 or wider, within the bound.
No kernel may reach another device: no remote copies, remote signals or barrier semaphores. Data moves between devices by JAX's collectives and lax.ppermute only.
A program may use at most 32 MiB of HBM per device.

v0:
```python
import jax
import jax.numpy as jnp
from jax import lax
from jax.sharding import Mesh
from jax.sharding import PartitionSpec as P

CL = ("cl_0", "cl_1", "cl_2")
CL_GRP = ("cl_0", "cl_1", "cl_2", "grp")


def with_halo(cells, sides, width):
    for axis, dim in sides:
        count = lax.axis_size(axis)
        ends = count - 1
        head = lax.slice_in_dim(cells, 0, width, axis=dim)
        tail = lax.slice_in_dim(cells, cells.shape[dim] - width, cells.shape[dim], axis=dim)
        cells = jnp.concatenate(
            [
                lax.ppermute(tail, axis, [(i, (i + 1) % count) for i in range(ends)]),
                cells,
                lax.ppermute(head, axis, [((i + 1) % count, i) for i in range(ends)]),
            ],
            axis=dim,
        )
    return cells


def passed_along(block, axis, distance):
    devices = range(lax.axis_size(axis))
    route = [(i - distance, i) for i in devices if i - distance in devices]
    return lax.ppermute(block, axis, route)


def from_behind(value, axis, steps):
    count = lax.axis_size(axis)
    pairs = [(source, (source + steps) % count) for source in range(count)]
    return lax.ppermute(value, axis, pairs)


def over_axes(array, axes):
    for axis in axes:
        array = lax.psum(array, axis)
    return array


def on_device(
    basis,
    near_blocks,
    near_list,
    source_basis,
    target_basis,
    coupling,
    far_target,
    far_source,
    far_count,
):
    basis_count = basis.shape[0]
    clusters = basis.shape[2]
    panels_cl = basis.shape[3]
    ranks = source_basis.shape[2]
    block_slots = coupling.shape[1]
    axis_length = lax.axis_size(CL)
    half_axis = axis_length // 2
    current = basis[basis_count - 1, 0]
    current_bf = current.astype(jnp.bfloat16)
    window = with_halo(current_bf, ((CL, 0),), clusters)
    gathered = window[near_list[0]]
    near_part = jnp.einsum(
        "tkij,tkj->ti", near_blocks[0], gathered, preferred_element_type=jnp.float32
    )
    expansion = jnp.einsum(
        "srp,sp->sr", source_basis[0], current_bf, preferred_element_type=jnp.float32
    ).astype(jnp.bfloat16)
    my_index = lax.axis_index(CL)
    slot_local = jnp.arange(block_slots, dtype=jnp.int32)
    my_sources = far_source[0]
    all_expansion = lax.all_gather(expansion, CL, axis=0, tiled=True)
    picked = all_expansion[my_sources]
    square_blocks = coupling[0].reshape(block_slots, ranks, ranks)
    live_mask = (slot_local < far_count[0, 0]).astype(jnp.float32)
    contributions = (
        jnp.einsum("bij,bj->bi", square_blocks, picked, preferred_element_type=jnp.float32)
        * live_mask[:, None]
    )
    my_targets = lax.dynamic_slice_in_dim(far_target[0], my_index * block_slots, block_slots)
    near_first = (my_index - 2) * clusters
    near_rows = near_first + jnp.arange(6 * clusters, dtype=jnp.int32)
    keep_near = (slot_local != 1).astype(jnp.float32)
    selector = (near_rows[:, None] == my_targets[None, :]).astype(jnp.float32) * keep_near[None, :]
    partial_value = jnp.dot(selector, contributions, precision=lax.Precision.HIGHEST)
    coupled = jnp.zeros((clusters, ranks), jnp.float32)
    for step in range(6):
        offset = step - 2
        block = partial_value[step * clusters : (step + 1) * clusters]
        coupled = coupled + passed_along(block, CL, offset)
    opposite_first = (my_index + half_axis) % axis_length * clusters
    far_rows = opposite_first + jnp.arange(clusters, dtype=jnp.int32)
    keep_far = (slot_local == 1).astype(jnp.float32)
    far_selector = (far_rows[:, None] == my_targets[None, :]).astype(jnp.float32) * keep_far[
        None, :
    ]
    far_block = jnp.dot(far_selector, contributions, precision=lax.Precision.HIGHEST)
    coupled = coupled + from_behind(far_block, CL, half_axis)
    coupled_bf = coupled.astype(jnp.bfloat16)
    far_part = jnp.einsum(
        "tr,trp->tp", coupled_bf, target_basis[0], preferred_element_type=jnp.float32
    )
    image = 0.5 * current + near_part + far_part
    flat_basis = basis[:, 0].reshape(basis_count, clusters * panels_cl)
    flat_image = image.reshape(-1)
    panels = float(lax.axis_size(CL) * lax.axis_size("grp") * clusters * panels_cl)
    local_products = jnp.dot(flat_basis, flat_image, precision=lax.Precision.HIGHEST)
    gram_local = jnp.dot(flat_basis, flat_basis.T, precision=lax.Precision.HIGHEST)
    products, image_squares, gram_matrix = (
        over_axes(local_products, CL_GRP),
        over_axes(jnp.sum(flat_image * flat_image), CL_GRP),
        over_axes(gram_local, CL_GRP),
    )
    projection = products / panels
    remainder = flat_image - jnp.dot(projection, flat_basis, precision=lax.Precision.HIGHEST)
    squares = (
        image_squares
        - 2.0 * jnp.sum(projection * products)
        + jnp.dot(
            projection,
            jnp.dot(gram_matrix, projection, precision=lax.Precision.HIGHEST),
            precision=lax.Precision.HIGHEST,
        )
    )
    new_norm = jnp.sqrt(squares / panels + 1e-06)
    next_vector = (remainder / new_norm).reshape(1, clusters, panels_cl)
    return (next_vector, jnp.concatenate([projection, new_norm[None]]))


def solution(mesh):
    torus = Mesh(mesh.devices.reshape(8, 8, 2, mesh.shape["grp"]), ("cl_0", "cl_1", "cl_2", "grp"))
    in_specs = (
        P(None, "grp", CL, None),
        P("grp", CL, None, None, None),
        P("grp", CL, None),
        P("grp", CL, None, None),
        P("grp", CL, None, None),
        P("grp", CL, None),
        P("grp", None),
        P("grp", CL),
        P("grp", CL),
    )
    out_specs = (P("grp", CL, None), P())
    return jax.shard_map(
        on_device, mesh=torus, in_specs=in_specs, out_specs=out_specs, check_vma=False
    )
```

profile of v0, /device:TPU:1, one launch (start us, length us, event | category | flops | bytes accessed | tf_op | source)
XLA Modules:
  0.0 154.8 jit_solution(18144861774632746159)
XLA Ops:
  0.7 0.8 fusion.41
  1.7 64.4 %all_gather.3 = bf16[1024,32]{1,0:T(8,128)(2,1)S(1)} all-gather(bf16[8,32]{1,0:T(8,128)(2,1)S(1)} %convert_element_type.38), channel_id=1, replica_groups=mesh['cl_0'=8,'cl_1'=8,'cl_2'=2,'grp'=8] {'cl_0','cl_1','cl_2'}, dimensions={0}, use_global_device_ids=true | all-gather | bytes 66048 | tf_op jit(solution)/shard_map/all_gather | solution.py:77
  67.0 0.7 dynamic-slice_bitcast_fusion
  67.7 0.6 gather_fusion.1
  68.8 2.8 %collective-permute-start.8 = (f32[8,32]{0,1:T(8,128)S(1)}, f32[8,32]{0,1:T(8,128)S(1)}, u32[]{:S(2)}, u32[]{:S(2)}) collective-permute-start(f32[8,32]{0,1:T(8,128)S(1)} %fusion.25), channel_id=1, source_target_pairs={{0,512},{8,520},{16,528},{24,536},{32,544},{40,552},{48,560},{56,5... | collective-permute-start | bytes 3080 | tf_op jit(solution)/shard_map/ppermute | solution.py:37
  72.0 1.3 collective-permute-start.2
  73.3 2.3 %collective-permute-start.3 = (f32[8,32]{0,1:T(8,128)S(1)}, f32[8,32]{0,1:T(8,128)S(1)}, u32[]{:S(2)}, u32[]{:S(2)}) collective-permute-start(f32[8,32]{0,1:T(8,128)S(1)} %get-tuple-element.18), channel_id=1, source_target_pairs={{8,0},{16,8},{24,16},{32,24},{40,32},{48,40},{56,48},{64,56},{72,6... | collective-permute-start | bytes 3080 | tf_op jit(solution)/shard_map/ppermute | solution.py:31
  75.7 4.2 %collective-permute-start.5 = (f32[8,32]{0,1:T(8,128)S(1)}, f32[8,32]{0,1:T(8,128)S(1)}, u32[]{:S(2)}, u32[]{:S(2)}) collective-permute-start(f32[8,32]{0,1:T(8,128)S(1)} %get-tuple-element.21), channel_id=1, source_target_pairs={{0,8},{8,16},{16,24},{24,32},{32,40},{40,48},{48,56},{56,64},{64,7... | collective-permute-start | bytes 3080 | tf_op jit(solution)/shard_map/ppermute | solution.py:31
  80.2 3.0 %collective-permute-start.6 = (f32[8,32]{0,1:T(8,128)S(1)}, f32[8,32]{0,1:T(8,128)S(1)}, u32[]{:S(2)}, u32[]{:S(2)}) collective-permute-start(f32[8,32]{0,1:T(8,128)S(1)} %get-tuple-element.20), channel_id=1, source_target_pairs={{0,16},{8,24},{16,32},{24,40},{32,48},{40,56},{48,64},{56,72},{64,... | collective-permute-start | bytes 3080 | tf_op jit(solution)/shard_map/ppermute | solution.py:31
  83.3 3.6 %collective-permute-start.7 = (f32[8,32]{0,1:T(8,128)S(1)}, f32[8,32]{0,1:T(8,128)S(1)}, u32[]{:S(2)}, u32[]{:S(2)}) collective-permute-start(f32[8,32]{0,1:T(8,128)S(1)} %get-tuple-element.19), channel_id=1, source_target_pairs={{0,24},{8,32},{16,40},{24,48},{32,56},{40,64},{48,72},{56,80},{64,... | collective-permute-start | bytes 3080 | tf_op jit(solution)/shard_map/ppermute | solution.py:31
  86.9 4.2 %collective-permute-start = (bf16[8,128]{1,0:T(8,128)(2,1)S(1)}, bf16[8,128]{1,0:T(8,128)(2,1)S(1)}, u32[]{:S(2)}, u32[]{:S(2)}) collective-permute-start(bf16[8,128]{1,0:T(8,128)(2,1)S(1)} %get-tuple-element.16), channel_id=1, source_target_pairs={{0,8},{8,16},{16,24},{24,32},{32,40},{40,48},{48,56},{56,64},{64,7... | collective-permute-start | bytes 6152 | tf_op jit(solution)/shard_map/ppermute | solution.py:19
  91.1 1.9 %collective-permute-start.1 = (bf16[8,128]{1,0:T(8,128)(2,1)S(1)}, bf16[8,128]{1,0:T(8,128)(2,1)S(1)}, u32[]{:S(2)}, u32[]{:S(2)}) collective-permute-start(bf16[8,128]{1,0:T(8,128)(2,1)S(1)} %get-tuple-element.16), channel_id=1, source_target_pairs={{8,0},{16,8},{24,16},{32,24},{40,32},{48,40},{56,48},{64,56},{72,6... | collective-permute-start | bytes 6152 | tf_op jit(solution)/shard_map/ppermute | solution.py:21
  93.3 2.7 %collective-permute-done.1 = bf16[8,128]{1,0:T(8,128)(2,1)S(1)} collective-permute-done((bf16[8,128]{1,0:T(8,128)(2,1)S(1)}, bf16[8,128]{1,0:T(8,128)(2,1)S(1)}, u32[]{:S(2)}, u32[]{:S(2)}) %collective-permute-start.1) | collective-permute-done | bytes 2080 | tf_op jit(solution)/shard_map/ppermute | solution.py:21
  96.0 0.6 gather_fusion
  96.6 0.4 fusion.1
  97.0 0.6 multiply_reduce_fusion
  97.8 13.8 %all-reduce.2 = (f32[16]{0:T(128)S(1)}, f32[]{:T(128)}, f32[16,16]{1,0:T(8,128)S(1)}) all-reduce(f32[16]{0:T(128)S(1)} %convolution_bitcast_fusion.2, f32[]{:T(128)} %get-tuple-element.14, f32[16,16]{1,0:T(8,128)S(1)} %convolution_bitcast_fusion), channel_id=1, replica_groups=mesh['cl_0'=8,'cl_1'=8,'cl_2'=2,'grp'=8] {'cl_0'}, use_global_device_ids=true, to_apply=%region_0.1 | all-reduce | flops 273 | bytes 2184 | tf_op jit(solution)/shard_map/psum | solution.py:42
  111.5 16.6 %all-reduce.1 = (f32[16]{0:T(128)S(1)}, f32[]{:T(128)}, f32[16,16]{1,0:T(8,128)S(1)}) all-reduce(f32[16]{0:T(128)S(1)} %get-tuple-element.8, f32[]{:T(128)} %get-tuple-element.9, f32[16,16]{1,0:T(8,128)S(1)} %get-tuple-element.10), channel_id=1, replica_groups=mesh['cl_0'=8,'cl_1'=8,'cl_2'=2,'grp'=8] {'cl_1'}, use_global_device_ids=true, to_apply=%region_1.2 | all-reduce | flops 273 | bytes 2184 | tf_op jit(solution)/shard_map/psum | solution.py:42
  128.1 6.2 %all-reduce.3 = (f32[16]{0:T(128)S(1)}, f32[]{:T(128)}, f32[16,16]{1,0:T(8,128)S(1)}) all-reduce(f32[16]{0:T(128)S(1)} %get-tuple-element.5, f32[]{:T(128)} %get-tuple-element.6, f32[16,16]{1,0:T(8,128)S(1)} %get-tuple-element.7), channel_id=1, replica_groups=mesh['cl_0'=8,'cl_1'=8,'cl_2'=2,'grp'=8] {'cl_2'}, use_global_device_ids=true, to_apply=%region_2.3 | all-reduce | flops 273 | bytes 2184 | tf_op jit(solution)/shard_map/psum | solution.py:42
  134.3 15.8 %all-reduce = (f32[16]{0:T(128)S(1)}, f32[]{:T(128)}, f32[16,16]{1,0:T(8,128)S(1)}) all-reduce(f32[16]{0:T(128)S(1)} %get-tuple-element.11, f32[]{:T(128)} %get-tuple-element.12, f32[16,16]{1,0:T(8,128)S(1)} %get-tuple-element.13), channel_id=1, replica_groups=mesh['cl_0'=8,'cl_1'=8,'cl_2'=2,'grp'=8] {'grp'}, use_global_device_ids=true, to_apply=%region_3.4 | all-reduce | flops 273 | bytes 2184 | tf_op jit(solution)/shard_map/psum | solution.py:42
  150.1 0.6 broadcast_multiply_fusion
  150.9 0.7 fusion.3
  153.6 0.6 fusion.29
  154.2 0.6 pad_maximum_fusion.1
  (47 shorter events, 2.2 us)
Async XLA Ops:
  0.6 96.0 %copy-start = (bf16[1,8,4,128,128]{4,3,2,1,0:T(8,128)(2,1)S(1)}, bf16[1,8,4,128,128]{4,3,2,1,0:T(8,128)(2,1)}, u32[]{:S(2)}) copy-start(bf16[1,8,4,128,128]{4,3,2,1,0:T(8,128)(2,1)} %param.10) | copy-start | bytes 3145732
  0.6 0.9 copy-start.4
  1.7 64.4 %copy-start.6 = (s32[1,16]{1,0:T(1,128)S(1)}, s32[1,16]{1,0:T(1,128)}, u32[]{:S(2)}) copy-start(s32[1,16]{1,0:T(1,128)} %param.16) | copy-start | bytes 196
  1.7 64.5 %copy-start.2 = (bf16[1,16,1024]{2,1,0:T(8,128)(2,1)S(1)}, bf16[1,16,1024]{2,1,0:T(8,128)(2,1)}, u32[]{:S(2)}) copy-start(bf16[1,16,1024]{2,1,0:T(8,128)(2,1)} %param.14) | copy-start | bytes 98308
  68.8 11.5 %collective-permute-start.8 = (f32[8,32]{0,1:T(8,128)S(1)}, f32[8,32]{0,1:T(8,128)S(1)}, u32[]{:S(2)}, u32[]{:S(2)}) collective-permute-start(f32[8,32]{0,1:T(8,128)S(1)} %fusion.25), channel_id=1, source_target_pairs={{0,512},{8,520},{16,528},{24,536},{32,544},{40,552},{48,560},{56,5... | collective-permute-start | bytes 3080 | tf_op jit(solution)/shard_map/ppermute | solution.py:37
  71.9 8.0 %copy-start.1 = (f32[16,1,8,128]{3,2,1,0:T(8,128)S(1)}, f32[16,1,8,128]{3,2,1,0:T(8,128)}, u32[]{:S(2)}) copy-start(f32[16,1,8,128]{3,2,1,0:T(8,128)} %param.9) | copy-start | bytes 196612
  72.0 11.3 %collective-permute-start.2 = (f32[8,32]{0,1:T(8,128)S(1)}, f32[8,32]{0,1:T(8,128)S(1)}, u32[]{:S(2)}, u32[]{:S(2)}) collective-permute-start(f32[8,32]{0,1:T(8,128)S(1)} %get-tuple-element.23), channel_id=1, source_target_pairs={{16,0},{24,8},{32,16},{40,24},{48,32},{56,40},{64,48},{72,56},{80,... | collective-permute-start | bytes 3080 | tf_op jit(solution)/shard_map/ppermute | solution.py:31
  73.3 6.6 %copy-start.3 = (s32[1,8,4]{1,2,0:T(4,128)S(1)}, s32[1,8,4]{1,2,0:T(4,128)}, u32[]{:S(2)}) copy-start(s32[1,8,4]{1,2,0:T(4,128)} %param.11) | copy-start | bytes 388
  73.3 13.6 %collective-permute-start.3 = (f32[8,32]{0,1:T(8,128)S(1)}, f32[8,32]{0,1:T(8,128)S(1)}, u32[]{:S(2)}, u32[]{:S(2)}) collective-permute-start(f32[8,32]{0,1:T(8,128)S(1)} %get-tuple-element.18), channel_id=1, source_target_pairs={{8,0},{16,8},{24,16},{32,24},{40,32},{48,40},{56,48},{64,56},{72,6... | collective-permute-start | bytes 3080 | tf_op jit(solution)/shard_map/ppermute | solution.py:31
  75.6 15.5 %collective-permute-start.4 = (f32[8,32]{0,1:T(8,128)S(1)}, f32[8,32]{0,1:T(8,128)S(1)}, u32[]{:S(2)}, u32[]{:S(2)}) collective-permute-start(f32[8,32]{0,1:T(8,128)S(1)} %get-tuple-element.22), channel_id=1, source_target_pairs={{0,0},{8,8},{16,16},{24,24},{32,32},{40,40},{48,48},{56,56},{64,64... | collective-permute-start | bytes 3080 | tf_op jit(solution)/shard_map/ppermute | solution.py:31
  75.7 17.4 %collective-permute-start.5 = (f32[8,32]{0,1:T(8,128)S(1)}, f32[8,32]{0,1:T(8,128)S(1)}, u32[]{:S(2)}, u32[]{:S(2)}) collective-permute-start(f32[8,32]{0,1:T(8,128)S(1)} %get-tuple-element.21), channel_id=1, source_target_pairs={{0,8},{8,16},{16,24},{24,32},{32,40},{40,48},{48,56},{56,64},{64,7... | collective-permute-start | bytes 3080 | tf_op jit(solution)/shard_map/ppermute | solution.py:31
  80.2 12.8 %collective-permute-start.6 = (f32[8,32]{0,1:T(8,128)S(1)}, f32[8,32]{0,1:T(8,128)S(1)}, u32[]{:S(2)}, u32[]{:S(2)}) collective-permute-start(f32[8,32]{0,1:T(8,128)S(1)} %get-tuple-element.20), channel_id=1, source_target_pairs={{0,16},{8,24},{16,32},{24,40},{32,48},{40,56},{48,64},{56,72},{64,... | collective-permute-start | bytes 3080 | tf_op jit(solution)/shard_map/ppermute | solution.py:31
  83.3 9.8 %collective-permute-start.7 = (f32[8,32]{0,1:T(8,128)S(1)}, f32[8,32]{0,1:T(8,128)S(1)}, u32[]{:S(2)}, u32[]{:S(2)}) collective-permute-start(f32[8,32]{0,1:T(8,128)S(1)} %get-tuple-element.19), channel_id=1, source_target_pairs={{0,24},{8,32},{16,40},{24,48},{32,56},{40,64},{48,72},{56,80},{64,... | collective-permute-start | bytes 3080 | tf_op jit(solution)/shard_map/ppermute | solution.py:31
  86.9 6.3 %copy-start.5 = (bf16[1,8,32,128]{3,2,1,0:T(8,128)(2,1)S(1)}, bf16[1,8,32,128]{3,2,1,0:T(8,128)(2,1)}, u32[]{:S(2)}) copy-start(bf16[1,8,32,128]{3,2,1,0:T(8,128)(2,1)} %param.13) | copy-start | bytes 196612
  86.9 6.4 %collective-permute-start = (bf16[8,128]{1,0:T(8,128)(2,1)S(1)}, bf16[8,128]{1,0:T(8,128)(2,1)S(1)}, u32[]{:S(2)}, u32[]{:S(2)}) collective-permute-start(bf16[8,128]{1,0:T(8,128)(2,1)S(1)} %get-tuple-element.16), channel_id=1, source_target_pairs={{0,8},{8,16},{16,24},{24,32},{32,40},{40,48},{48,56},{56,64},{64,7... | collective-permute-start | bytes 6152 | tf_op jit(solution)/shard_map/ppermute | solution.py:19
  91.1 4.9 %collective-permute-start.1 = (bf16[8,128]{1,0:T(8,128)(2,1)S(1)}, bf16[8,128]{1,0:T(8,128)(2,1)S(1)}, u32[]{:S(2)}, u32[]{:S(2)}) collective-permute-start(bf16[8,128]{1,0:T(8,128)(2,1)S(1)} %get-tuple-element.16), channel_id=1, source_target_pairs={{8,0},{16,8},{24,16},{32,24},{40,32},{48,40},{56,48},{64,56},{72,6... | collective-permute-start | bytes 6152 | tf_op jit(solution)/shard_map/ppermute | solution.py:21
where the time goes:
time: 157 us; the launch traced here: 155 us
  blocking collectives  117 us (75%)
  starting transfers between devices  23.3 us (15%)
  between operations  3.57 us (2%)
  local copies, waits for them, and re-layouts  3.33 us (2%)
  waiting for transfers between devices  2.74 us (2%)
  matrix products  2.6 us (2%)
  other arithmetic  2.47 us (2%)
    all_gather x1, blocking collectives, on_device(): all_expansion = lax.all_gather(expansion, CL, axis=0, tiled=True)  64.4 us
    psum x4, blocking collectives, over_axes(): array = lax.psum(array, axis)  52.3 us
    ppermute x6, starting transfers between devices, passed_along(): return lax.ppermute(block, axis, route)  14.4 us
    ppermute x1, starting transfers between devices, with_halo(): lax.ppermute(tail, axis, [(i, (i + 1) % count) for i in range(ends)])  4.17 us
  transfers between devices with their start and end apart: 9, of which 1 were waited for; matrix products, arithmetic and copies ran while one was open for 1% of the time, Pallas kernels for 0%

commit v1 on v0

v1 whole, which is shorter than its diff:
```python
import jax
import jax.numpy as jnp
from jax import lax
from jax.sharding import Mesh
from jax.sharding import PartitionSpec as P

CL = ("z", "x", "core")
ROW = ("x", "core")
COLUMN = ("z", "grp")
HIGHEST = lax.Precision.HIGHEST


def neighbour(value, step):
    count = lax.axis_size(CL)
    route = [(i, i + step) for i in range(count) if 0 <= i + step < count]
    return lax.ppermute(value, CL, route)


def exchange(rows, axes):
    return lax.all_to_all(rows, axes, 0, 0, tiled=True)


def summed(row, axes):
    sent = jnp.broadcast_to(row, (lax.axis_size(axes), row.shape[1]))
    return jnp.sum(exchange(sent, axes), axis=0, keepdims=True)


def on_device(
    basis,
    near_blocks,
    near_list,
    source_basis,
    target_basis,
    coupling,
    far_target,
    far_source,
    far_count,
):
    basis_count = basis.shape[0]
    clusters = basis.shape[2]
    panels_cl = basis.shape[3]
    ranks = source_basis.shape[2]
    slots = coupling.shape[1]
    owners = lax.axis_size(CL)
    me = lax.axis_index(CL)
    current = basis[basis_count - 1, 0]
    current_bf = current.astype(jnp.bfloat16)
    before = neighbour(current_bf, 1)
    after = neighbour(current_bf, -1)
    expansion = jnp.einsum(
        "srp,sp->sr", source_basis[0], current_bf, preferred_element_type=jnp.float32
    ).astype(jnp.bfloat16)
    row = expansion.astype(jnp.float32).reshape(1, clusters * ranks)
    everyone = exchange(jnp.broadcast_to(row, (owners, clusters * ranks)), CL)
    picked = everyone.reshape(owners * clusters, ranks)[far_source[0]].astype(jnp.bfloat16)
    slot = jnp.arange(slots, dtype=jnp.int32)
    live = (slot < far_count[0, 0]).astype(jnp.float32)
    term = (
        jnp.einsum(
            "bij,bj->bi",
            coupling[0].reshape(slots, ranks, ranks),
            picked,
            preferred_element_type=jnp.float32,
        )
        * live[:, None]
    )
    targets = lax.dynamic_slice_in_dim(far_target[0], me * slots, slots)
    selector = jnp.arange(owners * clusters, dtype=jnp.int32)[:, None] == targets[None, :]
    sums = jnp.dot(selector.astype(jnp.float32), term, precision=HIGHEST)
    arrived = exchange(sums.reshape(owners, clusters * ranks), CL)
    coupled = jnp.sum(arrived, axis=0).reshape(clusters, ranks).astype(jnp.bfloat16)
    far_part = jnp.einsum(
        "tr,trp->tp", coupled, target_basis[0], preferred_element_type=jnp.float32
    )
    window = jnp.concatenate([before, current_bf, after], axis=0)
    near_part = jnp.einsum(
        "tkij,tkj->ti", near_blocks[0], window[near_list[0]], preferred_element_type=jnp.float32
    )
    image = (0.5 * current + near_part + far_part).reshape(1, -1)
    flat_basis = basis[:, 0].reshape(basis_count, clusters * panels_cl)
    both = jnp.concatenate([flat_basis, image], axis=0)
    inner = jnp.dot(both, both.T, precision=HIGHEST)
    packed = jnp.concatenate([inner[k : k + 1] for k in range(basis_count + 1)], axis=1)
    total = summed(summed(packed, ROW), COLUMN).reshape(basis_count + 1, basis_count + 1)
    panels = float(owners * lax.axis_size("grp") * clusters * panels_cl)
    products = total[basis_count, :basis_count]
    gram = total[:basis_count, :basis_count]
    projection = products / panels
    remainder = image[0] - jnp.dot(projection, flat_basis, precision=HIGHEST)
    squares = (
        total[basis_count, basis_count]
        - 2.0 * jnp.sum(projection * products)
        + jnp.sum(projection * jnp.sum(gram * projection[None, :], axis=1))
    )
    new_norm = jnp.sqrt(squares / panels + 1e-06)
    next_vector = (remainder / new_norm).reshape(1, clusters, panels_cl)
    return (next_vector, jnp.concatenate([projection, new_norm[None]]))


def solution(mesh):
    torus = Mesh(mesh.devices.reshape(8, 8, 2, mesh.shape["grp"]), (*CL, "grp"))
    in_specs = (
        P(None, "grp", CL, None),
        P("grp", CL, None, None, None),
        P("grp", CL, None),
        P("grp", CL, None, None),
        P("grp", CL, None, None),
        P("grp", CL, None),
        P("grp", None),
        P("grp", CL),
        P("grp", CL),
    )
    return jax.shard_map(
        on_device,
        mesh=torus,
        in_specs=in_specs,
        out_specs=(P("grp", CL, None), P()),
        check_vma=False,
    )
```

time: 157 us -> 105 us (0.67); the launches traced: 155 us -> 105 us
  blocking collectives: 117 us -> 30.7 us
  waiting for transfers between devices: 2.74 us -> 21.6 us
  starting transfers between devices: 23.3 us -> 36.9 us
  local copies, waits for them, and re-layouts: 3.33 us -> 7.04 us
    all_gather x1 -> x0, blocking collectives: 64.4 us -> none  [on_device(): all_expansion = lax.all_gather(expansion, CL, axis=0, tiled=True)]
    psum x4 -> x0, blocking collectives: 52.3 us -> none  [over_axes(): array = lax.psum(array, axis)]
    all_to_all x0 -> x2, blocking collectives: none -> 30.7 us  [exchange(): return lax.all_to_all(rows, axes, 0, 0, tiled=True)]
    all_to_all x0 -> x2, waiting for transfers between devices: none -> 21.6 us  [exchange(): return lax.all_to_all(rows, axes, 0, 0, tiled=True)]
    all_to_all x0 -> x2, starting transfers between devices: none -> 19.6 us  [exchange(): return lax.all_to_all(rows, axes, 0, 0, tiled=True)]
    ppermute x9 -> x2, starting transfers between devices: 23.3 us -> 17.3 us  [neighbour(): return lax.ppermute(value, CL, route)]
    ppermute x9 -> x2, waiting for transfers between devices: 2.74 us -> 0.01 us  [neighbour(): return lax.ppermute(value, CL, route)]
  transfers between devices with their start and end apart: 9 -> 4, of which waited for: 1 -> 2; matrix products, arithmetic and copies ran while one was open for 1% -> 5% of each run, Pallas kernels for 0% -> 0%
where the time goes in v1:
time: 105 us
  starting transfers between devices  36.9 us (35%)
  blocking collectives  30.7 us (29%)
  waiting for transfers between devices  21.6 us (21%)
  local copies, waits for them, and re-layouts  7.04 us (7%)
  between operations  3.54 us (3%)
  other arithmetic  2.67 us (3%)
  matrix products  2.45 us (2%)
    all_to_all x2, blocking collectives, exchange(): return lax.all_to_all(rows, axes, 0, 0, tiled=True)  30.7 us
    all_to_all x2, waiting for transfers between devices, exchange(): return lax.all_to_all(rows, axes, 0, 0, tiled=True)  21.6 us
    all_to_all x2, starting transfers between devices, exchange(): return lax.all_to_all(rows, axes, 0, 0, tiled=True)  19.6 us
    ppermute x2, starting transfers between devices, neighbour(): return lax.ppermute(value, CL, route)  17.3 us
  transfers between devices with their start and end apart: 4, of which 2 were waited for; matrix products, arithmetic and copies ran while one was open for 5% of the time, Pallas kernels for 0%

profile of v1, /device:TPU:1, one launch (start us, length us, event | category | flops | bytes accessed | tf_op | source)
XLA Modules:
  0.0 104.8 jit_solution(7664094213000679475)
XLA Ops:
  0.6 0.8 fusion.23
  1.4 4.5 %collective-permute-start = (bf16[8,128]{1,0:T(8,128)(2,1)S(1)}, bf16[8,128]{1,0:T(8,128)(2,1)S(1)}, u32[]{:S(2)}, u32[]{:S(2)}) collective-permute-start(bf16[8,128]{1,0:T(8,128)(2,1)S(1)} %get-tuple-element.4), channel_id=1, source_target_pairs={{0,8},{8,16},{16,24},{24,32},{32,40},{40,48},{48,56},{56,64},{64,7... | collective-permute-start | bytes 6152 | tf_op jit(solution)/shard_map/ppermute | solution.py:16
  5.9 12.8 %collective-permute-start.1 = (bf16[8,128]{1,0:T(8,128)(2,1)S(1)}, bf16[8,128]{1,0:T(8,128)(2,1)S(1)}, u32[]{:S(2)}, u32[]{:S(2)}) collective-permute-start(bf16[8,128]{1,0:T(8,128)(2,1)S(1)} %get-tuple-element.4), channel_id=1, source_target_pairs={{8,0},{16,8},{24,16},{32,24},{40,32},{48,40},{56,48},{64,56},{72,6... | collective-permute-start | bytes 6152 | tf_op jit(solution)/shard_map/ppermute | solution.py:16
  18.8 1.0 fusion.10
  19.8 0.7 broadcast_in_dim.14
  20.6 14.0 %all-to-all-start = ((f32[128,1,256]{2,1,0:T(1,128)}), f32[128,1,256]{2,1,0:T(1,128)S(1)}, u32[]{:S(2)}, u32[]{:S(2)}) async-start(f32[128,1,256]{2,1,0:T(1,128)} %broadcast_in_dim.14), calls=%async_computation | async-start | bytes 262144 | tf_op jit(solution)/shard_map/all_to_all | solution.py:20
  35.3 0.7 copy-done.3
  36.0 0.7 dynamic-slice_bitcast_fusion
  37.0 0.5 copy-done.1
  37.6 9.7 %all-to-all-done = f32[128,1,256]{2,1,0:T(1,128)S(1)} async-done(((f32[128,1,256]{2,1,0:T(1,128)}), f32[128,1,256]{2,1,0:T(1,128)S(1)}, u32[]{:S(2)}, u32[]{:S(2)}) %all-to-all-start) | async-done | bytes 131104 | tf_op jit(solution)/shard_map/all_to_all | solution.py:20
  47.3 0.3 reduce.3
  47.8 0.6 gather_fusion.1
  48.5 0.5 fusion.2
  49.0 0.9 all_to_all.23
  49.9 5.6 %all-to-all-start.1 = ((f32[128,1,256]{2,1,0:T(1,128)}), f32[128,1,256]{2,1,0:T(1,128)S(1)}, u32[]{:S(2)}, u32[]{:S(2)}) async-start(f32[128,1,256]{2,1,0:T(1,128)} %all_to_all.23), calls=%async_computation.1 | async-start | bytes 262144 | tf_op jit(solution)/shard_map/all_to_all | solution.py:20
  55.5 0.6 gather_fusion
  56.1 0.4 fusion
  56.5 11.8 %all-to-all-done.1 = f32[128,1,256]{2,1,0:T(1,128)S(1)} async-done(((f32[128,1,256]{2,1,0:T(1,128)}), f32[128,1,256]{2,1,0:T(1,128)S(1)}, u32[]{:S(2)}, u32[]{:S(2)}) %all-to-all-start.1) | async-done | bytes 131104 | tf_op jit(solution)/shard_map/all_to_all | solution.py:20
  69.1 10.3 %all_to_all.28 = f32[16,1,289]{2,1,0:T(1,128)S(1)} all-to-all(f32[16,1,289]{2,1,0:T(1,128)S(1)} %broadcast_in_dim.15), channel_id=1, replica_groups=mesh['z'=8,'x'=8,'core'=2,'grp'=8] {'x','core'}, dimensions={0} | all-to-all | bytes 36992 | tf_op jit(solution)/shard_map/all_to_all | solution.py:20
  79.5 20.3 %all_to_all.29 = f32[64,1,289]{2,1,0:T(1,128)S(1)} all-to-all(f32[64,1,289]{2,1,0:T(1,128)S(1)} %broadcast_in_dim.16), channel_id=1, replica_groups=mesh['z'=8,'x'=8,'core'=2,'grp'=8] {'z','grp'}, dimensions={0} | all-to-all | bytes 147968 | tf_op jit(solution)/shard_map/all_to_all | solution.py:20
  100.0 0.6 slice.106
  100.9 0.7 multiply_reduce_fusion
  103.6 0.6 fusion.18
  104.2 0.6 pad_maximum_fusion.1
  (42 shorter events, 2.1 us)
Async XLA Ops:
  0.6 55.4 %copy-start = (bf16[1,8,4,128,128]{4,3,2,1,0:T(8,128)(2,1)S(1)}, bf16[1,8,4,128,128]{4,3,2,1,0:T(8,128)(2,1)}, u32[]{:S(2)}) copy-start(bf16[1,8,4,128,128]{4,3,2,1,0:T(8,128)(2,1)} %param.10) | copy-start | bytes 3145732
  1.4 54.0 %collective-permute-start = (bf16[8,128]{1,0:T(8,128)(2,1)S(1)}, bf16[8,128]{1,0:T(8,128)(2,1)S(1)}, u32[]{:S(2)}, u32[]{:S(2)}) collective-permute-start(bf16[8,128]{1,0:T(8,128)(2,1)S(1)} %get-tuple-element.4), channel_id=1, source_target_pairs={{0,8},{8,16},{16,24},{24,32},{32,40},{40,48},{48,56},{56,64},{64,7... | collective-permute-start | bytes 6152 | tf_op jit(solution)/shard_map/ppermute | solution.py:16
  5.9 49.5 %collective-permute-start.1 = (bf16[8,128]{1,0:T(8,128)(2,1)S(1)}, bf16[8,128]{1,0:T(8,128)(2,1)S(1)}, u32[]{:S(2)}, u32[]{:S(2)}) collective-permute-start(bf16[8,128]{1,0:T(8,128)(2,1)S(1)} %get-tuple-element.4), channel_id=1, source_target_pairs={{8,0},{16,8},{24,16},{32,24},{40,32},{48,40},{56,48},{64,56},{72,6... | collective-permute-start | bytes 6152 | tf_op jit(solution)/shard_map/ppermute | solution.py:16
  20.6 14.0 %copy-start.5 = (s32[1,16]{1,0:T(1,128)S(1)}, s32[1,16]{1,0:T(1,128)}, u32[]{:S(2)}) copy-start(s32[1,16]{1,0:T(1,128)} %param.16) | copy-start | bytes 196
  20.6 26.7 %all-to-all-start = ((f32[128,1,256]{2,1,0:T(1,128)}), f32[128,1,256]{2,1,0:T(1,128)S(1)}, u32[]{:S(2)}, u32[]{:S(2)}) async-start(f32[128,1,256]{2,1,0:T(1,128)} %broadcast_in_dim.14), calls=%async_computation | async-start | bytes 262144 | tf_op jit(solution)/shard_map/all_to_all | solution.py:20
  34.6 2.1 %copy-start.2 = (bf16[1,16,1024]{2,1,0:T(8,128)(2,1)S(1)}, bf16[1,16,1024]{2,1,0:T(8,128)(2,1)}, u32[]{:S(2)}) copy-start(bf16[1,16,1024]{2,1,0:T(8,128)(2,1)} %param.14) | copy-start | bytes 98308
  35.3 0.7 copy-start.3
  36.7 0.8 copy-start.1
  49.9 18.4 %all-to-all-start.1 = ((f32[128,1,256]{2,1,0:T(1,128)}), f32[128,1,256]{2,1,0:T(1,128)S(1)}, u32[]{:S(2)}, u32[]{:S(2)}) async-start(f32[128,1,256]{2,1,0:T(1,128)} %all_to_all.23), calls=%async_computation.1 | async-start | bytes 262144 | tf_op jit(solution)/shard_map/all_to_all | solution.py:20
  56.5 12.1 %copy-start.4 = (bf16[1,8,32,128]{3,2,1,0:T(8,128)(2,1)S(1)}, bf16[1,8,32,128]{3,2,1,0:T(8,128)(2,1)}, u32[]{:S(2)}) copy-start(bf16[1,8,32,128]{3,2,1,0:T(8,128)(2,1)} %param.13) | copy-start | bytes 196612

commit v2 on v1

v2 whole, which is shorter than its diff:
```python
import jax
import jax.numpy as jnp
from jax import lax
from jax.experimental import pallas as pl
from jax.experimental.pallas import tpu as pltpu
from jax.sharding import Mesh
from jax.sharding import PartitionSpec as P

CL = ("z", "x", "core")
ROW = ("x", "core")
COLUMN = ("z", "grp")
HIGHEST = lax.Precision.HIGHEST
LANES = 128
FIRST, LAST = -2, 3

SMALL = pltpu.CompilerParams(vmem_limit_bytes=4 * 1024 * 1024)
VMEM = pl.BlockSpec(memory_space=pltpu.VMEM)
SMEM = pl.BlockSpec(memory_space=pltpu.SMEM)


def iota(shape, dim):
    return lax.broadcasted_iota(jnp.int32, shape, dim)


def dot(a, b, contract=((1,), (0,)), precision=None):
    return lax.dot_general(
        a, b, (contract, ((), ())), precision=precision, preferred_element_type=jnp.float32
    )


def ones_where(mask, dtype):
    return jnp.where(mask, 1.0, 0.0).astype(dtype)


def position():
    return lax.axis_index("z") * 16 + lax.axis_index("x") * 2 + lax.axis_index("core")


def expand_kernel(basis_ref, source_ref, sent_ref, current_ref):
    current = basis_ref[0, 0].astype(jnp.bfloat16)
    current_ref[...] = current
    clusters, panels = current.shape
    ranks = source_ref.shape[2]
    width = clusters * ranks
    source = source_ref[0].reshape(width, panels)
    every = dot(current, source, ((1,), (1,)))
    own = iota((clusters, width), 1) // ranks == iota((clusters, width), 0)
    row = jnp.sum(jnp.where(own, every, 0.0), axis=0, keepdims=True)
    row = row.astype(jnp.bfloat16).astype(jnp.float32)
    sent_ref[...] = jnp.broadcast_to(row[None], sent_ref.shape)


def far_kernel(
    clusters, owners, source_ref, target_ref, count_ref, expansion_ref, coupling_ref, sent_ref
):
    slots = coupling_ref.shape[1]
    width = expansion_ref.shape[2]
    ranks = width // clusters
    groups = LANES // ranks
    parts = ranks // groups
    me = position()
    lane_cluster = iota((1, width), 1) // ranks
    picked, targets = [], []
    for b in range(slots):
        source = source_ref[0, b]
        row = expansion_ref[source // clusters]
        picked.append(jnp.where(lane_cluster == source % clusters, row, 0.0))
        target = jnp.where(b < count_ref[0, 0], target_ref[0, b], -1)
        targets.append(jnp.full((1, width), target, jnp.int32))
    picked = jnp.concatenate(picked, axis=0).astype(jnp.bfloat16)
    targets = jnp.concatenate(targets, axis=0)
    spread = iota((width, LANES), 0) % ranks == iota((width, LANES), 1) % ranks
    vector = dot(picked, ones_where(spread, jnp.bfloat16))
    coupling = coupling_ref[0].astype(jnp.float32)
    high, low = [], []
    for q in range(parts):
        product = coupling[:, q * LANES : (q + 1) * LANES] * vector
        top = product.astype(jnp.bfloat16)
        high.append(top)
        low.append((product - top.astype(jnp.float32)).astype(jnp.bfloat16))
    gather = iota((LANES, width), 0) // ranks == iota((LANES, width), 1) % groups
    sums = dot(jnp.concatenate(high + low, axis=0), ones_where(gather, jnp.bfloat16))
    part = (iota((slots, width), 1) % ranks) // groups
    term = jnp.zeros((slots, width), jnp.float32)
    for q in range(parts):
        value = sums[q * slots : (q + 1) * slots] + sums[(parts + q) * slots : (parts + q + 1) * slots]
        term = jnp.where(part == q, value, term)
    sent_ref[...] = jnp.zeros_like(sent_ref)

    def send(owner):
        mine = targets == owner * clusters + lane_cluster
        sent_ref[owner] = jnp.sum(jnp.where(mine, term, 0.0), axis=0, keepdims=True)

    for step in range(FIRST, LAST + 1):
        owner = me + step

        @pl.when(jnp.logical_and(owner >= 0, owner < owners))
        def _():
            send(owner)

    send(lax.rem(me + owners // 2, owners))


def gram_kernel(basis_ref, gram_ref):
    count, _, clusters, _ = basis_ref.shape
    gram = jnp.zeros((count, count), jnp.float32)
    for c in range(clusters):
        rows = basis_ref[:, 0, c, :]
        gram = gram + dot(rows, rows, ((1,), (1,)), HIGHEST)
    width = count * count
    tile = iota((count, width), 1) % count == iota((count, width), 0)
    rows = dot(gram, ones_where(tile, jnp.float32), precision=HIGHEST)
    own = iota((count, width), 1) // count == iota((count, width), 0)
    gram_ref[...] = jnp.sum(jnp.where(own, rows, 0.0), axis=0, keepdims=True)


def image_kernel(owners, basis_ref, target_ref, arrived_ref, near_ref, gram_ref, image_ref, sent_ref):
    count = basis_ref.shape[0]
    clusters, panels = near_ref.shape
    ranks = target_ref.shape[2]
    width = clusters * ranks
    me = position()
    coupled = arrived_ref[lax.rem(me + owners // 2, owners)]
    for step in range(-LAST, -FIRST + 1):
        owner = me + step
        inside = jnp.logical_and(owner >= 0, owner < owners)
        value = arrived_ref[jnp.clip(owner, 0, owners - 1)]
        coupled = coupled + jnp.where(inside, value, 0.0)
    own = iota((clusters, width), 1) // ranks == iota((clusters, width), 0)
    spread = jnp.where(own, coupled, 0.0).astype(jnp.bfloat16)
    far = dot(spread, target_ref[0].reshape(width, panels))
    image = 0.5 * basis_ref[count - 1, 0] + near_ref[...] + far
    image_ref[...] = image
    rows = [jnp.sum(basis_ref[k, 0] * image, axis=0, keepdims=True) for k in range(count)]
    rows.append(jnp.sum(image * image, axis=0, keepdims=True))
    rows.append(jnp.zeros((LANES - count - 1, panels), jnp.float32))
    products = dot(
        jnp.ones((8, panels), jnp.float32), jnp.concatenate(rows, axis=0), ((1,), (1,)), HIGHEST
    )
    row = jnp.concatenate([gram_ref[...], products[:1]], axis=1)
    sent_ref[...] = jnp.broadcast_to(row[None], sent_ref.shape)


def total_kernel(arrived_ref, sent_ref):
    sent_ref[...] = jnp.broadcast_to(
        jnp.sum(arrived_ref[...], axis=0, keepdims=True), sent_ref.shape
    )


def final_kernel(all_panels, basis_ref, image_ref, arrived_ref, next_ref, hessenberg_ref):
    count = basis_ref.shape[0]
    width = count * count
    total = jnp.sum(arrived_ref[...], axis=0)
    gram = total[:, :width]
    products = total[:, width:]
    lane = iota((1, LANES), 1)
    projection = jnp.where(lane < count, products / all_panels, 0.0)
    square = jnp.sum(jnp.where(lane == count, products, 0.0), axis=1, keepdims=True)
    index = iota((LANES, width), 1)
    which = iota((LANES, width), 0)
    many = jnp.broadcast_to(projection, (8, LANES))
    outer = dot(many, ones_where(index // count == which, jnp.float32), precision=HIGHEST)
    inner = dot(many, ones_where(index % count == which, jnp.float32), precision=HIGHEST)
    squares = (
        square
        - 2.0 * jnp.sum(projection * products, axis=1, keepdims=True)
        + jnp.sum(gram * outer[:1] * inner[:1], axis=1, keepdims=True)
    )
    new_norm = jnp.sqrt(squares / all_panels + 1e-06)
    remainder = image_ref[...]
    for k in range(count):
        remainder = remainder - projection[:, k : k + 1] * basis_ref[k, 0]
    next_ref[0] = remainder / new_norm
    column = jnp.where(lane == count, new_norm, projection)
    hessenberg_ref[...] = column[:, : count + 1]


def exchange(rows, axes):
    return lax.all_to_all(rows, axes, 0, 0)


def neighbour(value, step):
    count = lax.axis_size(CL)
    route = [(i, i + step) for i in range(count) if 0 <= i + step < count]
    return lax.ppermute(value, CL, route)


def f32(*shape):
    return jax.ShapeDtypeStruct(shape, jnp.float32)


def on_device(
    basis,
    near_blocks,
    near_list,
    source_basis,
    target_basis,
    coupling,
    far_target,
    far_source,
    far_count,
):
    count, _, clusters, panels = basis.shape
    ranks = source_basis.shape[2]
    slots = coupling.shape[1]
    owners = lax.axis_size(CL)
    width = clusters * ranks
    packed = count * count + LANES

    sent, current = pl.pallas_call(
        expand_kernel,
        grid=(1,),
        in_specs=[
            pl.BlockSpec((1, 1, clusters, panels), lambda i: (count - 1, 0, 0, 0)),
            pl.BlockSpec(source_basis.shape, lambda i: (0, 0, 0, 0)),
        ],
        out_specs=[
            pl.BlockSpec((owners, 1, width), lambda i: (0, 0, 0)),
            pl.BlockSpec((clusters, panels), lambda i: (0, 0)),
        ],
        out_shape=[f32(owners, 1, width), jax.ShapeDtypeStruct((clusters, panels), jnp.bfloat16)],
        name="expand",
    )(basis, source_basis)
    expansions = exchange(sent, CL)
    before = neighbour(current, 1)
    after = neighbour(current, -1)

    me = lax.axis_index(CL)
    targets = lax.dynamic_slice_in_dim(far_target, me * slots, slots, axis=1)
    sent = pl.pallas_call(
        lambda *refs: far_kernel(clusters, owners, *refs),
        in_specs=[SMEM, SMEM, SMEM, VMEM, VMEM],
        out_specs=VMEM,
        out_shape=f32(owners, 1, width),
        compiler_params=SMALL,
        name="far",
    )(far_source, targets, far_count, expansions, coupling)
    arrived = exchange(sent, CL)

    window = jnp.concatenate([before, current, after], axis=0)
    near = jnp.einsum(
        "tkij,tkj->ti", near_blocks[0], window[near_list[0]], preferred_element_type=jnp.float32
    )
    gram = pl.pallas_call(
        gram_kernel, in_specs=[VMEM], out_specs=VMEM, out_shape=f32(1, count * count), compiler_params=SMALL, name="gram"
    )(basis)
    image, sent = pl.pallas_call(
        lambda *refs: image_kernel(owners, *refs),
        in_specs=[VMEM] * 5,
        out_specs=[VMEM] * 2,
        out_shape=[f32(clusters, panels), f32(lax.axis_size(ROW), 1, packed)],
        compiler_params=SMALL,
        name="image",
    )(basis, target_basis, arrived, near, gram)
    sent = pl.pallas_call(
        total_kernel,
        in_specs=[VMEM],
        out_specs=VMEM,
        out_shape=f32(lax.axis_size(COLUMN), 1, packed),
        compiler_params=SMALL,
        name="total",
    )(exchange(sent, ROW))
    all_panels = float(owners * lax.axis_size("grp") * clusters * panels)
    next_vector, hessenberg = pl.pallas_call(
        lambda *refs: final_kernel(all_panels, *refs),
        in_specs=[VMEM] * 3,
        out_specs=[VMEM] * 2,
        out_shape=[f32(1, clusters, panels), f32(1, count + 1)],
        compiler_params=SMALL,
        name="final",
    )(basis, image, exchange(sent, COLUMN))
    return (next_vector, hessenberg.reshape(count + 1))


def solution(mesh):
    torus = Mesh(mesh.devices.reshape(8, 8, 2, mesh.shape["grp"]), (*CL, "grp"))
    in_specs = (
        P(None, "grp", CL, None),
        P("grp", CL, None, None, None),
        P("grp", CL, None),
        P("grp", CL, None, None),
        P("grp", CL, None, None),
        P("grp", CL, None),
        P("grp", None),
        P("grp", CL),
        P("grp", CL),
    )
    return jax.shard_map(
        on_device,
        mesh=torus,
        in_specs=in_specs,
        out_specs=(P("grp", CL, None), P()),
        check_vma=False,
    )
```

time: 105 us -> 99.2 us (0.945)
  local copies, waits for them, and re-layouts: 7.04 us -> 1.53 us
  Pallas kernels: 0 us -> 5.21 us
  other arithmetic: 2.67 us -> 0.02 us
  between operations: 3.54 us -> 1.44 us
  matrix products: 2.45 us -> 0.37 us
    pallas_call x0 -> x6, Pallas kernels: none -> 5.21 us  [the longest x1 1.8 us: on_device(): pl.pallas_call(expand_kernel, grid=(1,), in_specs=[pl.BlockSpec((1, 1, cl...]
    dot_general x6 -> x0, matrix products: 2.07 us -> none  [the longest x1 0.97 us: on_device(): jnp.einsum('srp,sp->sr', source_basis[0], current_bf, preferred_element_t...]
    unnamed x13 -> x14, local copies, waits for them, and re-layouts: 1.22 us -> 0.04 us
    reduce_sum x5 -> x0, other arithmetic: 1.1 us -> none  [the longest x1 0.69 us: on_device(): jnp.sum(projection * jnp.sum(gram * projection[None, :], axis=1))]
  transfers between devices with their start and end apart: 4 -> 4, of which waited for: 2 -> 2; matrix products, arithmetic and copies ran while one was open for 5% -> 2% of each run, Pallas kernels for 0% -> 2%
where the time goes in v2:
time: 99.2 us; the launch traced here: 98.7 us
  starting transfers between devices  37 us (37%)
  blocking collectives  30.7 us (31%)
  waiting for transfers between devices  22.5 us (23%)
  Pallas kernels  5.21 us (5%)
  local copies, waits for them, and re-layouts  1.53 us (2%)
  between operations  1.44 us (1%)
    all_to_all x2, blocking collectives, exchange(): return lax.all_to_all(rows, axes, 0, 0)  30.7 us
    all_to_all x2, waiting for transfers between devices, exchange(): return lax.all_to_all(rows, axes, 0, 0)  22.5 us
    all_to_all x2, starting transfers between devices, exchange(): return lax.all_to_all(rows, axes, 0, 0)  19.7 us
    ppermute x2, starting transfers between devices, neighbour(): return lax.ppermute(value, CL, route)  17.3 us
  transfers between devices with their start and end apart: 4, of which 2 were waited for; matrix products, arithmetic and copies ran while one was open for 2% of the time, Pallas kernels for 2%

profile of v2, /device:TPU:1, one launch (start us, length us, event | category | flops | bytes accessed | tf_op | source)
XLA Modules:
  0.0 98.7 jit_solution(2004652762350926363)
XLA Ops:
  0.6 0.0 copy-start
  0.6 1.8 %expand.1 = (f32[128,1,256]{2,1,0:T(1,128)}, bf16[8,128]{1,0:T(8,128)(2,1)}) custom-call(f32[16,1,8,128]{3,2,1,0:T(8,128)} %refs_0_.5, bf16[1,8,32,128]{3,2,1,0:T(8,128)(2,1)} %source_ref.1), custom_call_target="tpu_custom_call" | custom-call | tf_op jit(solution)/shard_map/expand/pallas_call | solution.py:210
  2.4 4.5 %collective-permute-start = (bf16[8,128]{1,0:T(8,128)(2,1)}, bf16[8,128]{1,0:T(8,128)(2,1)S(1)}, u32[]{:S(2)}, u32[]{:S(2)}) collective-permute-start(bf16[8,128]{1,0:T(8,128)(2,1)} %get-tuple-element.9), channel_id=1, source_target_pairs={{0,8},{8,16},{16,24},{24,32},{32,40},{40,48},{48,56},{56,64},{64,7... | collective-permute-start | bytes 6152 | tf_op jit(solution)/shard_map/ppermute | solution.py:185
  7.0 12.8 %collective-permute-start.1 = (bf16[8,128]{1,0:T(8,128)(2,1)}, bf16[8,128]{1,0:T(8,128)(2,1)S(1)}, u32[]{:S(2)}, u32[]{:S(2)}) collective-permute-start(bf16[8,128]{1,0:T(8,128)(2,1)} %get-tuple-element.9), channel_id=1, source_target_pairs={{8,0},{16,8},{24,16},{32,24},{40,32},{48,40},{56,48},{64,56},{72,6... | collective-permute-start | bytes 6152 | tf_op jit(solution)/shard_map/ppermute | solution.py:185
  19.8 0.0 copy-start.5
  19.8 0.0 copy-start.1
  19.8 14.0 %all-to-all-start = ((f32[128,1,256]{2,1,0:T(1,128)}), f32[128,1,256]{2,1,0:T(1,128)S(1)}, u32[]{:S(2)}, u32[]{:S(2)}) async-start(f32[128,1,256]{2,1,0:T(1,128)} %get-tuple-element.8), calls=%async_computation | async-start | bytes 262144 | tf_op jit(solution)/shard_map/all_to_all | solution.py:179
  33.9 0.1 copy.12
  34.0 0.1 reshape.38
  34.0 0.7 constant_dynamic-slice_fusion.refs_1_
  34.8 0.4 gram.1.refs_4_
  35.2 0.0 copy-start.4
  35.9 10.7 %all-to-all-done.refs_3_ = f32[128,1,256]{2,1,0:T(1,128)S(1)} async-done(((f32[128,1,256]{2,1,0:T(1,128)}), f32[128,1,256]{2,1,0:T(1,128)S(1)}, u32[]{:S(2)}, u32[]{:S(2)}) %all-to-all-start) | async-done | bytes 131104 | tf_op jit(solution)/shard_map/all_to_all | solution.py:179
  46.6 1.7 %far.1 = f32[128,1,256]{2,1,0:T(1,128)} custom-call(s32[1,16]{1,0:T(1,128)S(1)} %copy-done.4, s32[1,16]{1,0:T(1,128)S(1)} %constant_dynamic-slice_fusion.refs_1_, s32[1,1]{1,0:T(1,128)S(6)} %copy.17.refs_2_, f32[128,1,256]{2,1,0:T(1,128)S(1)} %all-to-all-done.refs_3_, bf16[1,16,1024]{2,1,0:T(8,128)(2,1)S(1)} %copy-done.3), custom_call_target="tpu_custom_call" | custom-call | tf_op jit(solution)/shard_map/far/pallas_call | solution.py:230
  48.3 5.7 %all-to-all-start.1 = ((f32[128,1,256]{2,1,0:T(1,128)}), f32[128,1,256]{2,1,0:T(1,128)S(1)}, u32[]{:S(2)}, u32[]{:S(2)}) async-start(f32[128,1,256]{2,1,0:T(1,128)} %far.1), calls=%async_computation.1 | async-start | bytes 262144 | tf_op jit(solution)/shard_map/all_to_all | solution.py:179
  53.9 0.0 collective-permute-done
  54.0 0.6 gather_fusion
  54.6 0.0 copy-start.2
  54.6 0.4 fusion
  55.0 11.8 %all-to-all-done.1.refs_2_ = f32[128,1,256]{2,1,0:T(1,128)S(1)} async-done(((f32[128,1,256]{2,1,0:T(1,128)}), f32[128,1,256]{2,1,0:T(1,128)S(1)}, u32[]{:S(2)}, u32[]{:S(2)}) %all-to-all-start.1) | async-done | bytes 131104 | tf_op jit(solution)/shard_map/all_to_all | solution.py:179
  66.8 0.3 image.1
  67.1 10.3 %all_to_all.20.arrived_ref = f32[16,1,384]{2,1,0:T(1,128)S(1)} all-to-all(f32[16,1,384]{2,1,0:T(1,128)S(1)} %get-tuple-element.11), channel_id=1, replica_groups=mesh['z'=8,'x'=8,'core'=2,'grp'=8] {'x','core'}, dimensions={0} | all-to-all | bytes 49152 | tf_op jit(solution)/shard_map/all_to_all | solution.py:179
  77.5 20.3 %all_to_all.21.refs_2_ = f32[64,1,384]{2,1,0:T(1,128)S(1)} all-to-all(f32[64,1,384]{2,1,0:T(1,128)S(1)} %total.1), channel_id=1, replica_groups=mesh['z'=8,'x'=8,'core'=2,'grp'=8] {'z','grp'}, dimensions={0} | all-to-all | bytes 196608 | tf_op jit(solution)/shard_map/all_to_all | solution.py:179
  97.8 0.9 final.1
  (14 shorter events, 0.1 us)
Async XLA Ops:
  0.6 54.0 %copy-start = (bf16[1,8,4,128,128]{4,3,2,1,0:T(8,128)(2,1)S(1)}, bf16[1,8,4,128,128]{4,3,2,1,0:T(8,128)(2,1)}, u32[]{:S(2)}) copy-start(bf16[1,8,4,128,128]{4,3,2,1,0:T(8,128)(2,1)} %param.10) | copy-start | bytes 3145732
  2.4 51.5 %collective-permute-start = (bf16[8,128]{1,0:T(8,128)(2,1)}, bf16[8,128]{1,0:T(8,128)(2,1)S(1)}, u32[]{:S(2)}, u32[]{:S(2)}) collective-permute-start(bf16[8,128]{1,0:T(8,128)(2,1)} %get-tuple-element.9), channel_id=1, source_target_pairs={{0,8},{8,16},{16,24},{24,32},{32,40},{40,48},{48,56},{56,64},{64,7... | collective-permute-start | bytes 6152 | tf_op jit(solution)/shard_map/ppermute | solution.py:185
  7.0 47.0 %collective-permute-start.1 = (bf16[8,128]{1,0:T(8,128)(2,1)}, bf16[8,128]{1,0:T(8,128)(2,1)S(1)}, u32[]{:S(2)}, u32[]{:S(2)}) collective-permute-start(bf16[8,128]{1,0:T(8,128)(2,1)} %get-tuple-element.9), channel_id=1, source_target_pairs={{8,0},{16,8},{24,16},{32,24},{40,32},{48,40},{56,48},{64,56},{72,6... | collective-permute-start | bytes 6152 | tf_op jit(solution)/shard_map/ppermute | solution.py:185
  19.8 14.0 %copy-start.5 = (s32[1,8,4]{1,2,0:T(4,128)S(1)}, s32[1,8,4]{1,2,0:T(4,128)}, u32[]{:S(2)}) copy-start(s32[1,8,4]{1,2,0:T(4,128)} %param.11) | copy-start | bytes 388
  19.8 15.0 %copy-start.1 = (f32[16,1,8,128]{3,2,1,0:T(8,128)S(1)}, f32[16,1,8,128]{3,2,1,0:T(8,128)}, u32[]{:S(2)}) copy-start(f32[16,1,8,128]{3,2,1,0:T(8,128)} %refs_0_.5) | copy-start | bytes 196612
  19.8 26.7 %all-to-all-start = ((f32[128,1,256]{2,1,0:T(1,128)}), f32[128,1,256]{2,1,0:T(1,128)S(1)}, u32[]{:S(2)}, u32[]{:S(2)}) async-start(f32[128,1,256]{2,1,0:T(1,128)} %get-tuple-element.8), calls=%async_computation | async-start | bytes 262144 | tf_op jit(solution)/shard_map/all_to_all | solution.py:179
  34.8 11.8 %copy-start.3 = (bf16[1,16,1024]{2,1,0:T(8,128)(2,1)S(1)}, bf16[1,16,1024]{2,1,0:T(8,128)(2,1)}, u32[]{:S(2)}) copy-start(bf16[1,16,1024]{2,1,0:T(8,128)(2,1)} %refs_4_.1) | copy-start | bytes 98308
  35.2 11.3 %copy-start.4 = (s32[1,16]{1,0:T(1,128)S(1)}, s32[1,16]{1,0:T(1,128)}, u32[]{:S(2)}) copy-start(s32[1,16]{1,0:T(1,128)} %refs_0_.3) | copy-start | bytes 196
  48.3 5.7 %copy-start.6 = (bf16[8,128]{1,0:T(8,128)(2,1)S(1)}, bf16[8,128]{1,0:T(8,128)(2,1)}, u32[]{:S(2)}) copy-start(bf16[8,128]{1,0:T(8,128)(2,1)} %get-tuple-element.9) | copy-start | bytes 6148
  48.3 18.5 %all-to-all-start.1 = ((f32[128,1,256]{2,1,0:T(1,128)}), f32[128,1,256]{2,1,0:T(1,128)S(1)}, u32[]{:S(2)}, u32[]{:S(2)}) async-start(f32[128,1,256]{2,1,0:T(1,128)} %far.1), calls=%async_computation.1 | async-start | bytes 262144 | tf_op jit(solution)/shard_map/all_to_all | solution.py:179
  54.6 12.2 %copy-start.2 = (bf16[1,8,32,128]{3,2,1,0:T(8,128)(2,1)S(1)}, bf16[1,8,32,128]{3,2,1,0:T(8,128)(2,1)}, u32[]{:S(2)}) copy-start(bf16[1,8,32,128]{3,2,1,0:T(8,128)(2,1)} %refs_1_.1) | copy-start | bytes 196612

commit v3 on v2

--- a/solution.py
+++ b/solution.py
@@ -36,9 +36,12 @@
     return lax.axis_index("z") * 16 + lax.axis_index("x") * 2 + lax.axis_index("core")
 
 
-def expand_kernel(basis_ref, source_ref, sent_ref, current_ref):
+def current_kernel(basis_ref, after_ref, current_ref):
+    current_ref[...] = basis_ref[0, 0].astype(jnp.bfloat16)
+
+
+def expand_kernel(basis_ref, source_ref, sent_ref):
     current = basis_ref[0, 0].astype(jnp.bfloat16)
-    current_ref[...] = current
     clusters, panels = current.shape
     ranks = source_ref.shape[2]
     width = clusters * ranks
@@ -46,30 +49,34 @@
     every = dot(current, source, ((1,), (1,)))
     own = iota((clusters, width), 1) // ranks == iota((clusters, width), 0)
     row = jnp.sum(jnp.where(own, every, 0.0), axis=0, keepdims=True)
-    row = row.astype(jnp.bfloat16).astype(jnp.float32)
-    sent_ref[...] = jnp.broadcast_to(row[None], sent_ref.shape)
+    pieces = [row[:, i : i + LANES] for i in range(0, width, LANES)]
+    tile = jnp.concatenate(pieces, axis=0).astype(jnp.bfloat16)
+    sent_ref[...] = jnp.broadcast_to(tile[None], sent_ref.shape)
 
 
 def far_kernel(
     clusters, owners, source_ref, target_ref, count_ref, expansion_ref, coupling_ref, sent_ref
 ):
     slots = coupling_ref.shape[1]
-    width = expansion_ref.shape[2]
+    width = sent_ref.shape[2]
     ranks = width // clusters
     groups = LANES // ranks
     parts = ranks // groups
     me = position()
     lane_cluster = iota((1, width), 1) // ranks
+    tile = expansion_ref.shape[1:]
+    place = iota(tile, 0) * groups + iota(tile, 1) // ranks
     picked, targets = [], []
     for b in range(slots):
         source = source_ref[0, b]
-        row = expansion_ref[source // clusters]
-        picked.append(jnp.where(lane_cluster == source % clusters, row, 0.0))
+        rows = expansion_ref[source // clusters].astype(jnp.float32)
+        rows = jnp.where(place == source % clusters, rows, 0.0)
+        picked.append(jnp.sum(rows, axis=0, keepdims=True))
         target = jnp.where(b < count_ref[0, 0], target_ref[0, b], -1)
         targets.append(jnp.full((1, width), target, jnp.int32))
     picked = jnp.concatenate(picked, axis=0).astype(jnp.bfloat16)
     targets = jnp.concatenate(targets, axis=0)
-    spread = iota((width, LANES), 0) % ranks == iota((width, LANES), 1) % ranks
+    spread = iota((LANES, LANES), 0) % ranks == iota((LANES, LANES), 1) % ranks
     vector = dot(picked, ones_where(spread, jnp.bfloat16))
     coupling = coupling_ref[0].astype(jnp.float32)
     high, low = [], []
@@ -189,6 +196,10 @@
     return jax.ShapeDtypeStruct(shape, jnp.float32)
 
 
+def bf16(*shape):
+    return jax.ShapeDtypeStruct(shape, jnp.bfloat16)
+
+
 def on_device(
     basis,
     near_blocks,
@@ -207,21 +218,25 @@
     width = clusters * ranks
     packed = count * count + LANES
 
-    sent, current = pl.pallas_call(
+    last = pl.BlockSpec((1, 1, clusters, panels), lambda i: (count - 1, 0, 0, 0))
+    sent = pl.pallas_call(
         expand_kernel,
         grid=(1,),
-        in_specs=[
-            pl.BlockSpec((1, 1, clusters, panels), lambda i: (count - 1, 0, 0, 0)),
-            pl.BlockSpec(source_basis.shape, lambda i: (0, 0, 0, 0)),
-        ],
-        out_specs=[
-            pl.BlockSpec((owners, 1, width), lambda i: (0, 0, 0)),
-            pl.BlockSpec((clusters, panels), lambda i: (0, 0)),
-        ],
-        out_shape=[f32(owners, 1, width), jax.ShapeDtypeStruct((clusters, panels), jnp.bfloat16)],
+        in_specs=[last, pl.BlockSpec(source_basis.shape, lambda i: (0, 0, 0, 0))],
+        out_specs=pl.BlockSpec((owners, width // LANES, LANES), lambda i: (0, 0, 0)),
+        out_shape=bf16(owners, width // LANES, LANES),
         name="expand",
     )(basis, source_basis)
     expansions = exchange(sent, CL)
+    current = pl.pallas_call(
+        current_kernel,
+        grid=(1,),
+        in_specs=[last, pl.BlockSpec(memory_space=pl.ANY)],
+        out_specs=pl.BlockSpec((clusters, panels), lambda i: (0, 0)),
+        out_shape=bf16(clusters, panels),
+        cost_estimate=pl.CostEstimate(flops=0, bytes_accessed=1 << 26, transcendentals=0),
+        name="current",
+    )(basis, sent)
     before = neighbour(current, 1)
     after = neighbour(current, -1)
 

time: 99.2 us -> 96.3 us (0.971)
  waiting for transfers between devices: 22.5 us -> 14.2 us
  starting transfers between devices: 37 us -> 41.2 us
  Pallas kernels: 5.21 us -> 6.48 us
    all_to_all x2, starting transfers between devices: 19.7 us -> 35.6 us  [exchange(): return lax.all_to_all(rows, axes, 0, 0)]
    ppermute x2, starting transfers between devices: 17.3 us -> 5.55 us  [neighbour(): return lax.ppermute(value, CL, route)]
    all_to_all x2, waiting for transfers between devices: 22.5 us -> 14.2 us  [exchange(): return lax.all_to_all(rows, axes, 0, 0)]
    pallas_call x1 -> x2, Pallas kernels: 1.8 us -> 3.08 us  [the longest x1 1.75 us: on_device(): pl.pallas_call(expand_kernel, grid=(1,), in_specs=[last, pl.BlockSpec(sou...]
  transfers between devices with their start and end apart: 4 -> 4, of which waited for: 2 -> 2; matrix products, arithmetic and copies ran while one was open for 2% -> 2% of each run, Pallas kernels for 2% -> 4%
where the time goes in v3:
time: 96.3 us; the launch traced here: 95.9 us
  starting transfers between devices  41.2 us (43%)
  blocking collectives  30.7 us (32%)
  waiting for transfers between devices  14.2 us (15%)
  Pallas kernels  6.48 us (7%)
  local copies, waits for them, and re-layouts  1.53 us (2%)
  between operations  1.44 us (1%)
    all_to_all x2, starting transfers between devices, exchange(): return lax.all_to_all(rows, axes, 0, 0)  35.6 us
    all_to_all x2, blocking collectives, exchange(): return lax.all_to_all(rows, axes, 0, 0)  30.7 us
    all_to_all x2, waiting for transfers between devices, exchange(): return lax.all_to_all(rows, axes, 0, 0)  14.2 us
    ppermute x2, starting transfers between devices, neighbour(): return lax.ppermute(value, CL, route)  5.55 us
  transfers between devices with their start and end apart: 4, of which 2 were waited for; matrix products, arithmetic and copies ran while one was open for 2% of the time, Pallas kernels for 4%

profile of v3, /device:TPU:1, one launch (start us, length us, event | category | flops | bytes accessed | tf_op | source)
XLA Modules:
  0.0 95.9 jit_solution(7427984957959619971)
XLA Ops:
  0.6 0.0 copy-start
  0.6 1.8 %expand.1.after_ref = bf16[128,2,128]{2,1,0:T(2,128)(2,1)} custom-call(f32[16,1,8,128]{3,2,1,0:T(8,128)} %refs_0_.5, bf16[1,8,32,128]{3,2,1,0:T(8,128)(2,1)} %source_ref.1), custom_call_target="tpu_custom_call" | custom-call | tf_op jit(solution)/shard_map/expand/pallas_call | solution.py:222
  2.4 24.4 %all-to-all-start = ((bf16[128,2,128]{2,1,0:T(2,128)(2,1)}), bf16[128,2,128]{2,1,0:T(2,128)(2,1)S(1)}, u32[]{:S(2)}, u32[]{:S(2)}) async-start(bf16[128,2,128]{2,1,0:T(2,128)(2,1)} %expand.1.after_ref), calls=%async_computation | async-start | bytes 131072 | tf_op jit(solution)/shard_map/all_to_all | solution.py:186
  26.9 0.0 copy-start.6
  26.9 0.0 copy-start.1
  26.9 1.3 %current.1 = bf16[8,128]{1,0:T(8,128)(2,1)} custom-call(f32[16,1,8,128]{3,2,1,0:T(8,128)} %refs_0_.5, bf16[128,2,128]{2,1,0:T(2,128)(2,1)} %expand.1.after_ref), custom_call_target="tpu_custom_call" | custom-call | bytes 67108864 | tf_op jit(solution)/shard_map/current/pallas_call | solution.py:231
  28.2 2.8 %collective-permute-start.1 = (bf16[8,128]{1,0:T(8,128)(2,1)}, bf16[8,128]{1,0:T(8,128)(2,1)S(1)}, u32[]{:S(2)}, u32[]{:S(2)}) collective-permute-start(bf16[8,128]{1,0:T(8,128)(2,1)} %current.1), channel_id=1, source_target_pairs={{8,0},{16,8},{24,16},{32,24},{40,32},{48,40},{56,48},{64,56},{72,6... | collective-permute-start | bytes 6152 | tf_op jit(solution)/shard_map/ppermute | solution.py:192
  31.0 2.8 %collective-permute-start = (bf16[8,128]{1,0:T(8,128)(2,1)}, bf16[8,128]{1,0:T(8,128)(2,1)S(1)}, u32[]{:S(2)}, u32[]{:S(2)}) collective-permute-start(bf16[8,128]{1,0:T(8,128)(2,1)} %current.1), channel_id=1, source_target_pairs={{0,8},{8,16},{16,24},{24,32},{32,40},{40,48},{48,56},{56,64},{64,7... | collective-permute-start | bytes 6152 | tf_op jit(solution)/shard_map/ppermute | solution.py:192
  33.8 0.1 copy.12
  33.9 0.1 reshape.38
  34.0 0.7 constant_dynamic-slice_fusion.refs_1_
  34.7 0.4 gram.1.refs_4_
  35.2 0.0 copy-start.4
  35.8 2.5 %all-to-all-done.refs_3_ = bf16[128,2,128]{2,1,0:T(2,128)(2,1)S(1)} async-done(((bf16[128,2,128]{2,1,0:T(2,128)(2,1)}), bf16[128,2,128]{2,1,0:T(2,128)(2,1)S(1)}, u32[]{:S(2)}, u32[]{:S(2)}) %all-to-all-start) | async-done | bytes 65568 | tf_op jit(solution)/shard_map/all_to_all | solution.py:186
  38.3 1.7 %far.1 = f32[128,1,256]{2,1,0:T(1,128)} custom-call(s32[1,16]{1,0:T(1,128)S(1)} %copy-done.4, s32[1,16]{1,0:T(1,128)S(1)} %constant_dynamic-slice_fusion.refs_1_, s32[1,1]{1,0:T(1,128)S(6)} %copy.17.refs_2_, bf16[128,2,128]{2,1,0:T(2,128)(2,1)S(1)} %all-to-all-done.refs_3_, bf16[1,16,1024]{2,1,0:T(8,128)(2,1)S(1)} %copy-done.3), custom_call_target="tpu_custom_call" | custom-call | tf_op jit(solution)/shard_map/far/pallas_call | solution.py:245
  40.0 11.2 %all-to-all-start.1 = ((f32[128,1,256]{2,1,0:T(1,128)}), f32[128,1,256]{2,1,0:T(1,128)S(1)}, u32[]{:S(2)}, u32[]{:S(2)}) async-start(f32[128,1,256]{2,1,0:T(1,128)} %far.1), calls=%async_computation.1 | async-start | bytes 262144 | tf_op jit(solution)/shard_map/all_to_all | solution.py:186
  51.2 0.6 gather_fusion
  51.8 0.0 copy-start.2
  51.8 0.4 fusion
  52.2 11.7 %all-to-all-done.1.refs_2_ = f32[128,1,256]{2,1,0:T(1,128)S(1)} async-done(((f32[128,1,256]{2,1,0:T(1,128)}), f32[128,1,256]{2,1,0:T(1,128)S(1)}, u32[]{:S(2)}, u32[]{:S(2)}) %all-to-all-start.1) | async-done | bytes 131104 | tf_op jit(solution)/shard_map/all_to_all | solution.py:186
  63.9 0.3 image.1
  64.2 10.3 %all_to_all.20.arrived_ref = f32[16,1,384]{2,1,0:T(1,128)S(1)} all-to-all(f32[16,1,384]{2,1,0:T(1,128)S(1)} %get-tuple-element.7), channel_id=1, replica_groups=mesh['z'=8,'x'=8,'core'=2,'grp'=8] {'x','core'}, dimensions={0} | all-to-all | bytes 49152 | tf_op jit(solution)/shard_map/all_to_all | solution.py:186
  74.6 20.3 %all_to_all.21.refs_2_ = f32[64,1,384]{2,1,0:T(1,128)S(1)} all-to-all(f32[64,1,384]{2,1,0:T(1,128)S(1)} %total.1), channel_id=1, replica_groups=mesh['z'=8,'x'=8,'core'=2,'grp'=8] {'z','grp'}, dimensions={0} | all-to-all | bytes 196608 | tf_op jit(solution)/shard_map/all_to_all | solution.py:186
  94.9 0.9 final.1
  (15 shorter events, 0.1 us)
Async XLA Ops:
  0.6 51.2 %copy-start = (bf16[1,8,4,128,128]{4,3,2,1,0:T(8,128)(2,1)S(1)}, bf16[1,8,4,128,128]{4,3,2,1,0:T(8,128)(2,1)}, u32[]{:S(2)}) copy-start(bf16[1,8,4,128,128]{4,3,2,1,0:T(8,128)(2,1)} %param.10) | copy-start | bytes 3145732
  2.4 35.9 %all-to-all-start = ((bf16[128,2,128]{2,1,0:T(2,128)(2,1)}), bf16[128,2,128]{2,1,0:T(2,128)(2,1)S(1)}, u32[]{:S(2)}, u32[]{:S(2)}) async-start(bf16[128,2,128]{2,1,0:T(2,128)(2,1)} %expand.1.after_ref), calls=%async_computation | async-start | bytes 131072 | tf_op jit(solution)/shard_map/all_to_all | solution.py:186
  26.9 6.9 %copy-start.6 = (s32[1,8,4]{1,2,0:T(4,128)S(1)}, s32[1,8,4]{1,2,0:T(4,128)}, u32[]{:S(2)}) copy-start(s32[1,8,4]{1,2,0:T(4,128)} %param.11) | copy-start | bytes 388
  26.9 7.8 %copy-start.1 = (f32[16,1,8,128]{3,2,1,0:T(8,128)S(1)}, f32[16,1,8,128]{3,2,1,0:T(8,128)}, u32[]{:S(2)}) copy-start(f32[16,1,8,128]{3,2,1,0:T(8,128)} %refs_0_.5) | copy-start | bytes 196612
  28.2 23.0 %collective-permute-start.1 = (bf16[8,128]{1,0:T(8,128)(2,1)}, bf16[8,128]{1,0:T(8,128)(2,1)S(1)}, u32[]{:S(2)}, u32[]{:S(2)}) collective-permute-start(bf16[8,128]{1,0:T(8,128)(2,1)} %current.1), channel_id=1, source_target_pairs={{8,0},{16,8},{24,16},{32,24},{40,32},{48,40},{56,48},{64,56},{72,6... | collective-permute-start | bytes 6152 | tf_op jit(solution)/shard_map/ppermute | solution.py:192
  31.0 20.2 %collective-permute-start = (bf16[8,128]{1,0:T(8,128)(2,1)}, bf16[8,128]{1,0:T(8,128)(2,1)S(1)}, u32[]{:S(2)}, u32[]{:S(2)}) collective-permute-start(bf16[8,128]{1,0:T(8,128)(2,1)} %current.1), channel_id=1, source_target_pairs={{0,8},{8,16},{16,24},{24,32},{32,40},{40,48},{48,56},{56,64},{64,7... | collective-permute-start | bytes 6152 | tf_op jit(solution)/shard_map/ppermute | solution.py:192
  34.7 3.6 %copy-start.3 = (bf16[1,16,1024]{2,1,0:T(8,128)(2,1)S(1)}, bf16[1,16,1024]{2,1,0:T(8,128)(2,1)}, u32[]{:S(2)}) copy-start(bf16[1,16,1024]{2,1,0:T(8,128)(2,1)} %refs_4_.1) | copy-start | bytes 98308
  35.2 3.1 %copy-start.4 = (s32[1,16]{1,0:T(1,128)S(1)}, s32[1,16]{1,0:T(1,128)}, u32[]{:S(2)}) copy-start(s32[1,16]{1,0:T(1,128)} %refs_0_.3) | copy-start | bytes 196
  40.0 11.2 %copy-start.5 = (bf16[8,128]{1,0:T(8,128)(2,1)S(1)}, bf16[8,128]{1,0:T(8,128)(2,1)}, u32[]{:S(2)}) copy-start(bf16[8,128]{1,0:T(8,128)(2,1)} %current.1) | copy-start | bytes 6148
  40.0 23.9 %all-to-all-start.1 = ((f32[128,1,256]{2,1,0:T(1,128)}), f32[128,1,256]{2,1,0:T(1,128)S(1)}, u32[]{:S(2)}, u32[]{:S(2)}) async-start(f32[128,1,256]{2,1,0:T(1,128)} %far.1), calls=%async_computation.1 | async-start | bytes 262144 | tf_op jit(solution)/shard_map/all_to_all | solution.py:186
  51.8 12.1 %copy-start.2 = (bf16[1,8,32,128]{3,2,1,0:T(8,128)(2,1)S(1)}, bf16[1,8,32,128]{3,2,1,0:T(8,128)(2,1)}, u32[]{:S(2)}) copy-start(bf16[1,8,32,128]{3,2,1,0:T(8,128)(2,1)} %refs_1_.1) | copy-start | bytes 196612

commit v4 on v3

--- a/solution.py
+++ b/solution.py
@@ -11,10 +11,13 @@
 COLUMN = ("z", "grp")
 HIGHEST = lax.Precision.HIGHEST
 LANES = 128
+SHARERS = 8
 FIRST, LAST = -2, 3
 
 SMALL = pltpu.CompilerParams(vmem_limit_bytes=4 * 1024 * 1024)
 VMEM = pl.BlockSpec(memory_space=pltpu.VMEM)
+ANY = pl.BlockSpec(memory_space=pl.ANY)
+HBM = pl.BlockSpec(memory_space=pltpu.HBM)
 SMEM = pl.BlockSpec(memory_space=pltpu.SMEM)
 
 
@@ -36,22 +39,43 @@
     return lax.axis_index("z") * 16 + lax.axis_index("x") * 2 + lax.axis_index("core")
 
 
-def current_kernel(basis_ref, after_ref, current_ref):
-    current_ref[...] = basis_ref[0, 0].astype(jnp.bfloat16)
-
-
-def expand_kernel(basis_ref, source_ref, sent_ref):
-    current = basis_ref[0, 0].astype(jnp.bfloat16)
-    clusters, panels = current.shape
+def relay_kernel(tile_ref, after_ref, relayed_ref):
+    relayed_ref[...] = tile_ref[...]
+
+
+def expand_kernel(
+    basis_ref,
+    source_ref,
+    target_ref,
+    sent_ref,
+    current_ref,
+    window_ref,
+    tile_ref,
+    matrix_ref,
+    semaphores,
+):
+    count, _, clusters, panels = basis_ref.shape
     ranks = source_ref.shape[2]
     width = clusters * ranks
-    source = source_ref[0].reshape(width, panels)
-    every = dot(current, source, ((1,), (1,)))
+    first = pl.multiple_of(position() // SHARERS * LANES, LANES)
+    copies = [
+        pltpu.make_async_copy(basis_ref.at[count - 1, 0], tile_ref, semaphores.at[0]),
+        pltpu.make_async_copy(source_ref.at[0], matrix_ref, semaphores.at[1]),
+        pltpu.make_async_copy(target_ref.at[:, pl.ds(first, LANES)], window_ref, semaphores.at[2]),
+    ]
+    for copy in copies:
+        copy.start()
+    copies[0].wait()
+    current = tile_ref[...].astype(jnp.bfloat16)
+    current_ref[...] = current
+    copies[1].wait()
+    every = dot(current, matrix_ref[...].reshape(width, panels), ((1,), (1,)))
     own = iota((clusters, width), 1) // ranks == iota((clusters, width), 0)
     row = jnp.sum(jnp.where(own, every, 0.0), axis=0, keepdims=True)
     pieces = [row[:, i : i + LANES] for i in range(0, width, LANES)]
     tile = jnp.concatenate(pieces, axis=0).astype(jnp.bfloat16)
     sent_ref[...] = jnp.broadcast_to(tile[None], sent_ref.shape)
+    copies[2].wait()
 
 
 def far_kernel(
@@ -72,7 +96,7 @@
         rows = expansion_ref[source // clusters].astype(jnp.float32)
         rows = jnp.where(place == source % clusters, rows, 0.0)
         picked.append(jnp.sum(rows, axis=0, keepdims=True))
-        target = jnp.where(b < count_ref[0, 0], target_ref[0, b], -1)
+        target = jnp.where(b < count_ref[0, 0], target_ref[0, lax.rem(me, SHARERS) * slots + b], -1)
         targets.append(jnp.full((1, width), target, jnp.int32))
     picked = jnp.concatenate(picked, axis=0).astype(jnp.bfloat16)
     targets = jnp.concatenate(targets, axis=0)
@@ -108,7 +132,7 @@
     send(lax.rem(me + owners // 2, owners))
 
 
-def gram_kernel(basis_ref, gram_ref):
+def gram_kernel(basis_ref, after_ref, gram_ref):
     count, _, clusters, _ = basis_ref.shape
     gram = jnp.zeros((count, count), jnp.float32)
     for c in range(clusters):
@@ -218,30 +242,35 @@
     width = clusters * ranks
     packed = count * count + LANES
 
-    last = pl.BlockSpec((1, 1, clusters, panels), lambda i: (count - 1, 0, 0, 0))
-    sent = pl.pallas_call(
+    sent, current, targets = pl.pallas_call(
         expand_kernel,
-        grid=(1,),
-        in_specs=[last, pl.BlockSpec(source_basis.shape, lambda i: (0, 0, 0, 0))],
-        out_specs=pl.BlockSpec((owners, width // LANES, LANES), lambda i: (0, 0, 0)),
-        out_shape=bf16(owners, width // LANES, LANES),
+        in_specs=[HBM, HBM, HBM],
+        out_specs=[VMEM, VMEM, SMEM],
+        out_shape=[
+            bf16(owners, width // LANES, LANES),
+            bf16(clusters, panels),
+            jax.ShapeDtypeStruct((1, LANES), jnp.int32),
+        ],
+        scratch_shapes=[
+            pltpu.VMEM((clusters, panels), jnp.float32),
+            pltpu.VMEM((clusters, ranks, panels), jnp.bfloat16),
+            pltpu.SemaphoreType.DMA((3,)),
+        ],
         name="expand",
-    )(basis, source_basis)
+    )(basis, source_basis, far_target)
     expansions = exchange(sent, CL)
     current = pl.pallas_call(
-        current_kernel,
-        grid=(1,),
-        in_specs=[last, pl.BlockSpec(memory_space=pl.ANY)],
-        out_specs=pl.BlockSpec((clusters, panels), lambda i: (0, 0)),
+        relay_kernel,
+        in_specs=[VMEM, ANY],
+        out_specs=VMEM,
         out_shape=bf16(clusters, panels),
+        compiler_params=SMALL,
         cost_estimate=pl.CostEstimate(flops=0, bytes_accessed=1 << 26, transcendentals=0),
-        name="current",
-    )(basis, sent)
+        name="relay",
+    )(current, sent)
     before = neighbour(current, 1)
     after = neighbour(current, -1)
 
-    me = lax.axis_index(CL)
-    targets = lax.dynamic_slice_in_dim(far_target, me * slots, slots, axis=1)
     sent = pl.pallas_call(
         lambda *refs: far_kernel(clusters, owners, *refs),
         in_specs=[SMEM, SMEM, SMEM, VMEM, VMEM],
@@ -257,8 +286,13 @@
         "tkij,tkj->ti", near_blocks[0], window[near_list[0]], preferred_element_type=jnp.float32
     )
     gram = pl.pallas_call(
-        gram_kernel, in_specs=[VMEM], out_specs=VMEM, out_shape=f32(1, count * count), compiler_params=SMALL, name="gram"
-    )(basis)
+        gram_kernel,
+        in_specs=[VMEM, ANY],
+        out_specs=VMEM,
+        out_shape=f32(1, count * count),
+        compiler_params=SMALL,
+        name="gram",
+    )(basis, after)
     image, sent = pl.pallas_call(
         lambda *refs: image_kernel(owners, *refs),
         in_specs=[VMEM] * 5,

time: 96.3 us -> 94.6 us (0.982)
  starting transfers between devices: 41.2 us -> 39.4 us
  waiting for transfers between devices: 14.2 us -> 16 us
  Pallas kernels: 6.48 us -> 5.25 us
    all_to_all x2, starting transfers between devices: 35.6 us -> 33.8 us  [exchange(): return lax.all_to_all(rows, axes, 0, 0)]
    all_to_all x2, waiting for transfers between devices: 14.2 us -> 16 us  [exchange(): return lax.all_to_all(rows, axes, 0, 0)]
    pallas_call x3, Pallas kernels: 3.53 us -> 2.26 us  [the longest x1 1.81 us: on_device(): pl.pallas_call(expand_kernel, in_specs=[HBM, HBM, HBM], out_specs=[VMEM,...]
  transfers between devices with their start and end apart: 4 -> 4, of which waited for: 2 -> 2; matrix products, arithmetic and copies ran while one was open for 2% -> 1% of each run, Pallas kernels for 4% -> 2%
where the time goes in v4:
time: 94.6 us; the launch traced here: 94.1 us
  starting transfers between devices  39.4 us (42%)
  blocking collectives  30.7 us (32%)
  waiting for transfers between devices  16 us (17%)
  Pallas kernels  5.25 us (6%)
  between operations  1.49 us (2%)
  local copies, waits for them, and re-layouts  1.02 us (1%)
    all_to_all x2, starting transfers between devices, exchange(): return lax.all_to_all(rows, axes, 0, 0)  33.8 us
    all_to_all x2, blocking collectives, exchange(): return lax.all_to_all(rows, axes, 0, 0)  30.7 us
    all_to_all x2, waiting for transfers between devices, exchange(): return lax.all_to_all(rows, axes, 0, 0)  16 us
    ppermute x2, starting transfers between devices, neighbour(): return lax.ppermute(value, CL, route)  5.56 us
  transfers between devices with their start and end apart: 4, of which 2 were waited for; matrix products, arithmetic and copies ran while one was open for 1% of the time, Pallas kernels for 2%

profile of v4, /device:TPU:1, one launch (start us, length us, event | category | flops | bytes accessed | tf_op | source)
XLA Modules:
  0.0 94.1 jit_solution(14869454005014191466)
XLA Ops:
  0.6 0.0 copy-start
  0.6 1.8 %expand.1 = (bf16[128,2,128]{2,1,0:T(2,128)(2,1)}, bf16[8,128]{1,0:T(8,128)(2,1)}, s32[1,128]{1,0:T(1,128)}) custom-call(f32[16,1,8,128]{3,2,1,0:T(8,128)} %refs_0_.5, bf16[1,8,32,128]{3,2,1,0:T(8,128)(2,1)} %source_ref.1, s32[1,2048]{1,0:T(1,128)} %target_ref.1), custom_call_target="tpu_custom_call" | custom-call | tf_op jit(solution)/shard_map/expand/pallas_call | solution.py:245
  2.5 0.0 copy-start.5
  2.5 24.6 %all-to-all-start = ((bf16[128,2,128]{2,1,0:T(2,128)(2,1)}), bf16[128,2,128]{2,1,0:T(2,128)(2,1)S(1)}, u32[]{:S(2)}, u32[]{:S(2)}) async-start(bf16[128,2,128]{2,1,0:T(2,128)(2,1)} %get-tuple-element.10.after_ref), calls=%async_computation | async-start | bytes 131072 | tf_op jit(solution)/shard_map/all_to_all | solution.py:210
  27.1 0.0 copy-start.8
  27.1 0.0 copy-start.4
  27.1 2.8 %collective-permute-start.1 = (bf16[8,128]{1,0:T(8,128)(2,1)S(1)}, bf16[8,128]{1,0:T(8,128)(2,1)S(1)}, u32[]{:S(2)}, u32[]{:S(2)}) collective-permute-start(bf16[8,128]{1,0:T(8,128)(2,1)S(1)} %relay.1), channel_id=1, source_target_pairs={{8,0},{16,8},{24,16},{32,24},{40,32},{48,40},{56,48},{64,56},{72,6... | collective-permute-start | bytes 6152 | tf_op jit(solution)/shard_map/ppermute | solution.py:216
  29.9 2.8 %collective-permute-start = (bf16[8,128]{1,0:T(8,128)(2,1)S(1)}, bf16[8,128]{1,0:T(8,128)(2,1)S(1)}, u32[]{:S(2)}, u32[]{:S(2)}) collective-permute-start(bf16[8,128]{1,0:T(8,128)(2,1)S(1)} %relay.1), channel_id=1, source_target_pairs={{0,8},{8,16},{16,24},{24,32},{32,40},{40,48},{48,56},{56,64},{64,7... | collective-permute-start | bytes 6152 | tf_op jit(solution)/shard_map/ppermute | solution.py:216
  32.7 0.1 copy.12
  32.8 0.1 reshape.38
  33.6 0.0 copy-start.6
  33.6 4.9 %all-to-all-done.refs_3_ = bf16[128,2,128]{2,1,0:T(2,128)(2,1)S(1)} async-done(((bf16[128,2,128]{2,1,0:T(2,128)(2,1)}), bf16[128,2,128]{2,1,0:T(2,128)(2,1)S(1)}, u32[]{:S(2)}, u32[]{:S(2)}) %all-to-all-start) | async-done | bytes 65568 | tf_op jit(solution)/shard_map/all_to_all | solution.py:210
  38.5 1.7 %far.1 = f32[128,1,256]{2,1,0:T(1,128)} custom-call(s32[1,16]{1,0:T(1,128)S(1)} %copy-done.6, s32[1,128]{1,0:T(1,128)S(1)} %copy-done.7, s32[1,1]{1,0:T(1,128)S(6)} %copy.17.refs_2_, bf16[128,2,128]{2,1,0:T(2,128)(2,1)S(1)} %all-to-all-done.refs_3_, bf16[1,16,1024]{2,1,0:T(8,128)(2,1)S(1)} %copy-done.4), custom_call_target="tpu_custom_call" | custom-call | tf_op jit(solution)/shard_map/far/pallas_call | solution.py:274
  40.3 9.2 %all-to-all-start.1 = ((f32[128,1,256]{2,1,0:T(1,128)}), f32[128,1,256]{2,1,0:T(1,128)S(1)}, u32[]{:S(2)}, u32[]{:S(2)}) async-start(f32[128,1,256]{2,1,0:T(1,128)} %far.1), calls=%async_computation.1 | async-start | bytes 262144 | tf_op jit(solution)/shard_map/all_to_all | solution.py:210
  49.5 0.6 gather_fusion
  50.1 0.2 copy-done.1
  50.3 0.4 gram.1.refs_4_
  50.8 0.0 copy-start.3
  50.8 0.4 fusion
  51.2 11.1 %all-to-all-done.1.refs_2_ = f32[128,1,256]{2,1,0:T(1,128)S(1)} async-done(((f32[128,1,256]{2,1,0:T(1,128)}), f32[128,1,256]{2,1,0:T(1,128)S(1)}, u32[]{:S(2)}, u32[]{:S(2)}) %all-to-all-start.1) | async-done | bytes 131104 | tf_op jit(solution)/shard_map/all_to_all | solution.py:210
  62.2 0.3 image.1
  62.5 10.3 %all_to_all.20.arrived_ref = f32[16,1,384]{2,1,0:T(1,128)S(1)} all-to-all(f32[16,1,384]{2,1,0:T(1,128)S(1)} %get-tuple-element.13), channel_id=1, replica_groups=mesh['z'=8,'x'=8,'core'=2,'grp'=8] {'x','core'}, dimensions={0} | all-to-all | bytes 49152 | tf_op jit(solution)/shard_map/all_to_all | solution.py:210
  72.9 20.3 %all_to_all.21.refs_2_ = f32[64,1,384]{2,1,0:T(1,128)S(1)} all-to-all(f32[64,1,384]{2,1,0:T(1,128)S(1)} %total.1), channel_id=1, replica_groups=mesh['z'=8,'x'=8,'core'=2,'grp'=8] {'z','grp'}, dimensions={0} | all-to-all | bytes 196608 | tf_op jit(solution)/shard_map/all_to_all | solution.py:210
  93.2 0.9 final.1
  (18 shorter events, 0.1 us)
Async XLA Ops:
  0.6 50.1 %copy-start = (bf16[1,8,4,128,128]{4,3,2,1,0:T(8,128)(2,1)S(1)}, bf16[1,8,4,128,128]{4,3,2,1,0:T(8,128)(2,1)}, u32[]{:S(2)}) copy-start(bf16[1,8,4,128,128]{4,3,2,1,0:T(8,128)(2,1)} %param.10) | copy-start | bytes 3145732
  2.5 24.6 %copy-start.2 = (bf16[128,2,128]{2,1,0:T(2,128)(2,1)S(1)}, bf16[128,2,128]{2,1,0:T(2,128)(2,1)}, u32[]{:S(2)}) copy-start(bf16[128,2,128]{2,1,0:T(2,128)(2,1)} %get-tuple-element.10.after_ref) | copy-start | bytes 196612
  2.5 24.6 %copy-start.5 = (bf16[8,128]{1,0:T(8,128)(2,1)S(1)}, bf16[8,128]{1,0:T(8,128)(2,1)}, u32[]{:S(2)}) copy-start(bf16[8,128]{1,0:T(8,128)(2,1)} %get-tuple-element.11.tile_ref) | copy-start | bytes 6148
  2.5 36.0 %all-to-all-start = ((bf16[128,2,128]{2,1,0:T(2,128)(2,1)}), bf16[128,2,128]{2,1,0:T(2,128)(2,1)S(1)}, u32[]{:S(2)}, u32[]{:S(2)}) async-start(bf16[128,2,128]{2,1,0:T(2,128)(2,1)} %get-tuple-element.10.after_ref), calls=%async_computation | async-start | bytes 131072 | tf_op jit(solution)/shard_map/all_to_all | solution.py:210
  27.1 5.6 %copy-start.8 = (s32[1,8,4]{1,2,0:T(4,128)S(1)}, s32[1,8,4]{1,2,0:T(4,128)}, u32[]{:S(2)}) copy-start(s32[1,8,4]{1,2,0:T(4,128)} %param.11) | copy-start | bytes 388
  27.1 11.4 %copy-start.4 = (bf16[1,16,1024]{2,1,0:T(8,128)(2,1)S(1)}, bf16[1,16,1024]{2,1,0:T(8,128)(2,1)}, u32[]{:S(2)}) copy-start(bf16[1,16,1024]{2,1,0:T(8,128)(2,1)} %refs_4_.1) | copy-start | bytes 98308
  27.1 22.3 %collective-permute-start.1 = (bf16[8,128]{1,0:T(8,128)(2,1)S(1)}, bf16[8,128]{1,0:T(8,128)(2,1)S(1)}, u32[]{:S(2)}, u32[]{:S(2)}) collective-permute-start(bf16[8,128]{1,0:T(8,128)(2,1)S(1)} %relay.1), channel_id=1, source_target_pairs={{8,0},{16,8},{24,16},{32,24},{40,32},{48,40},{56,48},{64,56},{72,6... | collective-permute-start | bytes 6152 | tf_op jit(solution)/shard_map/ppermute | solution.py:216
  29.9 19.5 %collective-permute-start = (bf16[8,128]{1,0:T(8,128)(2,1)S(1)}, bf16[8,128]{1,0:T(8,128)(2,1)S(1)}, u32[]{:S(2)}, u32[]{:S(2)}) collective-permute-start(bf16[8,128]{1,0:T(8,128)(2,1)S(1)} %relay.1), channel_id=1, source_target_pairs={{0,8},{8,16},{16,24},{24,32},{32,40},{40,48},{48,56},{56,64},{64,7... | collective-permute-start | bytes 6152 | tf_op jit(solution)/shard_map/ppermute | solution.py:216
  33.6 5.0 %copy-start.6 = (s32[1,16]{1,0:T(1,128)S(1)}, s32[1,16]{1,0:T(1,128)}, u32[]{:S(2)}) copy-start(s32[1,16]{1,0:T(1,128)} %refs_0_.3) | copy-start | bytes 196
  33.6 5.0 %copy-start.7 = (s32[1,128]{1,0:T(1,128)S(1)}, s32[1,128]{1,0:T(1,128)}, u32[]{:S(2)}) copy-start(s32[1,128]{1,0:T(1,128)} %get-tuple-element.9.refs_1_) | copy-start | bytes 1540
  40.3 22.0 %all-to-all-start.1 = ((f32[128,1,256]{2,1,0:T(1,128)}), f32[128,1,256]{2,1,0:T(1,128)S(1)}, u32[]{:S(2)}, u32[]{:S(2)}) async-start(f32[128,1,256]{2,1,0:T(1,128)} %far.1), calls=%async_computation.1 | async-start | bytes 262144 | tf_op jit(solution)/shard_map/all_to_all | solution.py:210
  49.5 0.8 copy-start.1
  50.8 11.4 %copy-start.3 = (bf16[1,8,32,128]{3,2,1,0:T(8,128)(2,1)S(1)}, bf16[1,8,32,128]{3,2,1,0:T(8,128)(2,1)}, u32[]{:S(2)}) copy-start(bf16[1,8,32,128]{3,2,1,0:T(8,128)(2,1)} %refs_1_.1) | copy-start | bytes 196612

commit v5 on v4

--- a/solution.py
+++ b/solution.py
@@ -79,10 +79,20 @@
 
 
 def far_kernel(
-    clusters, owners, source_ref, target_ref, count_ref, expansion_ref, coupling_ref, sent_ref
+    clusters,
+    owners,
+    source_ref,
+    target_ref,
+    count_ref,
+    expansion_ref,
+    coupling_ref,
+    current_ref,
+    sent_ref,
+    held_ref,
 ):
+    held_ref[...] = current_ref[...]
     slots = coupling_ref.shape[1]
-    width = sent_ref.shape[2]
+    width = expansion_ref.shape[1] * LANES
     ranks = width // clusters
     groups = LANES // ranks
     parts = ranks // groups
@@ -120,7 +130,9 @@
 
     def send(owner):
         mine = targets == owner * clusters + lane_cluster
-        sent_ref[owner] = jnp.sum(jnp.where(mine, term, 0.0), axis=0, keepdims=True)
+        row = jnp.sum(jnp.where(mine, term, 0.0), axis=0, keepdims=True)
+        pieces = [row[:, i : i + LANES] for i in range(0, width, LANES)]
+        sent_ref[owner] = jnp.concatenate(pieces, axis=0).astype(jnp.bfloat16)
 
     for step in range(FIRST, LAST + 1):
         owner = me + step
@@ -130,6 +142,10 @@
             send(owner)
 
     send(lax.rem(me + owners // 2, owners))
+
+
+def kept(count):
+    return count * (count // 2 + 1)
 
 
 def gram_kernel(basis_ref, after_ref, gram_ref):
@@ -138,11 +154,11 @@
     for c in range(clusters):
         rows = basis_ref[:, 0, c, :]
         gram = gram + dot(rows, rows, ((1,), (1,)), HIGHEST)
-    width = count * count
-    tile = iota((count, width), 1) % count == iota((count, width), 0)
-    rows = dot(gram, ones_where(tile, jnp.float32), precision=HIGHEST)
-    own = iota((count, width), 1) // count == iota((count, width), 0)
-    gram_ref[...] = jnp.sum(jnp.where(own, rows, 0.0), axis=0, keepdims=True)
+    lane = iota((count, gram_ref.shape[1]), 1)
+    row = iota((count, gram_ref.shape[1]), 0)
+    pick = jnp.logical_and((lane + lane // count) % count == row, lane < kept(count))
+    rows = dot(gram, ones_where(pick, jnp.float32), precision=HIGHEST)
+    gram_ref[...] = jnp.sum(jnp.where(lane % count == row, rows, 0.0), axis=0, keepdims=True)
 
 
 def image_kernel(owners, basis_ref, target_ref, arrived_ref, near_ref, gram_ref, image_ref, sent_ref):
@@ -151,24 +167,28 @@
     ranks = target_ref.shape[2]
     width = clusters * ranks
     me = position()
-    coupled = arrived_ref[lax.rem(me + owners // 2, owners)]
+    coupled = arrived_ref[lax.rem(me + owners // 2, owners)].astype(jnp.float32)
     for step in range(-LAST, -FIRST + 1):
         owner = me + step
         inside = jnp.logical_and(owner >= 0, owner < owners)
-        value = arrived_ref[jnp.clip(owner, 0, owners - 1)]
+        value = arrived_ref[jnp.clip(owner, 0, owners - 1)].astype(jnp.float32)
         coupled = coupled + jnp.where(inside, value, 0.0)
+    coupled = jnp.concatenate([coupled[i : i + 1] for i in range(coupled.shape[0])], axis=1)
     own = iota((clusters, width), 1) // ranks == iota((clusters, width), 0)
     spread = jnp.where(own, coupled, 0.0).astype(jnp.bfloat16)
     far = dot(spread, target_ref[0].reshape(width, panels))
     image = 0.5 * basis_ref[count - 1, 0] + near_ref[...] + far
     image_ref[...] = image
-    rows = [jnp.sum(basis_ref[k, 0] * image, axis=0, keepdims=True) for k in range(count)]
+    first = kept(count) % LANES
+    rows = [jnp.zeros((first, panels), jnp.float32)]
+    rows += [jnp.sum(basis_ref[k, 0] * image, axis=0, keepdims=True) for k in range(count)]
     rows.append(jnp.sum(image * image, axis=0, keepdims=True))
-    rows.append(jnp.zeros((LANES - count - 1, panels), jnp.float32))
+    rows.append(jnp.zeros((LANES - first - count - 1, panels), jnp.float32))
     products = dot(
         jnp.ones((8, panels), jnp.float32), jnp.concatenate(rows, axis=0), ((1,), (1,)), HIGHEST
     )
-    row = jnp.concatenate([gram_ref[...], products[:1]], axis=1)
+    gram = gram_ref[...]
+    row = jnp.concatenate([gram[:, :LANES], gram[:, LANES:] + products[:1]], axis=1)
     sent_ref[...] = jnp.broadcast_to(row[None], sent_ref.shape)
 
 
@@ -180,18 +200,22 @@
 
 def final_kernel(all_panels, basis_ref, image_ref, arrived_ref, next_ref, hessenberg_ref):
     count = basis_ref.shape[0]
-    width = count * count
+    first = kept(count) % LANES
     total = jnp.sum(arrived_ref[...], axis=0)
-    gram = total[:, :width]
-    products = total[:, width:]
+    products = total[:, LANES:]
     lane = iota((1, LANES), 1)
-    projection = jnp.where(lane < count, products / all_panels, 0.0)
-    square = jnp.sum(jnp.where(lane == count, products, 0.0), axis=1, keepdims=True)
-    index = iota((LANES, width), 1)
-    which = iota((LANES, width), 0)
+    inside = jnp.logical_and(lane >= first, lane < first + count)
+    projection = jnp.where(inside, products / all_panels, 0.0)
+    square = jnp.sum(jnp.where(lane == first + count, products, 0.0), axis=1, keepdims=True)
+    index = iota((LANES, total.shape[1]), 1)
+    which = iota((LANES, total.shape[1]), 0) - first
     many = jnp.broadcast_to(projection, (8, LANES))
-    outer = dot(many, ones_where(index // count == which, jnp.float32), precision=HIGHEST)
-    inner = dot(many, ones_where(index % count == which, jnp.float32), precision=HIGHEST)
+    outer = dot(many, ones_where(index % count == which, jnp.float32), precision=HIGHEST)
+    shifted = (index + index // count) % count == which
+    inner = dot(many, ones_where(shifted, jnp.float32), precision=HIGHEST)
+    diagonal = iota(total.shape, 1) // count
+    once = jnp.logical_or(diagonal == 0, diagonal == count // 2)
+    gram = jnp.where(diagonal <= count // 2, total * jnp.where(once, 1.0, 2.0), 0.0)
     squares = (
         square
         - 2.0 * jnp.sum(projection * products, axis=1, keepdims=True)
@@ -200,10 +224,10 @@
     new_norm = jnp.sqrt(squares / all_panels + 1e-06)
     remainder = image_ref[...]
     for k in range(count):
-        remainder = remainder - projection[:, k : k + 1] * basis_ref[k, 0]
+        remainder = remainder - projection[:, first + k : first + k + 1] * basis_ref[k, 0]
     next_ref[0] = remainder / new_norm
-    column = jnp.where(lane == count, new_norm, projection)
-    hessenberg_ref[...] = column[:, : count + 1]
+    column = jnp.where(lane == first + count, new_norm, projection)
+    hessenberg_ref[...] = column[:, first : first + count + 1]
 
 
 def exchange(rows, axes):
@@ -240,7 +264,7 @@
     slots = coupling.shape[1]
     owners = lax.axis_size(CL)
     width = clusters * ranks
-    packed = count * count + LANES
+    packed = 2 * LANES
 
     sent, current, targets = pl.pallas_call(
         expand_kernel,
@@ -271,17 +295,17 @@
     before = neighbour(current, 1)
     after = neighbour(current, -1)
 
-    sent = pl.pallas_call(
+    sent, held = pl.pallas_call(
         lambda *refs: far_kernel(clusters, owners, *refs),
-        in_specs=[SMEM, SMEM, SMEM, VMEM, VMEM],
-        out_specs=VMEM,
-        out_shape=f32(owners, 1, width),
+        in_specs=[SMEM, SMEM, SMEM, VMEM, VMEM, VMEM],
+        out_specs=[VMEM, VMEM],
+        out_shape=[bf16(owners, width // LANES, LANES), bf16(clusters, panels)],
         compiler_params=SMALL,
         name="far",
-    )(far_source, targets, far_count, expansions, coupling)
+    )(far_source, targets, far_count, expansions, coupling, current)
     arrived = exchange(sent, CL)
 
-    window = jnp.concatenate([before, current, after], axis=0)
+    window = jnp.concatenate([before, held, after], axis=0)
     near = jnp.einsum(
         "tkij,tkj->ti", near_blocks[0], window[near_list[0]], preferred_element_type=jnp.float32
     )
@@ -289,10 +313,10 @@
         gram_kernel,
         in_specs=[VMEM, ANY],
         out_specs=VMEM,
-        out_shape=f32(1, count * count),
+        out_shape=f32(1, packed),
         compiler_params=SMALL,
         name="gram",
-    )(basis, after)
+    )(basis, held)
     image, sent = pl.pallas_call(
         lambda *refs: image_kernel(owners, *refs),
         in_specs=[VMEM] * 5,

time: 94.6 us -> 93.3 us (0.986)
  waiting for transfers between devices: 16 us -> 14.9 us
    all_to_all x2, waiting for transfers between devices: 16 us -> 14.9 us  [exchange(): return lax.all_to_all(rows, axes, 0, 0)]
where the time goes in v5:
time: 93.3 us; the launch traced here: 92.8 us
  starting transfers between devices  39.5 us (42%)
  blocking collectives  30.5 us (33%)
  waiting for transfers between devices  14.9 us (16%)
  Pallas kernels  5.31 us (6%)
  between operations  1.49 us (2%)
    all_to_all x2, starting transfers between devices, exchange(): return lax.all_to_all(rows, axes, 0, 0)  33.9 us
    all_to_all x2, blocking collectives, exchange(): return lax.all_to_all(rows, axes, 0, 0)  30.5 us
    all_to_all x2, waiting for transfers between devices, exchange(): return lax.all_to_all(rows, axes, 0, 0)  14.9 us
    ppermute x2, starting transfers between devices, neighbour(): return lax.ppermute(value, CL, route)  5.56 us
  transfers between devices with their start and end apart: 4, of which 2 were waited for; matrix products, arithmetic and copies ran while one was open for 1% of the time, Pallas kernels for 2%

profile of v5, /device:TPU:1, one launch (start us, length us, event | category | flops | bytes accessed | tf_op | source)
XLA Modules:
  0.0 92.8 jit_solution(16898476756839768633)
XLA Ops:
  0.6 0.0 copy-start
  0.6 1.8 %expand.1 = (bf16[128,2,128]{2,1,0:T(2,128)(2,1)}, bf16[8,128]{1,0:T(8,128)(2,1)}, s32[1,128]{1,0:T(1,128)}) custom-call(f32[16,1,8,128]{3,2,1,0:T(8,128)} %refs_0_.5, bf16[1,8,32,128]{3,2,1,0:T(8,128)(2,1)} %source_ref.1, s32[1,2048]{1,0:T(1,128)} %target_ref.1), custom_call_target="tpu_custom_call" | custom-call | tf_op jit(solution)/shard_map/expand/pallas_call | solution.py:269
  2.5 0.0 copy-start.5
  2.5 24.6 %all-to-all-start = ((bf16[128,2,128]{2,1,0:T(2,128)(2,1)}), bf16[128,2,128]{2,1,0:T(2,128)(2,1)S(1)}, u32[]{:S(2)}, u32[]{:S(2)}) async-start(bf16[128,2,128]{2,1,0:T(2,128)(2,1)} %get-tuple-element.12.after_ref), calls=%async_computation | async-start | bytes 131072 | tf_op jit(solution)/shard_map/all_to_all | solution.py:234
  27.1 0.0 copy-start.8
  27.1 0.0 copy-start.4
  27.1 2.8 %collective-permute-start.1 = (bf16[8,128]{1,0:T(8,128)(2,1)S(1)}, bf16[8,128]{1,0:T(8,128)(2,1)S(1)}, u32[]{:S(2)}, u32[]{:S(2)}) collective-permute-start(bf16[8,128]{1,0:T(8,128)(2,1)S(1)} %relay.1.refs_5_), channel_id=1, source_target_pairs={{8,0},{16,8},{24,16},{32,24},{40,32},{48,40},{56,48},{64,56},{72,6... | collective-permute-start | bytes 6152 | tf_op jit(solution)/shard_map/ppermute | solution.py:240
  30.0 2.8 %collective-permute-start = (bf16[8,128]{1,0:T(8,128)(2,1)S(1)}, bf16[8,128]{1,0:T(8,128)(2,1)S(1)}, u32[]{:S(2)}, u32[]{:S(2)}) collective-permute-start(bf16[8,128]{1,0:T(8,128)(2,1)S(1)} %relay.1.refs_5_), channel_id=1, source_target_pairs={{0,8},{8,16},{16,24},{24,32},{32,40},{40,48},{48,56},{56,64},{64,7... | collective-permute-start | bytes 6152 | tf_op jit(solution)/shard_map/ppermute | solution.py:240
  32.7 0.1 copy.12
  32.8 0.1 reshape.38
  33.6 0.0 copy-start.6
  33.6 0.0 copy-start.7
  33.6 4.9 %all-to-all-done.refs_3_ = bf16[128,2,128]{2,1,0:T(2,128)(2,1)S(1)} async-done(((bf16[128,2,128]{2,1,0:T(2,128)(2,1)}), bf16[128,2,128]{2,1,0:T(2,128)(2,1)S(1)}, u32[]{:S(2)}, u32[]{:S(2)}) %all-to-all-start) | async-done | bytes 65568 | tf_op jit(solution)/shard_map/all_to_all | solution.py:234
  38.5 1.7 %far.1 = (bf16[128,2,128]{2,1,0:T(2,128)(2,1)}, bf16[8,128]{1,0:T(8,128)(2,1)S(1)}) custom-call(s32[1,16]{1,0:T(1,128)S(1)} %copy-done.6, s32[1,128]{1,0:T(1,128)S(1)} %copy-done.7, s32[1,1]{1,0:T(1,128)S(6)} %copy.17.refs_2_, bf16[128,2,128]{2,1,0:T(2,128)(2,1)S(1)} %all-to-all-done.refs_3_, bf16[1,16,1024]{2,1,0:T(8,128)(2,1)S(1)} %copy-done.4, ...), custom_call_target="tpu_custom_call" | custom-call | tf_op jit(solution)/shard_map/far/pallas_call | solution.py:298
  40.2 9.3 %all-to-all-start.1 = ((bf16[128,2,128]{2,1,0:T(2,128)(2,1)}), bf16[128,2,128]{2,1,0:T(2,128)(2,1)S(1)}, u32[]{:S(2)}, u32[]{:S(2)}) async-start(bf16[128,2,128]{2,1,0:T(2,128)(2,1)} %get-tuple-element.14), calls=%async_computation.1 | async-start | bytes 131072 | tf_op jit(solution)/shard_map/all_to_all | solution.py:234
  49.6 0.5 gram.1.refs_4_
  50.1 0.6 gather_fusion
  50.7 0.0 copy-start.3
  50.7 0.4 fusion
  51.0 10.0 %all-to-all-done.1.refs_2_ = bf16[128,2,128]{2,1,0:T(2,128)(2,1)S(1)} async-done(((bf16[128,2,128]{2,1,0:T(2,128)(2,1)}), bf16[128,2,128]{2,1,0:T(2,128)(2,1)S(1)}, u32[]{:S(2)}, u32[]{:S(2)}) %all-to-all-start.1) | async-done | bytes 65568 | tf_op jit(solution)/shard_map/all_to_all | solution.py:234
  61.0 0.3 image.1
  61.3 10.3 %all_to_all.20.arrived_ref = f32[16,1,256]{2,1,0:T(1,128)S(1)} all-to-all(f32[16,1,256]{2,1,0:T(1,128)S(1)} %get-tuple-element.17), channel_id=1, replica_groups=mesh['z'=8,'x'=8,'core'=2,'grp'=8] {'x','core'}, dimensions={0} | all-to-all | bytes 32768 | tf_op jit(solution)/shard_map/all_to_all | solution.py:234
  71.7 20.1 %all_to_all.21.refs_2_ = f32[64,1,256]{2,1,0:T(1,128)S(1)} all-to-all(f32[64,1,256]{2,1,0:T(1,128)S(1)} %total.1), channel_id=1, replica_groups=mesh['z'=8,'x'=8,'core'=2,'grp'=8] {'z','grp'}, dimensions={0} | all-to-all | bytes 131072 | tf_op jit(solution)/shard_map/all_to_all | solution.py:234
  91.8 1.0 %final.1 = (f32[1,8,128]{2,1,0:T(8,128)}, f32[1,17]{1,0:T(1,128)}) custom-call(f32[16,1,8,128]{3,2,1,0:T(8,128)S(1)} %copy-done.1, f32[8,128]{1,0:T(8,128)S(1)} %get-tuple-element.16.refs_1_, f32[64,1,256]{2,1,0:T(1,128)S(1)} %all_to_all.21.refs_2_), custom_call_target="tpu_custom_call" | custom-call | tf_op jit(solution)/shard_map/final/pallas_call | solution.py:337
  (18 shorter events, 0.1 us)
Async XLA Ops:
  0.6 50.0 %copy-start = (bf16[1,8,4,128,128]{4,3,2,1,0:T(8,128)(2,1)S(1)}, bf16[1,8,4,128,128]{4,3,2,1,0:T(8,128)(2,1)}, u32[]{:S(2)}) copy-start(bf16[1,8,4,128,128]{4,3,2,1,0:T(8,128)(2,1)} %param.10) | copy-start | bytes 3145732
  2.5 24.6 %copy-start.2 = (bf16[128,2,128]{2,1,0:T(2,128)(2,1)S(1)}, bf16[128,2,128]{2,1,0:T(2,128)(2,1)}, u32[]{:S(2)}) copy-start(bf16[128,2,128]{2,1,0:T(2,128)(2,1)} %get-tuple-element.12.after_ref) | copy-start | bytes 196612
  2.5 24.6 %copy-start.5 = (bf16[8,128]{1,0:T(8,128)(2,1)S(1)}, bf16[8,128]{1,0:T(8,128)(2,1)}, u32[]{:S(2)}) copy-start(bf16[8,128]{1,0:T(8,128)(2,1)} %get-tuple-element.13.tile_ref) | copy-start | bytes 6148
  2.5 36.0 %all-to-all-start = ((bf16[128,2,128]{2,1,0:T(2,128)(2,1)}), bf16[128,2,128]{2,1,0:T(2,128)(2,1)S(1)}, u32[]{:S(2)}, u32[]{:S(2)}) async-start(bf16[128,2,128]{2,1,0:T(2,128)(2,1)} %get-tuple-element.12.after_ref), calls=%async_computation | async-start | bytes 131072 | tf_op jit(solution)/shard_map/all_to_all | solution.py:234
  27.1 5.6 %copy-start.8 = (s32[1,8,4]{1,2,0:T(4,128)S(1)}, s32[1,8,4]{1,2,0:T(4,128)}, u32[]{:S(2)}) copy-start(s32[1,8,4]{1,2,0:T(4,128)} %param.11) | copy-start | bytes 388
  27.1 11.4 %copy-start.4 = (bf16[1,16,1024]{2,1,0:T(8,128)(2,1)S(1)}, bf16[1,16,1024]{2,1,0:T(8,128)(2,1)}, u32[]{:S(2)}) copy-start(bf16[1,16,1024]{2,1,0:T(8,128)(2,1)} %refs_4_.1) | copy-start | bytes 98308
  27.1 22.9 %collective-permute-start.1 = (bf16[8,128]{1,0:T(8,128)(2,1)S(1)}, bf16[8,128]{1,0:T(8,128)(2,1)S(1)}, u32[]{:S(2)}, u32[]{:S(2)}) collective-permute-start(bf16[8,128]{1,0:T(8,128)(2,1)S(1)} %relay.1.refs_5_), channel_id=1, source_target_pairs={{8,0},{16,8},{24,16},{32,24},{40,32},{48,40},{56,48},{64,56},{72,6... | collective-permute-start | bytes 6152 | tf_op jit(solution)/shard_map/ppermute | solution.py:240
  30.0 20.1 %collective-permute-start = (bf16[8,128]{1,0:T(8,128)(2,1)S(1)}, bf16[8,128]{1,0:T(8,128)(2,1)S(1)}, u32[]{:S(2)}, u32[]{:S(2)}) collective-permute-start(bf16[8,128]{1,0:T(8,128)(2,1)S(1)} %relay.1.refs_5_), channel_id=1, source_target_pairs={{0,8},{8,16},{16,24},{24,32},{32,40},{40,48},{48,56},{56,64},{64,7... | collective-permute-start | bytes 6152 | tf_op jit(solution)/shard_map/ppermute | solution.py:240
  33.6 5.0 %copy-start.6 = (s32[1,16]{1,0:T(1,128)S(1)}, s32[1,16]{1,0:T(1,128)}, u32[]{:S(2)}) copy-start(s32[1,16]{1,0:T(1,128)} %refs_0_.3) | copy-start | bytes 196
  33.6 4.9 %copy-start.7 = (s32[1,128]{1,0:T(1,128)S(1)}, s32[1,128]{1,0:T(1,128)}, u32[]{:S(2)}) copy-start(s32[1,128]{1,0:T(1,128)} %get-tuple-element.11.refs_1_) | copy-start | bytes 1540
  40.2 9.3 %copy-start.1 = (f32[16,1,8,128]{3,2,1,0:T(8,128)S(1)}, f32[16,1,8,128]{3,2,1,0:T(8,128)}, u32[]{:S(2)}) copy-start(f32[16,1,8,128]{3,2,1,0:T(8,128)} %refs_0_.5) | copy-start | bytes 196612
  40.2 20.8 %all-to-all-start.1 = ((bf16[128,2,128]{2,1,0:T(2,128)(2,1)}), bf16[128,2,128]{2,1,0:T(2,128)(2,1)S(1)}, u32[]{:S(2)}, u32[]{:S(2)}) async-start(bf16[128,2,128]{2,1,0:T(2,128)(2,1)} %get-tuple-element.14), calls=%async_computation.1 | async-start | bytes 131072 | tf_op jit(solution)/shard_map/all_to_all | solution.py:234
  50.7 10.3 %copy-start.3 = (bf16[1,8,32,128]{3,2,1,0:T(8,128)(2,1)S(1)}, bf16[1,8,32,128]{3,2,1,0:T(8,128)(2,1)}, u32[]{:S(2)}) copy-start(bf16[1,8,32,128]{3,2,1,0:T(8,128)(2,1)} %refs_1_.1) | copy-start | bytes 196612

commit v6 on v5

--- a/solution.py
+++ b/solution.py
@@ -39,8 +39,9 @@
     return lax.axis_index("z") * 16 + lax.axis_index("x") * 2 + lax.axis_index("core")
 
 
-def relay_kernel(tile_ref, after_ref, relayed_ref):
-    relayed_ref[...] = tile_ref[...]
+def relay_kernel(tile_ref, targets_ref, sources_ref, after_ref, *relayed):
+    for given, passed in zip((tile_ref, targets_ref, sources_ref), relayed):
+        passed[...] = given[...]
 
 
 def expand_kernel(
@@ -234,9 +235,11 @@
     return lax.all_to_all(rows, axes, 0, 0)
 
 
-def neighbour(value, step):
+def swapped(value, first):
     count = lax.axis_size(CL)
-    route = [(i, i + step) for i in range(count) if 0 <= i + step < count]
+    route = []
+    for i in range(first, count - 1, 2):
+        route += [(i, i + 1), (i + 1, i)]
     return lax.ppermute(value, CL, route)
 
 
@@ -283,17 +286,25 @@
         name="expand",
     )(basis, source_basis, far_target)
     expansions = exchange(sent, CL)
-    current = pl.pallas_call(
+    current, targets, sources = pl.pallas_call(
         relay_kernel,
-        in_specs=[VMEM, ANY],
-        out_specs=VMEM,
-        out_shape=bf16(clusters, panels),
+        in_specs=[VMEM, VMEM, VMEM, ANY],
+        out_specs=[VMEM] * 3,
+        out_shape=[
+            bf16(clusters, panels),
+            jax.ShapeDtypeStruct(targets.shape, jnp.int32),
+            jax.ShapeDtypeStruct(far_source.shape, jnp.int32),
+        ],
         compiler_params=SMALL,
         cost_estimate=pl.CostEstimate(flops=0, bytes_accessed=1 << 26, transcendentals=0),
         name="relay",
-    )(current, sent)
-    before = neighbour(current, 1)
-    after = neighbour(current, -1)
+    )(current, targets, far_source, sent)
+    other = swapped(current, 1)
+    pair = swapped(current, 0)
+    even = lax.axis_index("core") == 0
+    near_ids = near_list[0]
+    mirrored = (2 - near_ids // clusters) * clusters + near_ids % clusters
+    near_ids = jnp.where(even, mirrored, near_ids)
 
     sent, held = pl.pallas_call(
         lambda *refs: far_kernel(clusters, owners, *refs),
@@ -302,12 +313,12 @@
         out_shape=[bf16(owners, width // LANES, LANES), bf16(clusters, panels)],
         compiler_params=SMALL,
         name="far",
-    )(far_source, targets, far_count, expansions, coupling, current)
+    )(sources, targets, far_count, expansions, coupling, current)
     arrived = exchange(sent, CL)
 
-    window = jnp.concatenate([before, held, after], axis=0)
+    window = jnp.concatenate([pair, held, other], axis=0)
     near = jnp.einsum(
-        "tkij,tkj->ti", near_blocks[0], window[near_list[0]], preferred_element_type=jnp.float32
+        "tkij,tkj->ti", near_blocks[0], window[near_ids], preferred_element_type=jnp.float32
     )
     gram = pl.pallas_call(
         gram_kernel,

time: 93.3 us -> 92.5 us (level)
  no operation moved by 1% of the time
where the time goes in v6:
time: 92.5 us; the launch traced here: 92 us
  starting transfers between devices  38.6 us (42%)
  blocking collectives  30.5 us (33%)
  waiting for transfers between devices  14.3 us (15%)
  Pallas kernels  5.29 us (6%)
  between operations  1.47 us (2%)
  local copies, waits for them, and re-layouts  1.45 us (2%)
    all_to_all x2, starting transfers between devices, exchange(): return lax.all_to_all(rows, axes, 0, 0)  33.1 us
    all_to_all x2, blocking collectives, exchange(): return lax.all_to_all(rows, axes, 0, 0)  30.5 us
    all_to_all x2, waiting for transfers between devices, exchange(): return lax.all_to_all(rows, axes, 0, 0)  14.3 us
    ppermute x2, starting transfers between devices, swapped(): return lax.ppermute(value, CL, route)  5.46 us
  transfers between devices with their start and end apart: 4, of which 2 were waited for; matrix products, arithmetic and copies ran while one was open for 1% of the time, Pallas kernels for 2%

profile of v6, /device:TPU:1, one launch (start us, length us, event | category | flops | bytes accessed | tf_op | source)
XLA Modules:
  0.0 92.0 jit_solution(9534470475199857780)
XLA Ops:
  0.6 0.0 copy-start
  0.6 1.8 %expand.1 = (bf16[128,2,128]{2,1,0:T(2,128)(2,1)}, bf16[8,128]{1,0:T(8,128)(2,1)}, s32[1,128]{1,0:T(1,128)}) custom-call(f32[16,1,8,128]{3,2,1,0:T(8,128)} %refs_0_.3, bf16[1,8,32,128]{3,2,1,0:T(8,128)(2,1)} %source_ref.1, s32[1,2048]{1,0:T(1,128)} %target_ref.1), custom_call_target="tpu_custom_call" | custom-call | tf_op jit(solution)/shard_map/expand/pallas_call | solution.py:272
  2.5 24.6 %all-to-all-start = ((bf16[128,2,128]{2,1,0:T(2,128)(2,1)}), bf16[128,2,128]{2,1,0:T(2,128)(2,1)S(1)}, u32[]{:S(2)}, u32[]{:S(2)}) async-start(bf16[128,2,128]{2,1,0:T(2,128)(2,1)} %get-tuple-element.16.after_ref), calls=%async_computation | async-start | bytes 131072 | tf_op jit(solution)/shard_map/all_to_all | solution.py:235
  27.1 0.0 copy-start.5
  27.1 0.0 copy-start.6
  27.1 0.0 copy-start.7
  27.1 0.6 copy-done.5
  27.8 0.0 copy-start.4
  27.8 3.5 %collective-permute-start.1 = (bf16[8,128]{1,0:T(8,128)(2,1)S(1)}, bf16[8,128]{1,0:T(8,128)(2,1)S(1)}, u32[]{:S(2)}, u32[]{:S(2)}) collective-permute-start(bf16[8,128]{1,0:T(8,128)(2,1)S(1)} %get-tuple-element.19.refs_5_), channel_id=1, source_target_pairs={{8,16},{16,8},{24,32},{32,24},{40,48},{48,40},{56,64},{64,56},{72,... | collective-permute-start | bytes 6152 | tf_op jit(solution)/shard_map/ppermute | solution.py:243
  31.3 1.9 %collective-permute-start = (bf16[8,128]{1,0:T(8,128)(2,1)S(1)}, bf16[8,128]{1,0:T(8,128)(2,1)S(1)}, u32[]{:S(2)}, u32[]{:S(2)}) collective-permute-start(bf16[8,128]{1,0:T(8,128)(2,1)S(1)} %get-tuple-element.19.refs_5_), channel_id=1, source_target_pairs={{0,8},{8,0},{16,24},{24,16},{32,40},{40,32},{48,56},{56,48},{64,72... | collective-permute-start | bytes 6152 | tf_op jit(solution)/shard_map/ppermute | solution.py:243
  33.3 0.1 copy.12
  33.4 0.1 reshape.132
  34.1 4.4 %all-to-all-done.refs_3_ = bf16[128,2,128]{2,1,0:T(2,128)(2,1)S(1)} async-done(((bf16[128,2,128]{2,1,0:T(2,128)(2,1)}), bf16[128,2,128]{2,1,0:T(2,128)(2,1)S(1)}, u32[]{:S(2)}, u32[]{:S(2)}) %all-to-all-start) | async-done | bytes 65568 | tf_op jit(solution)/shard_map/all_to_all | solution.py:235
  38.5 1.7 %far.1 = (bf16[128,2,128]{2,1,0:T(2,128)(2,1)}, bf16[8,128]{1,0:T(8,128)(2,1)S(1)}) custom-call(s32[1,16]{1,0:T(1,128)S(1)} %get-tuple-element.17.refs_0_, s32[1,128]{1,0:T(1,128)S(1)} %get-tuple-element.18.refs_1_, s32[1,1]{1,0:T(1,128)S(6)} %copy.17.refs_2_, bf16[128,2,128]{2,1,0:T(2,128)(2,1)S(1)} %all-to-all-done.refs_3_, ...), custom_call_target="tpu_custom_call" | custom-call | tf_op jit(solution)/shard_map/far/pallas_call | solution.py:309
  40.2 8.6 %all-to-all-start.1 = ((bf16[128,2,128]{2,1,0:T(2,128)(2,1)}), bf16[128,2,128]{2,1,0:T(2,128)(2,1)S(1)}, u32[]{:S(2)}, u32[]{:S(2)}) async-start(bf16[128,2,128]{2,1,0:T(2,128)(2,1)} %get-tuple-element.20), calls=%async_computation.1 | async-start | bytes 131072 | tf_op jit(solution)/shard_map/all_to_all | solution.py:235
  48.8 0.5 gram.1.refs_4_
  49.3 0.6 gather_fusion
  49.9 0.0 copy-start.3
  49.9 0.4 fusion
  50.2 10.0 %all-to-all-done.1.refs_2_ = bf16[128,2,128]{2,1,0:T(2,128)(2,1)S(1)} async-done(((bf16[128,2,128]{2,1,0:T(2,128)(2,1)}), bf16[128,2,128]{2,1,0:T(2,128)(2,1)S(1)}, u32[]{:S(2)}, u32[]{:S(2)}) %all-to-all-start.1) | async-done | bytes 65568 | tf_op jit(solution)/shard_map/all_to_all | solution.py:235
  60.2 0.3 image.1
  60.5 10.4 %all_to_all.20.arrived_ref = f32[16,1,256]{2,1,0:T(1,128)S(1)} all-to-all(f32[16,1,256]{2,1,0:T(1,128)S(1)} %get-tuple-element.23), channel_id=1, replica_groups=mesh['z'=8,'x'=8,'core'=2,'grp'=8] {'x','core'}, dimensions={0} | all-to-all | bytes 32768 | tf_op jit(solution)/shard_map/all_to_all | solution.py:235
  71.0 20.1 %all_to_all.21.refs_2_ = f32[64,1,256]{2,1,0:T(1,128)S(1)} all-to-all(f32[64,1,256]{2,1,0:T(1,128)S(1)} %total.1), channel_id=1, replica_groups=mesh['z'=8,'x'=8,'core'=2,'grp'=8] {'z','grp'}, dimensions={0} | all-to-all | bytes 131072 | tf_op jit(solution)/shard_map/all_to_all | solution.py:235
  91.0 1.0 %final.1 = (f32[1,8,128]{2,1,0:T(8,128)}, f32[1,17]{1,0:T(1,128)}) custom-call(f32[16,1,8,128]{3,2,1,0:T(8,128)S(1)} %copy-done.1, f32[8,128]{1,0:T(8,128)S(1)} %get-tuple-element.22.refs_1_, f32[64,1,256]{2,1,0:T(1,128)S(1)} %all_to_all.21.refs_2_), custom_call_target="tpu_custom_call" | custom-call | tf_op jit(solution)/shard_map/final/pallas_call | solution.py:348
  (18 shorter events, 0.1 us)
Async XLA Ops:
  0.6 49.2 %copy-start = (bf16[1,8,4,128,128]{4,3,2,1,0:T(8,128)(2,1)S(1)}, bf16[1,8,4,128,128]{4,3,2,1,0:T(8,128)(2,1)}, u32[]{:S(2)}) copy-start(bf16[1,8,4,128,128]{4,3,2,1,0:T(8,128)(2,1)} %param.10) | copy-start | bytes 3145732
  2.5 24.6 %copy-start.2 = (bf16[128,2,128]{2,1,0:T(2,128)(2,1)S(1)}, bf16[128,2,128]{2,1,0:T(2,128)(2,1)}, u32[]{:S(2)}) copy-start(bf16[128,2,128]{2,1,0:T(2,128)(2,1)} %get-tuple-element.16.after_ref) | copy-start | bytes 196612
  2.5 36.0 %all-to-all-start = ((bf16[128,2,128]{2,1,0:T(2,128)(2,1)}), bf16[128,2,128]{2,1,0:T(2,128)(2,1)S(1)}, u32[]{:S(2)}, u32[]{:S(2)}) async-start(bf16[128,2,128]{2,1,0:T(2,128)(2,1)} %get-tuple-element.16.after_ref), calls=%async_computation | async-start | bytes 131072 | tf_op jit(solution)/shard_map/all_to_all | solution.py:235
  27.1 0.7 copy-start.5
  27.1 0.7 copy-start.6
  27.1 0.7 copy-start.7
  27.8 5.5 %copy-start.8 = (s32[1,8,4]{1,2,0:T(4,128)S(1)}, s32[1,8,4]{1,2,0:T(4,128)}, u32[]{:S(2)}) copy-start(s32[1,8,4]{1,2,0:T(4,128)} %param.11) | copy-start | bytes 388
  27.8 10.7 %copy-start.4 = (bf16[1,16,1024]{2,1,0:T(8,128)(2,1)S(1)}, bf16[1,16,1024]{2,1,0:T(8,128)(2,1)}, u32[]{:S(2)}) copy-start(bf16[1,16,1024]{2,1,0:T(8,128)(2,1)} %refs_4_.1) | copy-start | bytes 98308
  27.8 21.5 %collective-permute-start.1 = (bf16[8,128]{1,0:T(8,128)(2,1)S(1)}, bf16[8,128]{1,0:T(8,128)(2,1)S(1)}, u32[]{:S(2)}, u32[]{:S(2)}) collective-permute-start(bf16[8,128]{1,0:T(8,128)(2,1)S(1)} %get-tuple-element.19.refs_5_), channel_id=1, source_target_pairs={{8,16},{16,8},{24,32},{32,24},{40,48},{48,40},{56,64},{64,56},{72,... | collective-permute-start | bytes 6152 | tf_op jit(solution)/shard_map/ppermute | solution.py:243
  31.3 17.9 %collective-permute-start = (bf16[8,128]{1,0:T(8,128)(2,1)S(1)}, bf16[8,128]{1,0:T(8,128)(2,1)S(1)}, u32[]{:S(2)}, u32[]{:S(2)}) collective-permute-start(bf16[8,128]{1,0:T(8,128)(2,1)S(1)} %get-tuple-element.19.refs_5_), channel_id=1, source_target_pairs={{0,8},{8,0},{16,24},{24,16},{32,40},{40,32},{48,56},{56,48},{64,72... | collective-permute-start | bytes 6152 | tf_op jit(solution)/shard_map/ppermute | solution.py:243
  40.2 8.6 %copy-start.1 = (f32[16,1,8,128]{3,2,1,0:T(8,128)S(1)}, f32[16,1,8,128]{3,2,1,0:T(8,128)}, u32[]{:S(2)}) copy-start(f32[16,1,8,128]{3,2,1,0:T(8,128)} %refs_0_.3) | copy-start | bytes 196612
  40.2 20.0 %all-to-all-start.1 = ((bf16[128,2,128]{2,1,0:T(2,128)(2,1)}), bf16[128,2,128]{2,1,0:T(2,128)(2,1)S(1)}, u32[]{:S(2)}, u32[]{:S(2)}) async-start(bf16[128,2,128]{2,1,0:T(2,128)(2,1)} %get-tuple-element.20), calls=%async_computation.1 | async-start | bytes 131072 | tf_op jit(solution)/shard_map/all_to_all | solution.py:235
  49.9 10.3 %copy-start.3 = (bf16[1,8,32,128]{3,2,1,0:T(8,128)(2,1)S(1)}, bf16[1,8,32,128]{3,2,1,0:T(8,128)(2,1)}, u32[]{:S(2)}) copy-start(bf16[1,8,32,128]{3,2,1,0:T(8,128)(2,1)} %refs_1_.1) | copy-start | bytes 196612

commit v7 on v6

--- a/solution.py
+++ b/solution.py
@@ -39,18 +39,19 @@
     return lax.axis_index("z") * 16 + lax.axis_index("x") * 2 + lax.axis_index("core")
 
 
-def relay_kernel(tile_ref, targets_ref, sources_ref, after_ref, *relayed):
-    for given, passed in zip((tile_ref, targets_ref, sources_ref), relayed):
-        passed[...] = given[...]
+def relay_kernel(tile_ref, after_ref, relayed_ref):
+    relayed_ref[...] = tile_ref[...]
 
 
 def expand_kernel(
     basis_ref,
     source_ref,
     target_ref,
+    slot_ref,
     sent_ref,
     current_ref,
     window_ref,
+    sources_ref,
     tile_ref,
     matrix_ref,
     semaphores,
@@ -63,6 +64,7 @@
         pltpu.make_async_copy(basis_ref.at[count - 1, 0], tile_ref, semaphores.at[0]),
         pltpu.make_async_copy(source_ref.at[0], matrix_ref, semaphores.at[1]),
         pltpu.make_async_copy(target_ref.at[:, pl.ds(first, LANES)], window_ref, semaphores.at[2]),
+        pltpu.make_async_copy(slot_ref, sources_ref, semaphores.at[3]),
     ]
     for copy in copies:
         copy.start()
@@ -77,6 +79,7 @@
     tile = jnp.concatenate(pieces, axis=0).astype(jnp.bfloat16)
     sent_ref[...] = jnp.broadcast_to(tile[None], sent_ref.shape)
     copies[2].wait()
+    copies[3].wait()
 
 
 def far_kernel(
@@ -269,36 +272,33 @@
     width = clusters * ranks
     packed = 2 * LANES
 
-    sent, current, targets = pl.pallas_call(
+    sent, current, targets, sources = pl.pallas_call(
         expand_kernel,
-        in_specs=[HBM, HBM, HBM],
-        out_specs=[VMEM, VMEM, SMEM],
+        in_specs=[HBM] * 4,
+        out_specs=[VMEM] * 4,
         out_shape=[
             bf16(owners, width // LANES, LANES),
-            bf16(clusters, panels),
-            jax.ShapeDtypeStruct((1, LANES), jnp.int32),
+            pltpu.VMEM((clusters, panels), jnp.bfloat16),
+            pltpu.VMEM((1, LANES), jnp.int32),
+            pltpu.VMEM(far_source.shape, jnp.int32),
         ],
         scratch_shapes=[
             pltpu.VMEM((clusters, panels), jnp.float32),
             pltpu.VMEM((clusters, ranks, panels), jnp.bfloat16),
-            pltpu.SemaphoreType.DMA((3,)),
+            pltpu.SemaphoreType.DMA((4,)),
         ],
         name="expand",
-    )(basis, source_basis, far_target)
+    )(basis, source_basis, far_target, far_source)
     expansions = exchange(sent, CL)
-    current, targets, sources = pl.pallas_call(
+    current = pl.pallas_call(
         relay_kernel,
-        in_specs=[VMEM, VMEM, VMEM, ANY],
-        out_specs=[VMEM] * 3,
-        out_shape=[
-            bf16(clusters, panels),
-            jax.ShapeDtypeStruct(targets.shape, jnp.int32),
-            jax.ShapeDtypeStruct(far_source.shape, jnp.int32),
-        ],
+        in_specs=[VMEM, ANY],
+        out_specs=VMEM,
+        out_shape=bf16(clusters, panels),
         compiler_params=SMALL,
         cost_estimate=pl.CostEstimate(flops=0, bytes_accessed=1 << 26, transcendentals=0),
         name="relay",
-    )(current, targets, far_source, sent)
+    )(current, sent)
     other = swapped(current, 1)
     pair = swapped(current, 0)
     even = lax.axis_index("core") == 0

time: 92.5 us -> 91.8 us (level)
  no operation moved by 1% of the time
where the time goes in v7:
time: 91.8 us; the launch traced here: 91.3 us
  starting transfers between devices  37.9 us (41%)
  blocking collectives  30.5 us (33%)
  waiting for transfers between devices  15 us (16%)
  Pallas kernels  5.26 us (6%)
  between operations  1.46 us (2%)
    all_to_all x2, starting transfers between devices, exchange(): return lax.all_to_all(rows, axes, 0, 0)  32.5 us
    all_to_all x2, blocking collectives, exchange(): return lax.all_to_all(rows, axes, 0, 0)  30.5 us
    all_to_all x2, waiting for transfers between devices, exchange(): return lax.all_to_all(rows, axes, 0, 0)  15 us
    ppermute x2, starting transfers between devices, swapped(): return lax.ppermute(value, CL, route)  5.46 us
  transfers between devices with their start and end apart: 4, of which 2 were waited for; matrix products, arithmetic and copies ran while one was open for 1% of the time, Pallas kernels for 2%

profile of v7, /device:TPU:1, one launch (start us, length us, event | category | flops | bytes accessed | tf_op | source)
XLA Modules:
  0.0 91.3 jit_solution(16953903898347664258)
XLA Ops:
  0.6 0.0 copy-start
  0.6 1.8 %expand.1 = (bf16[128,2,128]{2,1,0:T(2,128)(2,1)}, bf16[8,128]{1,0:T(8,128)(2,1)S(1)}, s32[1,128]{1,0:T(1,128)S(1)}, s32[1,16]{1,0:T(1,128)S(1)}) custom-call(f32[16,1,8,128]{3,2,1,0:T(8,128)} %refs_0_.3, bf16[1,8,32,128]{3,2,1,0:T(8,128)(2,1)} %source_ref.1, s32[1,2048]{1,0:T(1,128)} %target_ref.1, s32[1,16]{1,0:T(1,128)} %slot_ref.1), custom_call_target="tpu_custom_call" | custom-call | tf_op jit(solution)/shard_map/expand/pallas_call | solution.py:275
  2.4 0.0 copy-start.2
  2.5 24.6 %all-to-all-start = ((bf16[128,2,128]{2,1,0:T(2,128)(2,1)}), bf16[128,2,128]{2,1,0:T(2,128)(2,1)S(1)}, u32[]{:S(2)}, u32[]{:S(2)}) async-start(bf16[128,2,128]{2,1,0:T(2,128)(2,1)} %get-tuple-element.14.after_ref), calls=%async_computation | async-start | bytes 131072 | tf_op jit(solution)/shard_map/all_to_all | solution.py:238
  27.1 0.0 copy-start.5
  27.1 0.0 copy-start.4
  27.1 3.5 %collective-permute-start.1 = (bf16[8,128]{1,0:T(8,128)(2,1)S(1)}, bf16[8,128]{1,0:T(8,128)(2,1)S(1)}, u32[]{:S(2)}, u32[]{:S(2)}) collective-permute-start(bf16[8,128]{1,0:T(8,128)(2,1)S(1)} %relay.1.refs_5_), channel_id=1, source_target_pairs={{8,16},{16,8},{24,32},{32,24},{40,48},{48,40},{56,64},{64,56},{72,... | collective-permute-start | bytes 6152 | tf_op jit(solution)/shard_map/ppermute | solution.py:246
  30.6 1.9 %collective-permute-start = (bf16[8,128]{1,0:T(8,128)(2,1)S(1)}, bf16[8,128]{1,0:T(8,128)(2,1)S(1)}, u32[]{:S(2)}, u32[]{:S(2)}) collective-permute-start(bf16[8,128]{1,0:T(8,128)(2,1)S(1)} %relay.1.refs_5_), channel_id=1, source_target_pairs={{0,8},{8,0},{16,24},{24,16},{32,40},{40,32},{48,56},{56,48},{64,72... | collective-permute-start | bytes 6152 | tf_op jit(solution)/shard_map/ppermute | solution.py:246
  32.6 0.1 copy.12
  32.7 0.1 reshape.132
  33.4 5.0 %all-to-all-done.refs_3_ = bf16[128,2,128]{2,1,0:T(2,128)(2,1)S(1)} async-done(((bf16[128,2,128]{2,1,0:T(2,128)(2,1)}), bf16[128,2,128]{2,1,0:T(2,128)(2,1)S(1)}, u32[]{:S(2)}, u32[]{:S(2)}) %all-to-all-start) | async-done | bytes 65568 | tf_op jit(solution)/shard_map/all_to_all | solution.py:238
  38.5 1.7 %far.1 = (bf16[128,2,128]{2,1,0:T(2,128)(2,1)}, bf16[8,128]{1,0:T(8,128)(2,1)S(1)}) custom-call(s32[1,16]{1,0:T(1,128)S(1)} %get-tuple-element.12.refs_0_, s32[1,128]{1,0:T(1,128)S(1)} %get-tuple-element.13.refs_1_, s32[1,1]{1,0:T(1,128)S(6)} %copy.17.refs_2_, bf16[128,2,128]{2,1,0:T(2,128)(2,1)S(1)} %all-to-all-done.refs_3_, ...), custom_call_target="tpu_custom_call" | custom-call | tf_op jit(solution)/shard_map/far/pallas_call | solution.py:309
  40.2 7.9 %all-to-all-start.1 = ((bf16[128,2,128]{2,1,0:T(2,128)(2,1)}), bf16[128,2,128]{2,1,0:T(2,128)(2,1)S(1)}, u32[]{:S(2)}, u32[]{:S(2)}) async-start(bf16[128,2,128]{2,1,0:T(2,128)(2,1)} %get-tuple-element.16), calls=%async_computation.1 | async-start | bytes 131072 | tf_op jit(solution)/shard_map/all_to_all | solution.py:238
  48.1 0.5 gram.1.refs_4_
  48.5 0.0 collective-permute-done.1
  48.5 0.0 collective-permute-done
  48.6 0.6 gather_fusion
  49.2 0.0 copy-start.3
  49.2 0.4 fusion
  49.5 10.0 %all-to-all-done.1.refs_2_ = bf16[128,2,128]{2,1,0:T(2,128)(2,1)S(1)} async-done(((bf16[128,2,128]{2,1,0:T(2,128)(2,1)}), bf16[128,2,128]{2,1,0:T(2,128)(2,1)S(1)}, u32[]{:S(2)}, u32[]{:S(2)}) %all-to-all-start.1) | async-done | bytes 65568 | tf_op jit(solution)/shard_map/all_to_all | solution.py:238
  59.5 0.3 image.1
  59.8 10.4 %all_to_all.20.arrived_ref = f32[16,1,256]{2,1,0:T(1,128)S(1)} all-to-all(f32[16,1,256]{2,1,0:T(1,128)S(1)} %get-tuple-element.19), channel_id=1, replica_groups=mesh['z'=8,'x'=8,'core'=2,'grp'=8] {'x','core'}, dimensions={0} | all-to-all | bytes 32768 | tf_op jit(solution)/shard_map/all_to_all | solution.py:238
  70.3 20.1 %all_to_all.21.refs_2_ = f32[64,1,256]{2,1,0:T(1,128)S(1)} all-to-all(f32[64,1,256]{2,1,0:T(1,128)S(1)} %total.1), channel_id=1, replica_groups=mesh['z'=8,'x'=8,'core'=2,'grp'=8] {'z','grp'}, dimensions={0} | all-to-all | bytes 131072 | tf_op jit(solution)/shard_map/all_to_all | solution.py:238
  90.3 1.0 %final.1 = (f32[1,8,128]{2,1,0:T(8,128)}, f32[1,17]{1,0:T(1,128)}) custom-call(f32[16,1,8,128]{3,2,1,0:T(8,128)S(1)} %copy-done.1, f32[8,128]{1,0:T(8,128)S(1)} %get-tuple-element.18.refs_1_, f32[64,1,256]{2,1,0:T(1,128)S(1)} %all_to_all.21.refs_2_), custom_call_target="tpu_custom_call" | custom-call | tf_op jit(solution)/shard_map/final/pallas_call | solution.py:348
  (12 shorter events, 0.1 us)
Async XLA Ops:
  0.6 48.5 %copy-start = (bf16[1,8,4,128,128]{4,3,2,1,0:T(8,128)(2,1)S(1)}, bf16[1,8,4,128,128]{4,3,2,1,0:T(8,128)(2,1)}, u32[]{:S(2)}) copy-start(bf16[1,8,4,128,128]{4,3,2,1,0:T(8,128)(2,1)} %param.10) | copy-start | bytes 3145732
  2.4 24.6 %copy-start.2 = (bf16[128,2,128]{2,1,0:T(2,128)(2,1)S(1)}, bf16[128,2,128]{2,1,0:T(2,128)(2,1)}, u32[]{:S(2)}) copy-start(bf16[128,2,128]{2,1,0:T(2,128)(2,1)} %get-tuple-element.14.after_ref) | copy-start | bytes 196612
  2.5 36.0 %all-to-all-start = ((bf16[128,2,128]{2,1,0:T(2,128)(2,1)}), bf16[128,2,128]{2,1,0:T(2,128)(2,1)S(1)}, u32[]{:S(2)}, u32[]{:S(2)}) async-start(bf16[128,2,128]{2,1,0:T(2,128)(2,1)} %get-tuple-element.14.after_ref), calls=%async_computation | async-start | bytes 131072 | tf_op jit(solution)/shard_map/all_to_all | solution.py:238
  27.1 5.5 %copy-start.5 = (s32[1,8,4]{1,2,0:T(4,128)S(1)}, s32[1,8,4]{1,2,0:T(4,128)}, u32[]{:S(2)}) copy-start(s32[1,8,4]{1,2,0:T(4,128)} %param.11) | copy-start | bytes 388
  27.1 11.4 %copy-start.4 = (bf16[1,16,1024]{2,1,0:T(8,128)(2,1)S(1)}, bf16[1,16,1024]{2,1,0:T(8,128)(2,1)}, u32[]{:S(2)}) copy-start(bf16[1,16,1024]{2,1,0:T(8,128)(2,1)} %refs_4_.1) | copy-start | bytes 98308
  27.1 21.4 %collective-permute-start.1 = (bf16[8,128]{1,0:T(8,128)(2,1)S(1)}, bf16[8,128]{1,0:T(8,128)(2,1)S(1)}, u32[]{:S(2)}, u32[]{:S(2)}) collective-permute-start(bf16[8,128]{1,0:T(8,128)(2,1)S(1)} %relay.1.refs_5_), channel_id=1, source_target_pairs={{8,16},{16,8},{24,32},{32,24},{40,48},{48,40},{56,64},{64,56},{72,... | collective-permute-start | bytes 6152 | tf_op jit(solution)/shard_map/ppermute | solution.py:246
  30.6 17.9 %collective-permute-start = (bf16[8,128]{1,0:T(8,128)(2,1)S(1)}, bf16[8,128]{1,0:T(8,128)(2,1)S(1)}, u32[]{:S(2)}, u32[]{:S(2)}) collective-permute-start(bf16[8,128]{1,0:T(8,128)(2,1)S(1)} %relay.1.refs_5_), channel_id=1, source_target_pairs={{0,8},{8,0},{16,24},{24,16},{32,40},{40,32},{48,56},{56,48},{64,72... | collective-permute-start | bytes 6152 | tf_op jit(solution)/shard_map/ppermute | solution.py:246
  40.2 7.9 %copy-start.1 = (f32[16,1,8,128]{3,2,1,0:T(8,128)S(1)}, f32[16,1,8,128]{3,2,1,0:T(8,128)}, u32[]{:S(2)}) copy-start(f32[16,1,8,128]{3,2,1,0:T(8,128)} %refs_0_.3) | copy-start | bytes 196612
  40.2 19.3 %all-to-all-start.1 = ((bf16[128,2,128]{2,1,0:T(2,128)(2,1)}), bf16[128,2,128]{2,1,0:T(2,128)(2,1)S(1)}, u32[]{:S(2)}, u32[]{:S(2)}) async-start(bf16[128,2,128]{2,1,0:T(2,128)(2,1)} %get-tuple-element.16), calls=%async_computation.1 | async-start | bytes 131072 | tf_op jit(solution)/shard_map/all_to_all | solution.py:238
  49.2 10.3 %copy-start.3 = (bf16[1,8,32,128]{3,2,1,0:T(8,128)(2,1)S(1)}, bf16[1,8,32,128]{3,2,1,0:T(8,128)(2,1)}, u32[]{:S(2)}) copy-start(bf16[1,8,32,128]{3,2,1,0:T(8,128)(2,1)} %refs_1_.1) | copy-start | bytes 196612

commit v8 on v7

--- a/solution.py
+++ b/solution.py
@@ -290,7 +290,7 @@
         name="expand",
     )(basis, source_basis, far_target, far_source)
     expansions = exchange(sent, CL)
-    current = pl.pallas_call(
+    relay = pl.pallas_call(
         relay_kernel,
         in_specs=[VMEM, ANY],
         out_specs=VMEM,
@@ -298,9 +298,10 @@
         compiler_params=SMALL,
         cost_estimate=pl.CostEstimate(flops=0, bytes_accessed=1 << 26, transcendentals=0),
         name="relay",
-    )(current, sent)
-    other = swapped(current, 1)
+    )
+    current = relay(current, sent)
     pair = swapped(current, 0)
+    other = swapped(relay(current, sent), 1)
     even = lax.axis_index("core") == 0
     near_ids = near_list[0]
     mirrored = (2 - near_ids // clusters) * clusters + near_ids % clusters
@@ -327,7 +328,7 @@
         out_shape=f32(1, packed),
         compiler_params=SMALL,
         name="gram",
-    )(basis, held)
+    )(basis, near)
     image, sent = pl.pallas_call(
         lambda *refs: image_kernel(owners, *refs),
         in_specs=[VMEM] * 5,

time: 91.8 us -> 91.7 us (level)
  no operation moved by 1% of the time
where the time goes in v8:
time: 91.7 us; the launch traced here: 91.2 us
  starting transfers between devices  37.9 us (41%)
  blocking collectives  30.5 us (33%)
  waiting for transfers between devices  14.4 us (16%)
  Pallas kernels  5.26 us (6%)
  between operations  1.46 us (2%)
  local copies, waits for them, and re-layouts  1.25 us (1%)
    all_to_all x2, starting transfers between devices, exchange(): return lax.all_to_all(rows, axes, 0, 0)  32.3 us
    all_to_all x2, blocking collectives, exchange(): return lax.all_to_all(rows, axes, 0, 0)  30.5 us
    all_to_all x2, waiting for transfers between devices, exchange(): return lax.all_to_all(rows, axes, 0, 0)  14.4 us
    ppermute x2, starting transfers between devices, swapped(): return lax.ppermute(value, CL, route)  5.6 us
  transfers between devices with their start and end apart: 4, of which 2 were waited for; matrix products, arithmetic and copies ran while one was open for 1% of the time, Pallas kernels for 2%

profile of v8, /device:TPU:1, one launch (start us, length us, event | category | flops | bytes accessed | tf_op | source)
XLA Modules:
  0.0 91.2 jit_solution(13989222276203635478)
XLA Ops:
  0.6 0.0 copy-start
  0.6 1.8 %expand.1 = (bf16[128,2,128]{2,1,0:T(2,128)(2,1)}, bf16[8,128]{1,0:T(8,128)(2,1)S(1)}, s32[1,128]{1,0:T(1,128)S(1)}, s32[1,16]{1,0:T(1,128)S(1)}) custom-call(f32[16,1,8,128]{3,2,1,0:T(8,128)} %refs_0_.3, bf16[1,8,32,128]{3,2,1,0:T(8,128)(2,1)} %source_ref.1, s32[1,2048]{1,0:T(1,128)} %target_ref.1, s32[1,16]{1,0:T(1,128)} %slot_ref.1), custom_call_target="tpu_custom_call" | custom-call | tf_op jit(solution)/shard_map/expand/pallas_call | solution.py:275
  2.5 24.6 %all-to-all-start = ((bf16[128,2,128]{2,1,0:T(2,128)(2,1)}), bf16[128,2,128]{2,1,0:T(2,128)(2,1)S(1)}, u32[]{:S(2)}, u32[]{:S(2)}) async-start(bf16[128,2,128]{2,1,0:T(2,128)(2,1)} %get-tuple-element.14.after_ref), calls=%async_computation | async-start | bytes 131072 | tf_op jit(solution)/shard_map/all_to_all | solution.py:238
  27.1 2.8 %collective-permute-start = (bf16[8,128]{1,0:T(8,128)(2,1)S(1)}, bf16[8,128]{1,0:T(8,128)(2,1)S(1)}, u32[]{:S(2)}, u32[]{:S(2)}) collective-permute-start(bf16[8,128]{1,0:T(8,128)(2,1)S(1)} %relay.2.refs_5_.tile_ref), channel_id=1, source_target_pairs={{0,8},{8,0},{16,24},{24,16},{32,40},{40,32},{48,56},{56,48},{64,72... | collective-permute-start | bytes 6152 | tf_op jit(solution)/shard_map/ppermute | solution.py:246
  29.9 0.0 copy-start.5
  29.9 0.0 copy-start.4
  29.9 2.8 %collective-permute-start.1 = (bf16[8,128]{1,0:T(8,128)(2,1)S(1)}, bf16[8,128]{1,0:T(8,128)(2,1)S(1)}, u32[]{:S(2)}, u32[]{:S(2)}) collective-permute-start(bf16[8,128]{1,0:T(8,128)(2,1)S(1)} %relay.3), channel_id=1, source_target_pairs={{8,16},{16,8},{24,32},{32,24},{40,48},{48,40},{56,64},{64,56},{72,... | collective-permute-start | bytes 6152 | tf_op jit(solution)/shard_map/ppermute | solution.py:246
  32.8 0.1 copy.12
  32.8 0.1 reshape.132
  33.6 4.9 %all-to-all-done.refs_3_ = bf16[128,2,128]{2,1,0:T(2,128)(2,1)S(1)} async-done(((bf16[128,2,128]{2,1,0:T(2,128)(2,1)}), bf16[128,2,128]{2,1,0:T(2,128)(2,1)S(1)}, u32[]{:S(2)}, u32[]{:S(2)}) %all-to-all-start) | async-done | bytes 65568 | tf_op jit(solution)/shard_map/all_to_all | solution.py:238
  38.5 1.7 %far.1 = (bf16[128,2,128]{2,1,0:T(2,128)(2,1)}, bf16[8,128]{1,0:T(8,128)(2,1)S(1)}) custom-call(s32[1,16]{1,0:T(1,128)S(1)} %get-tuple-element.12.refs_0_, s32[1,128]{1,0:T(1,128)S(1)} %get-tuple-element.13.refs_1_, s32[1,1]{1,0:T(1,128)S(6)} %copy.17.refs_2_, bf16[128,2,128]{2,1,0:T(2,128)(2,1)S(1)} %all-to-all-done.refs_3_, ...), custom_call_target="tpu_custom_call" | custom-call | tf_op jit(solution)/shard_map/far/pallas_call | solution.py:310
  40.2 7.8 %all-to-all-start.1 = ((bf16[128,2,128]{2,1,0:T(2,128)(2,1)}), bf16[128,2,128]{2,1,0:T(2,128)(2,1)S(1)}, u32[]{:S(2)}, u32[]{:S(2)}) async-start(bf16[128,2,128]{2,1,0:T(2,128)(2,1)} %get-tuple-element.16), calls=%async_computation.1 | async-start | bytes 131072 | tf_op jit(solution)/shard_map/all_to_all | solution.py:238
  47.9 0.0 collective-permute-done.1
  47.9 0.0 collective-permute-done
  48.0 0.6 gather_fusion
  48.6 0.0 copy-start.1
  48.6 0.4 fusion
  48.9 0.5 copy-done.1
  49.4 0.4 gram.1.refs_4_
  49.9 9.5 %all-to-all-done.1.refs_2_ = bf16[128,2,128]{2,1,0:T(2,128)(2,1)S(1)} async-done(((bf16[128,2,128]{2,1,0:T(2,128)(2,1)}), bf16[128,2,128]{2,1,0:T(2,128)(2,1)S(1)}, u32[]{:S(2)}, u32[]{:S(2)}) %all-to-all-start.1) | async-done | bytes 65568 | tf_op jit(solution)/shard_map/all_to_all | solution.py:238
  59.4 0.3 image.1
  59.7 10.4 %all_to_all.20.arrived_ref = f32[16,1,256]{2,1,0:T(1,128)S(1)} all-to-all(f32[16,1,256]{2,1,0:T(1,128)S(1)} %get-tuple-element.19), channel_id=1, replica_groups=mesh['z'=8,'x'=8,'core'=2,'grp'=8] {'x','core'}, dimensions={0} | all-to-all | bytes 32768 | tf_op jit(solution)/shard_map/all_to_all | solution.py:238
  70.1 20.1 %all_to_all.21.refs_2_ = f32[64,1,256]{2,1,0:T(1,128)S(1)} all-to-all(f32[64,1,256]{2,1,0:T(1,128)S(1)} %total.1), channel_id=1, replica_groups=mesh['z'=8,'x'=8,'core'=2,'grp'=8] {'z','grp'}, dimensions={0} | all-to-all | bytes 131072 | tf_op jit(solution)/shard_map/all_to_all | solution.py:238
  90.2 1.0 %final.1 = (f32[1,8,128]{2,1,0:T(8,128)}, f32[1,17]{1,0:T(1,128)}) custom-call(f32[16,1,8,128]{3,2,1,0:T(8,128)S(1)} %copy-done.1, f32[8,128]{1,0:T(8,128)S(1)} %get-tuple-element.18.refs_1_, f32[64,1,256]{2,1,0:T(1,128)S(1)} %all_to_all.21.refs_2_), custom_call_target="tpu_custom_call" | custom-call | tf_op jit(solution)/shard_map/final/pallas_call | solution.py:349
  (13 shorter events, 0.1 us)
Async XLA Ops:
  0.6 47.9 %copy-start = (bf16[1,8,4,128,128]{4,3,2,1,0:T(8,128)(2,1)S(1)}, bf16[1,8,4,128,128]{4,3,2,1,0:T(8,128)(2,1)}, u32[]{:S(2)}) copy-start(bf16[1,8,4,128,128]{4,3,2,1,0:T(8,128)(2,1)} %param.10) | copy-start | bytes 3145732
  2.4 24.6 %copy-start.2 = (bf16[128,2,128]{2,1,0:T(2,128)(2,1)S(1)}, bf16[128,2,128]{2,1,0:T(2,128)(2,1)}, u32[]{:S(2)}) copy-start(bf16[128,2,128]{2,1,0:T(2,128)(2,1)} %get-tuple-element.14.after_ref) | copy-start | bytes 196612
  2.5 36.0 %all-to-all-start = ((bf16[128,2,128]{2,1,0:T(2,128)(2,1)}), bf16[128,2,128]{2,1,0:T(2,128)(2,1)S(1)}, u32[]{:S(2)}, u32[]{:S(2)}) async-start(bf16[128,2,128]{2,1,0:T(2,128)(2,1)} %get-tuple-element.14.after_ref), calls=%async_computation | async-start | bytes 131072 | tf_op jit(solution)/shard_map/all_to_all | solution.py:238
  27.1 20.9 %collective-permute-start = (bf16[8,128]{1,0:T(8,128)(2,1)S(1)}, bf16[8,128]{1,0:T(8,128)(2,1)S(1)}, u32[]{:S(2)}, u32[]{:S(2)}) collective-permute-start(bf16[8,128]{1,0:T(8,128)(2,1)S(1)} %relay.2.refs_5_.tile_ref), channel_id=1, source_target_pairs={{0,8},{8,0},{16,24},{24,16},{32,40},{40,32},{48,56},{56,48},{64,72... | collective-permute-start | bytes 6152 | tf_op jit(solution)/shard_map/ppermute | solution.py:246
  29.9 2.8 %copy-start.5 = (s32[1,8,4]{1,2,0:T(4,128)S(1)}, s32[1,8,4]{1,2,0:T(4,128)}, u32[]{:S(2)}) copy-start(s32[1,8,4]{1,2,0:T(4,128)} %param.11) | copy-start | bytes 388
  29.9 8.6 %copy-start.4 = (bf16[1,16,1024]{2,1,0:T(8,128)(2,1)S(1)}, bf16[1,16,1024]{2,1,0:T(8,128)(2,1)}, u32[]{:S(2)}) copy-start(bf16[1,16,1024]{2,1,0:T(8,128)(2,1)} %refs_4_.1) | copy-start | bytes 98308
  29.9 18.0 %collective-permute-start.1 = (bf16[8,128]{1,0:T(8,128)(2,1)S(1)}, bf16[8,128]{1,0:T(8,128)(2,1)S(1)}, u32[]{:S(2)}, u32[]{:S(2)}) collective-permute-start(bf16[8,128]{1,0:T(8,128)(2,1)S(1)} %relay.3), channel_id=1, source_target_pairs={{8,16},{16,8},{24,32},{32,24},{40,48},{48,40},{56,64},{64,56},{72,... | collective-permute-start | bytes 6152 | tf_op jit(solution)/shard_map/ppermute | solution.py:246
  40.2 19.2 %all-to-all-start.1 = ((bf16[128,2,128]{2,1,0:T(2,128)(2,1)}), bf16[128,2,128]{2,1,0:T(2,128)(2,1)S(1)}, u32[]{:S(2)}, u32[]{:S(2)}) async-start(bf16[128,2,128]{2,1,0:T(2,128)(2,1)} %get-tuple-element.16), calls=%async_computation.1 | async-start | bytes 131072 | tf_op jit(solution)/shard_map/all_to_all | solution.py:238
  48.6 0.8 copy-start.1
  48.9 10.4 %copy-start.3 = (bf16[1,8,32,128]{3,2,1,0:T(8,128)(2,1)S(1)}, bf16[1,8,32,128]{3,2,1,0:T(8,128)(2,1)}, u32[]{:S(2)}) copy-start(bf16[1,8,32,128]{3,2,1,0:T(8,128)(2,1)} %refs_1_.1) | copy-start | bytes 196612

commit v9 on v7

--- a/solution.py
+++ b/solution.py
@@ -152,6 +152,27 @@
     return count * (count // 2 + 1)
 
 
+def near_kernel(list_ref, pair_ref, held_ref, other_ref, blocks_ref, near_ref, window_ref):
+    _, clusters, blocks, panels, _ = blocks_ref.shape
+    for i, tile in enumerate((pair_ref, held_ref, other_ref)):
+        window_ref[i * clusters : (i + 1) * clusters] = tile[...].astype(jnp.float32)
+    even = lax.axis_index("core") == 0
+    for t in range(clusters):
+        rows = []
+        for k in range(blocks):
+            index = list_ref[k, t]
+            mirrored = (2 - index // clusters) * clusters + index % clusters
+            rows.append(window_ref[pl.ds(jnp.where(even, mirrored, index), 1), :])
+        rows.append(jnp.zeros((8 - blocks, panels), jnp.float32))
+        vectors = jnp.concatenate(rows, axis=0).astype(jnp.bfloat16)
+        matrix = blocks_ref[0, t].reshape(blocks * panels, panels)
+        every = dot(vectors, matrix, ((1,), (1,)))
+        total = every[0:1, :panels]
+        for k in range(1, blocks):
+            total = total + every[k : k + 1, k * panels : (k + 1) * panels]
+        near_ref[t : t + 1, :] = total
+
+
 def gram_kernel(basis_ref, after_ref, gram_ref):
     count, _, clusters, _ = basis_ref.shape
     gram = jnp.zeros((count, count), jnp.float32)
@@ -301,10 +322,6 @@
     )(current, sent)
     other = swapped(current, 1)
     pair = swapped(current, 0)
-    even = lax.axis_index("core") == 0
-    near_ids = near_list[0]
-    mirrored = (2 - near_ids // clusters) * clusters + near_ids % clusters
-    near_ids = jnp.where(even, mirrored, near_ids)
 
     sent, held = pl.pallas_call(
         lambda *refs: far_kernel(clusters, owners, *refs),
@@ -316,10 +333,15 @@
     )(sources, targets, far_count, expansions, coupling, current)
     arrived = exchange(sent, CL)
 
-    window = jnp.concatenate([pair, held, other], axis=0)
-    near = jnp.einsum(
-        "tkij,tkj->ti", near_blocks[0], window[near_ids], preferred_element_type=jnp.float32
-    )
+    near = pl.pallas_call(
+        near_kernel,
+        in_specs=[SMEM, VMEM, VMEM, VMEM, VMEM],
+        out_specs=VMEM,
+        out_shape=f32(clusters, panels),
+        scratch_shapes=[pltpu.VMEM((3 * clusters, panels), jnp.float32)],
+        compiler_params=SMALL,
+        name="near",
+    )(near_list[0].T, pair, held, other, near_blocks)
     gram = pl.pallas_call(
         gram_kernel,
         in_specs=[VMEM, ANY],
@@ -327,7 +349,7 @@
         out_shape=f32(1, packed),
         compiler_params=SMALL,
         name="gram",
-    )(basis, held)
+    )(basis, near)
     image, sent = pl.pallas_call(
         lambda *refs: image_kernel(owners, *refs),
         in_specs=[VMEM] * 5,

time: 91.8 us -> 95.7 us (1.042)
  blocking collectives: 30.5 us -> 36.5 us
  starting transfers between devices: 37.9 us -> 35.8 us
    all_to_all x2, blocking collectives: 30.5 us -> 36.5 us  [exchange(): return lax.all_to_all(rows, axes, 0, 0)]
    all_to_all x2, starting transfers between devices: 32.5 us -> 30.3 us  [exchange(): return lax.all_to_all(rows, axes, 0, 0)]
    all_to_all x2, waiting for transfers between devices: 15 us -> 13 us  [exchange(): return lax.all_to_all(rows, axes, 0, 0)]
    unnamed x12, local copies, waits for them, and re-layouts: 0.04 us -> 1.25 us
    ppermute x2, waiting for transfers between devices: 0.01 us -> 1.11 us  [swapped(): return lax.ppermute(value, CL, route)]
  transfers between devices with their start and end apart: 4 -> 4, of which waited for: 2 -> 3; matrix products, arithmetic and copies ran while one was open for 1% -> 0% of each run, Pallas kernels for 2% -> 1%
where the time goes in v9:
time: 95.7 us; the launch traced here: 95.2 us
  blocking collectives  36.5 us (38%)
  starting transfers between devices  35.8 us (37%)
  waiting for transfers between devices  14.1 us (15%)
  Pallas kernels  6.12 us (6%)
  between operations  1.41 us (1%)
  local copies, waits for them, and re-layouts  1.25 us (1%)
    all_to_all x2, blocking collectives, exchange(): return lax.all_to_all(rows, axes, 0, 0)  36.5 us
    all_to_all x2, starting transfers between devices, exchange(): return lax.all_to_all(rows, axes, 0, 0)  30.3 us
    all_to_all x2, waiting for transfers between devices, exchange(): return lax.all_to_all(rows, axes, 0, 0)  13 us
    ppermute x2, starting transfers between devices, swapped(): return lax.ppermute(value, CL, route)  5.47 us
  transfers between devices with their start and end apart: 4, of which 3 were waited for; matrix products, arithmetic and copies ran while one was open for 0% of the time, Pallas kernels for 1%

profile of v9, /device:TPU:1, one launch (start us, length us, event | category | flops | bytes accessed | tf_op | source)
XLA Modules:
  0.0 95.2 jit_solution(2071800055143511121)
XLA Ops:
  0.6 1.7 %expand.1 = (bf16[128,2,128]{2,1,0:T(2,128)(2,1)}, bf16[8,128]{1,0:T(8,128)(2,1)S(1)}, s32[1,128]{1,0:T(1,128)S(1)}, s32[1,16]{1,0:T(1,128)S(1)}) custom-call(f32[16,1,8,128]{3,2,1,0:T(8,128)} %refs_0_.3, bf16[1,8,32,128]{3,2,1,0:T(8,128)(2,1)} %source_ref.1, s32[1,2048]{1,0:T(1,128)} %target_ref.1, s32[1,16]{1,0:T(1,128)} %slot_ref.1), custom_call_target="tpu_custom_call" | custom-call | tf_op jit(solution)/shard_map/expand/pallas_call | solution.py:296
  2.3 0.0 copy-start.2
  2.4 24.6 %all-to-all-start = ((bf16[128,2,128]{2,1,0:T(2,128)(2,1)}), bf16[128,2,128]{2,1,0:T(2,128)(2,1)S(1)}, u32[]{:S(2)}, u32[]{:S(2)}) async-start(bf16[128,2,128]{2,1,0:T(2,128)(2,1)} %get-tuple-element.14.after_ref), calls=%async_computation | async-start | bytes 131072 | tf_op jit(solution)/shard_map/all_to_all | solution.py:259
  27.6 0.0 copy-done.2
  27.6 0.0 copy-start.4
  27.6 10.8 %all-to-all-done.refs_3_ = bf16[128,2,128]{2,1,0:T(2,128)(2,1)S(1)} async-done(((bf16[128,2,128]{2,1,0:T(2,128)(2,1)}), bf16[128,2,128]{2,1,0:T(2,128)(2,1)S(1)}, u32[]{:S(2)}, u32[]{:S(2)}) %all-to-all-start) | async-done | bytes 65568 | tf_op jit(solution)/shard_map/all_to_all | solution.py:259
  38.4 0.0 copy-done.4
  38.4 1.7 %far.1 = (bf16[128,2,128]{2,1,0:T(2,128)(2,1)}, bf16[8,128]{1,0:T(8,128)(2,1)S(1)}) custom-call(s32[1,16]{1,0:T(1,128)S(1)} %get-tuple-element.12.refs_0_, s32[1,128]{1,0:T(1,128)S(1)} %get-tuple-element.13.refs_1_, s32[1,1]{1,0:T(1,128)S(6)} %copy.11.refs_2_, bf16[128,2,128]{2,1,0:T(2,128)(2,1)S(1)} %all-to-all-done.refs_3_, ...), custom_call_target="tpu_custom_call" | custom-call | tf_op jit(solution)/shard_map/far/pallas_call | solution.py:326
  40.1 5.7 %all-to-all-start.1 = ((bf16[128,2,128]{2,1,0:T(2,128)(2,1)}), bf16[128,2,128]{2,1,0:T(2,128)(2,1)S(1)}, u32[]{:S(2)}, u32[]{:S(2)}) async-start(bf16[128,2,128]{2,1,0:T(2,128)(2,1)} %get-tuple-element.16), calls=%async_computation.1 | async-start | bytes 131072 | tf_op jit(solution)/shard_map/all_to_all | solution.py:259
  45.8 0.0 copy-start.5
  45.8 3.5 %collective-permute-start.1 = (bf16[8,128]{1,0:T(8,128)(2,1)S(1)}, bf16[8,128]{1,0:T(8,128)(2,1)S(1)}, u32[]{:S(2)}, u32[]{:S(2)}) collective-permute-start(bf16[8,128]{1,0:T(8,128)(2,1)S(1)} %relay.1.refs_5_), channel_id=1, source_target_pairs={{8,16},{16,8},{24,32},{32,24},{40,48},{48,40},{56,64},{64,56},{72,... | collective-permute-start | bytes 6152 | tf_op jit(solution)/shard_map/ppermute | solution.py:267
  49.4 1.9 %collective-permute-start = (bf16[8,128]{1,0:T(8,128)(2,1)S(1)}, bf16[8,128]{1,0:T(8,128)(2,1)S(1)}, u32[]{:S(2)}, u32[]{:S(2)}) collective-permute-start(bf16[8,128]{1,0:T(8,128)(2,1)S(1)} %relay.1.refs_5_), channel_id=1, source_target_pairs={{0,8},{8,0},{16,24},{24,16},{32,40},{40,32},{48,56},{56,48},{64,72... | collective-permute-start | bytes 6152 | tf_op jit(solution)/shard_map/ppermute | solution.py:267
  51.3 0.0 collective-permute-done.1.other_ref
  51.3 1.1 %collective-permute-done.pair_ref = bf16[8,128]{1,0:T(8,128)(2,1)S(1)} collective-permute-done((bf16[8,128]{1,0:T(8,128)(2,1)S(1)}, bf16[8,128]{1,0:T(8,128)(2,1)S(1)}, u32[]{:S(2)}, u32[]{:S(2)}) %collective-permute-start) | collective-permute-done | bytes 2080 | tf_op jit(solution)/shard_map/ppermute | solution.py:267
  52.4 0.0 copy-done.5
  52.4 1.2 %copy-done.1 = bf16[1,8,4,128,128]{4,3,2,1,0:T(8,128)(2,1)S(1)} copy-done((bf16[1,8,4,128,128]{4,3,2,1,0:T(8,128)(2,1)S(1)}, bf16[1,8,4,128,128]{4,3,2,1,0:T(8,128)(2,1)}, u32[]{:S(2)}) %copy-start.1) | copy-done | bytes 1048600
  53.6 0.9 near.1.after_ref.refs_3_
  54.6 0.5 gram.1.refs_4_
  55.1 2.3 %all-to-all-done.1.refs_2_ = bf16[128,2,128]{2,1,0:T(2,128)(2,1)S(1)} async-done(((bf16[128,2,128]{2,1,0:T(2,128)(2,1)}), bf16[128,2,128]{2,1,0:T(2,128)(2,1)S(1)}, u32[]{:S(2)}, u32[]{:S(2)}) %all-to-all-start.1) | async-done | bytes 65568 | tf_op jit(solution)/shard_map/all_to_all | solution.py:259
  57.3 0.0 copy-done.3
  57.3 0.3 image.1
  57.7 12.0 %all_to_all.20.arrived_ref = f32[16,1,256]{2,1,0:T(1,128)S(1)} all-to-all(f32[16,1,256]{2,1,0:T(1,128)S(1)} %get-tuple-element.19), channel_id=1, replica_groups=mesh['z'=8,'x'=8,'core'=2,'grp'=8] {'x','core'}, dimensions={0} | all-to-all | bytes 32768 | tf_op jit(solution)/shard_map/all_to_all | solution.py:259
  69.7 24.5 %all_to_all.21.refs_2_ = f32[64,1,256]{2,1,0:T(1,128)S(1)} all-to-all(f32[64,1,256]{2,1,0:T(1,128)S(1)} %total.1), channel_id=1, replica_groups=mesh['z'=8,'x'=8,'core'=2,'grp'=8] {'z','grp'}, dimensions={0} | all-to-all | bytes 131072 | tf_op jit(solution)/shard_map/all_to_all | solution.py:259
  94.2 1.0 %final.1 = (f32[1,8,128]{2,1,0:T(8,128)}, f32[1,17]{1,0:T(1,128)}) custom-call(f32[16,1,8,128]{3,2,1,0:T(8,128)S(1)} %copy-done, f32[8,128]{1,0:T(8,128)S(1)} %get-tuple-element.18.refs_1_, f32[64,1,256]{2,1,0:T(1,128)S(1)} %all_to_all.21.refs_2_), custom_call_target="tpu_custom_call" | custom-call | tf_op jit(solution)/shard_map/final/pallas_call | solution.py:370
  (6 shorter events, 0.0 us)
Async XLA Ops:
  2.3 25.3 %copy-start.2 = (bf16[128,2,128]{2,1,0:T(2,128)(2,1)S(1)}, bf16[128,2,128]{2,1,0:T(2,128)(2,1)}, u32[]{:S(2)}) copy-start(bf16[128,2,128]{2,1,0:T(2,128)(2,1)} %get-tuple-element.14.after_ref) | copy-start | bytes 196612
  2.4 36.0 %all-to-all-start = ((bf16[128,2,128]{2,1,0:T(2,128)(2,1)}), bf16[128,2,128]{2,1,0:T(2,128)(2,1)S(1)}, u32[]{:S(2)}, u32[]{:S(2)}) async-start(bf16[128,2,128]{2,1,0:T(2,128)(2,1)} %get-tuple-element.14.after_ref), calls=%async_computation | async-start | bytes 131072 | tf_op jit(solution)/shard_map/all_to_all | solution.py:259
  27.6 10.8 %copy-start.4 = (bf16[1,16,1024]{2,1,0:T(8,128)(2,1)S(1)}, bf16[1,16,1024]{2,1,0:T(8,128)(2,1)}, u32[]{:S(2)}) copy-start(bf16[1,16,1024]{2,1,0:T(8,128)(2,1)} %refs_4_.1) | copy-start | bytes 98308
  40.1 17.3 %all-to-all-start.1 = ((bf16[128,2,128]{2,1,0:T(2,128)(2,1)}), bf16[128,2,128]{2,1,0:T(2,128)(2,1)S(1)}, u32[]{:S(2)}, u32[]{:S(2)}) async-start(bf16[128,2,128]{2,1,0:T(2,128)(2,1)} %get-tuple-element.16), calls=%async_computation.1 | async-start | bytes 131072 | tf_op jit(solution)/shard_map/all_to_all | solution.py:259
  45.8 6.6 %copy-start.5 = (s32[1,8,4]{1,2,0:T(4,128)S(1)}, s32[1,8,4]{1,2,0:T(4,128)}, u32[]{:S(2)}) copy-start(s32[1,8,4]{1,2,0:T(4,128)} %param.11) | copy-start | bytes 388
  45.8 5.5 %collective-permute-start.1 = (bf16[8,128]{1,0:T(8,128)(2,1)S(1)}, bf16[8,128]{1,0:T(8,128)(2,1)S(1)}, u32[]{:S(2)}, u32[]{:S(2)}) collective-permute-start(bf16[8,128]{1,0:T(8,128)(2,1)S(1)} %relay.1.refs_5_), channel_id=1, source_target_pairs={{8,16},{16,8},{24,32},{32,24},{40,48},{48,40},{56,64},{64,56},{72,... | collective-permute-start | bytes 6152 | tf_op jit(solution)/shard_map/ppermute | solution.py:267
  49.4 3.1 %collective-permute-start = (bf16[8,128]{1,0:T(8,128)(2,1)S(1)}, bf16[8,128]{1,0:T(8,128)(2,1)S(1)}, u32[]{:S(2)}, u32[]{:S(2)}) collective-permute-start(bf16[8,128]{1,0:T(8,128)(2,1)S(1)} %relay.1.refs_5_), channel_id=1, source_target_pairs={{0,8},{8,0},{16,24},{24,16},{32,40},{40,32},{48,56},{56,48},{64,72... | collective-permute-start | bytes 6152 | tf_op jit(solution)/shard_map/ppermute | solution.py:267
  52.4 1.2 %copy-start.1 = (bf16[1,8,4,128,128]{4,3,2,1,0:T(8,128)(2,1)S(1)}, bf16[1,8,4,128,128]{4,3,2,1,0:T(8,128)(2,1)}, u32[]{:S(2)}) copy-start(bf16[1,8,4,128,128]{4,3,2,1,0:T(8,128)(2,1)} %blocks_ref.1) | copy-start | bytes 3145732
  53.6 0.9 copy-start
  54.6 2.8 %copy-start.3 = (bf16[1,8,32,128]{3,2,1,0:T(8,128)(2,1)S(1)}, bf16[1,8,32,128]{3,2,1,0:T(8,128)(2,1)}, u32[]{:S(2)}) copy-start(bf16[1,8,32,128]{3,2,1,0:T(8,128)(2,1)} %refs_1_.1) | copy-start | bytes 196612

commit v10 on v9

--- a/solution.py
+++ b/solution.py
@@ -91,6 +91,7 @@
     expansion_ref,
     coupling_ref,
     current_ref,
+    after_ref,
     sent_ref,
     held_ref,
 ):
@@ -325,12 +326,12 @@
 
     sent, held = pl.pallas_call(
         lambda *refs: far_kernel(clusters, owners, *refs),
-        in_specs=[SMEM, SMEM, SMEM, VMEM, VMEM, VMEM],
+        in_specs=[SMEM, SMEM, SMEM, VMEM, VMEM, VMEM, ANY],
         out_specs=[VMEM, VMEM],
         out_shape=[bf16(owners, width // LANES, LANES), bf16(clusters, panels)],
         compiler_params=SMALL,
         name="far",
-    )(sources, targets, far_count, expansions, coupling, current)
+    )(sources, targets, far_count, expansions, coupling, current, other)
     arrived = exchange(sent, CL)
 
     near = pl.pallas_call(
@@ -349,7 +350,7 @@
         out_shape=f32(1, packed),
         compiler_params=SMALL,
         name="gram",
-    )(basis, near)
+    )(basis, held)
     image, sent = pl.pallas_call(
         lambda *refs: image_kernel(owners, *refs),
         in_specs=[VMEM] * 5,

time: 95.7 us -> 94.5 us (0.987)
  blocking collectives: 36.5 us -> 32.6 us
  starting transfers between devices: 35.8 us -> 39.5 us
    all_to_all x2, blocking collectives: 36.5 us -> 32.6 us  [exchange(): return lax.all_to_all(rows, axes, 0, 0)]
    all_to_all x2, starting transfers between devices: 30.3 us -> 33.2 us  [exchange(): return lax.all_to_all(rows, axes, 0, 0)]
    all_to_all x2, waiting for transfers between devices: 13 us -> 11.9 us  [exchange(): return lax.all_to_all(rows, axes, 0, 0)]
  transfers between devices with their start and end apart: 4 -> 4, of which waited for: 3 -> 4; matrix products, arithmetic and copies ran while one was open for 0% -> 0% of each run, Pallas kernels for 1% -> 1%
where the time goes in v10:
time: 94.5 us; the launch traced here: 94 us
  starting transfers between devices  39.5 us (42%)
  blocking collectives  32.6 us (34%)
  waiting for transfers between devices  13.2 us (14%)
  Pallas kernels  6.11 us (6%)
  between operations  1.39 us (1%)
  local copies, waits for them, and re-layouts  1.25 us (1%)
    all_to_all x2, starting transfers between devices, exchange(): return lax.all_to_all(rows, axes, 0, 0)  33.2 us
    all_to_all x2, blocking collectives, exchange(): return lax.all_to_all(rows, axes, 0, 0)  32.6 us
    all_to_all x2, waiting for transfers between devices, exchange(): return lax.all_to_all(rows, axes, 0, 0)  11.9 us
    ppermute x2, starting transfers between devices, swapped(): return lax.ppermute(value, CL, route)  6.34 us
  transfers between devices with their start and end apart: 4, of which 4 were waited for; matrix products, arithmetic and copies ran while one was open for 0% of the time, Pallas kernels for 1%

profile of v10, /device:TPU:1, one launch (start us, length us, event | category | flops | bytes accessed | tf_op | source)
XLA Modules:
  0.0 94.0 jit_solution(10364850083876508549)
XLA Ops:
  0.6 1.7 %expand.1 = (bf16[128,2,128]{2,1,0:T(2,128)(2,1)}, bf16[8,128]{1,0:T(8,128)(2,1)S(1)}, s32[1,128]{1,0:T(1,128)S(1)}, s32[1,16]{1,0:T(1,128)S(1)}) custom-call(f32[16,1,8,128]{3,2,1,0:T(8,128)} %refs_0_.3, bf16[1,8,32,128]{3,2,1,0:T(8,128)(2,1)} %source_ref.1, s32[1,2048]{1,0:T(1,128)} %target_ref.1, s32[1,16]{1,0:T(1,128)} %slot_ref.1), custom_call_target="tpu_custom_call" | custom-call | tf_op jit(solution)/shard_map/expand/pallas_call | solution.py:297
  2.3 0.0 copy-start.2
  2.4 24.6 %all-to-all-start = ((bf16[128,2,128]{2,1,0:T(2,128)(2,1)}), bf16[128,2,128]{2,1,0:T(2,128)(2,1)S(1)}, u32[]{:S(2)}, u32[]{:S(2)}) async-start(bf16[128,2,128]{2,1,0:T(2,128)(2,1)} %get-tuple-element.14.after_ref), calls=%async_computation | async-start | bytes 131072 | tf_op jit(solution)/shard_map/all_to_all | solution.py:260
  26.9 0.0 copy-done.2
  27.0 0.0 copy-start.4
  27.0 3.5 %collective-permute-start = (bf16[8,128]{1,0:T(8,128)(2,1)S(1)}, bf16[8,128]{1,0:T(8,128)(2,1)S(1)}, u32[]{:S(2)}, u32[]{:S(2)}) collective-permute-start(bf16[8,128]{1,0:T(8,128)(2,1)S(1)} %relay.1.refs_5_), channel_id=1, source_target_pairs={{8,16},{16,8},{24,32},{32,24},{40,48},{48,40},{56,64},{64,56},{72,... | collective-permute-start | bytes 6152 | tf_op jit(solution)/shard_map/ppermute | solution.py:268
  31.2 1.0 %collective-permute-done.refs_6_.other_ref = bf16[8,128]{1,0:T(8,128)(2,1)S(1)} collective-permute-done((bf16[8,128]{1,0:T(8,128)(2,1)S(1)}, bf16[8,128]{1,0:T(8,128)(2,1)S(1)}, u32[]{:S(2)}, u32[]{:S(2)}) %collective-permute-start) | collective-permute-done | bytes 2080 | tf_op jit(solution)/shard_map/ppermute | solution.py:268
  32.2 6.2 %all-to-all-done.refs_3_ = bf16[128,2,128]{2,1,0:T(2,128)(2,1)S(1)} async-done(((bf16[128,2,128]{2,1,0:T(2,128)(2,1)}), bf16[128,2,128]{2,1,0:T(2,128)(2,1)S(1)}, u32[]{:S(2)}, u32[]{:S(2)}) %all-to-all-start) | async-done | bytes 65568 | tf_op jit(solution)/shard_map/all_to_all | solution.py:260
  38.4 0.0 copy-done.4
  38.4 1.7 %far.1 = (bf16[128,2,128]{2,1,0:T(2,128)(2,1)}, bf16[8,128]{1,0:T(8,128)(2,1)S(1)}) custom-call(s32[1,16]{1,0:T(1,128)S(1)} %get-tuple-element.12.refs_0_, s32[1,128]{1,0:T(1,128)S(1)} %get-tuple-element.13.refs_1_, s32[1,1]{1,0:T(1,128)S(6)} %copy.11.refs_2_, bf16[128,2,128]{2,1,0:T(2,128)(2,1)S(1)} %all-to-all-done.refs_3_, ...), custom_call_target="tpu_custom_call" | custom-call | tf_op jit(solution)/shard_map/far/pallas_call | solution.py:327
  40.1 8.6 %all-to-all-start.1 = ((bf16[128,2,128]{2,1,0:T(2,128)(2,1)}), bf16[128,2,128]{2,1,0:T(2,128)(2,1)S(1)}, u32[]{:S(2)}, u32[]{:S(2)}) async-start(bf16[128,2,128]{2,1,0:T(2,128)(2,1)} %get-tuple-element.16), calls=%async_computation.1 | async-start | bytes 131072 | tf_op jit(solution)/shard_map/all_to_all | solution.py:260
  48.7 2.8 %collective-permute-start.1 = (bf16[8,128]{1,0:T(8,128)(2,1)S(1)}, bf16[8,128]{1,0:T(8,128)(2,1)S(1)}, u32[]{:S(2)}, u32[]{:S(2)}) collective-permute-start(bf16[8,128]{1,0:T(8,128)(2,1)S(1)} %relay.1.refs_5_), channel_id=1, source_target_pairs={{0,8},{8,0},{16,24},{24,16},{32,40},{40,32},{48,56},{56,48},{64,72... | collective-permute-start | bytes 6152 | tf_op jit(solution)/shard_map/ppermute | solution.py:268
  51.5 0.0 copy-done
  51.5 0.0 copy-start.5
  51.5 0.5 gram.1.refs_4_
  51.9 0.3 collective-permute-done.1.pair_ref
  52.3 0.0 copy-done.5
  52.3 1.2 %copy-done.1 = bf16[1,8,4,128,128]{4,3,2,1,0:T(8,128)(2,1)S(1)} copy-done((bf16[1,8,4,128,128]{4,3,2,1,0:T(8,128)(2,1)S(1)}, bf16[1,8,4,128,128]{4,3,2,1,0:T(8,128)(2,1)}, u32[]{:S(2)}) %copy-start.1) | copy-done | bytes 1048600
  53.5 0.9 near.1.refs_3_
  54.4 5.7 %all-to-all-done.1.refs_2_ = bf16[128,2,128]{2,1,0:T(2,128)(2,1)S(1)} async-done(((bf16[128,2,128]{2,1,0:T(2,128)(2,1)}), bf16[128,2,128]{2,1,0:T(2,128)(2,1)S(1)}, u32[]{:S(2)}, u32[]{:S(2)}) %all-to-all-start.1) | async-done | bytes 65568 | tf_op jit(solution)/shard_map/all_to_all | solution.py:260
  60.1 0.3 image.1
  60.4 10.4 %all_to_all.20.arrived_ref = f32[16,1,256]{2,1,0:T(1,128)S(1)} all-to-all(f32[16,1,256]{2,1,0:T(1,128)S(1)} %get-tuple-element.19), channel_id=1, replica_groups=mesh['z'=8,'x'=8,'core'=2,'grp'=8] {'x','core'}, dimensions={0} | all-to-all | bytes 32768 | tf_op jit(solution)/shard_map/all_to_all | solution.py:260
  70.8 22.2 %all_to_all.21.refs_2_ = f32[64,1,256]{2,1,0:T(1,128)S(1)} all-to-all(f32[64,1,256]{2,1,0:T(1,128)S(1)} %total.1), channel_id=1, replica_groups=mesh['z'=8,'x'=8,'core'=2,'grp'=8] {'z','grp'}, dimensions={0} | all-to-all | bytes 131072 | tf_op jit(solution)/shard_map/all_to_all | solution.py:260
  93.0 1.0 %final.1 = (f32[1,8,128]{2,1,0:T(8,128)}, f32[1,17]{1,0:T(1,128)}) custom-call(f32[16,1,8,128]{3,2,1,0:T(8,128)S(1)} %copy-done, f32[8,128]{1,0:T(8,128)S(1)} %get-tuple-element.18.refs_1_, f32[64,1,256]{2,1,0:T(1,128)S(1)} %all_to_all.21.refs_2_), custom_call_target="tpu_custom_call" | custom-call | tf_op jit(solution)/shard_map/final/pallas_call | solution.py:371
  (6 shorter events, 0.0 us)
Async XLA Ops:
  2.3 24.6 %copy-start.2 = (bf16[128,2,128]{2,1,0:T(2,128)(2,1)S(1)}, bf16[128,2,128]{2,1,0:T(2,128)(2,1)}, u32[]{:S(2)}) copy-start(bf16[128,2,128]{2,1,0:T(2,128)(2,1)} %get-tuple-element.14.after_ref) | copy-start | bytes 196612
  2.4 36.0 %all-to-all-start = ((bf16[128,2,128]{2,1,0:T(2,128)(2,1)}), bf16[128,2,128]{2,1,0:T(2,128)(2,1)S(1)}, u32[]{:S(2)}, u32[]{:S(2)}) async-start(bf16[128,2,128]{2,1,0:T(2,128)(2,1)} %get-tuple-element.14.after_ref), calls=%async_computation | async-start | bytes 131072 | tf_op jit(solution)/shard_map/all_to_all | solution.py:260
  27.0 11.4 %copy-start.4 = (bf16[1,16,1024]{2,1,0:T(8,128)(2,1)S(1)}, bf16[1,16,1024]{2,1,0:T(8,128)(2,1)}, u32[]{:S(2)}) copy-start(bf16[1,16,1024]{2,1,0:T(8,128)(2,1)} %refs_4_.1) | copy-start | bytes 98308
  27.0 5.2 %collective-permute-start = (bf16[8,128]{1,0:T(8,128)(2,1)S(1)}, bf16[8,128]{1,0:T(8,128)(2,1)S(1)}, u32[]{:S(2)}, u32[]{:S(2)}) collective-permute-start(bf16[8,128]{1,0:T(8,128)(2,1)S(1)} %relay.1.refs_5_), channel_id=1, source_target_pairs={{8,16},{16,8},{24,32},{32,24},{40,48},{48,40},{56,64},{64,56},{72,... | collective-permute-start | bytes 6152 | tf_op jit(solution)/shard_map/ppermute | solution.py:268
  40.1 11.4 %copy-start = (f32[16,1,8,128]{3,2,1,0:T(8,128)S(1)}, f32[16,1,8,128]{3,2,1,0:T(8,128)}, u32[]{:S(2)}) copy-start(f32[16,1,8,128]{3,2,1,0:T(8,128)} %refs_0_.3) | copy-start | bytes 196612
  40.1 20.0 %all-to-all-start.1 = ((bf16[128,2,128]{2,1,0:T(2,128)(2,1)}), bf16[128,2,128]{2,1,0:T(2,128)(2,1)S(1)}, u32[]{:S(2)}, u32[]{:S(2)}) async-start(bf16[128,2,128]{2,1,0:T(2,128)(2,1)} %get-tuple-element.16), calls=%async_computation.1 | async-start | bytes 131072 | tf_op jit(solution)/shard_map/all_to_all | solution.py:260
  48.7 3.6 %collective-permute-start.1 = (bf16[8,128]{1,0:T(8,128)(2,1)S(1)}, bf16[8,128]{1,0:T(8,128)(2,1)S(1)}, u32[]{:S(2)}, u32[]{:S(2)}) collective-permute-start(bf16[8,128]{1,0:T(8,128)(2,1)S(1)} %relay.1.refs_5_), channel_id=1, source_target_pairs={{0,8},{8,0},{16,24},{24,16},{32,40},{40,32},{48,56},{56,48},{64,72... | collective-permute-start | bytes 6152 | tf_op jit(solution)/shard_map/ppermute | solution.py:268
  51.5 0.8 copy-start.5
  52.3 1.2 %copy-start.1 = (bf16[1,8,4,128,128]{4,3,2,1,0:T(8,128)(2,1)S(1)}, bf16[1,8,4,128,128]{4,3,2,1,0:T(8,128)(2,1)}, u32[]{:S(2)}) copy-start(bf16[1,8,4,128,128]{4,3,2,1,0:T(8,128)(2,1)} %blocks_ref.1) | copy-start | bytes 3145732
  53.5 6.6 %copy-start.3 = (bf16[1,8,32,128]{3,2,1,0:T(8,128)(2,1)S(1)}, bf16[1,8,32,128]{3,2,1,0:T(8,128)(2,1)}, u32[]{:S(2)}) copy-start(bf16[1,8,32,128]{3,2,1,0:T(8,128)(2,1)} %refs_1_.1) | copy-start | bytes 196612
